TPU v7x, 32 devices: a whole 2x2x4 slice. The times are simulated.
32 devices in a mesh: dp: 8 (over y, x, core), mp: 4 (over z).
Axes of the slice: x: 2, y: 2, z: 4, core: 2. Of those that a mesh axis runs over, the one named last changes fastest.
Arguments:
- block_in: bfloat16 [8192, 1536], P(('dp', 'mp')), may hold values from -6 to 6
- grad_out: bfloat16 [8192, 1536], P(('dp', 'mp')), may hold values from -6 to 6
- resets: int32 [8, 16], P('dp'), may hold values 0 or 1
- counts: int32 [8], P('dp'), may hold values from 512 to 1024
- gain_in: bfloat16 [1536], P(('dp', 'mp')), may hold values from 0.5 to 1.5
- w_forget: bfloat16 [1536], P(('dp', 'mp')), may hold values from -2.5 to 2.5
- w_momentum: bfloat16 [1536], P(('dp', 'mp')), may hold values from -2.5 to 2.5
- project_in: bfloat16 [3, 1536, 1536], P(None, 'dp', 'mp'), may hold values from -0.15625 to 0.15625
- project_out: bfloat16 [1536, 1536], P('mp', 'dp'), may hold values from -0.625 to 0.625
- memory_in: bfloat16 [1536, 6144], P('dp', 'mp'), may hold values from -0.15625 to 0.15625
- memory_out: bfloat16 [6144, 1536], P('mp', 'dp'), may hold values from -0.078125 to 0.078125
- gain_mid: bfloat16 [1536], P(('dp', 'mp')), may hold values from 0.5 to 1.5
- gate_weight: bfloat16 [1536, 4096], P('dp', 'mp'), may hold values from -0.15625 to 0.15625
- up_weight: bfloat16 [1536, 4096], P('dp', 'mp'), may hold values from -0.15625 to 0.15625
- down_weight: bfloat16 [4096, 1536], P('mp', 'dp'), may hold values from -0.09375 to 0.09375
Outputs:
- block_out: bfloat16 [8192, 1536], P(('dp', 'mp'))
- grad_block_in: float32 [8192, 1536], P(('dp', 'mp'))
- grad_gain_in: float32 [1536], P(('dp', 'mp'))
- grad_forget: float32 [1536], P(('dp', 'mp'))
- grad_momentum: float32 [1536], P(('dp', 'mp'))
- grad_project_in: float32 [3, 1536, 1536], P(None, 'dp', 'mp')
- grad_project_out: float32 [1536, 1536], P('mp', 'dp')
- grad_memory_in: float32 [1536, 6144], P('dp', 'mp')
- grad_memory_out: float32 [6144, 1536], P('mp', 'dp')
- grad_gain_mid: float32 [1536], P(('dp', 'mp'))
- grad_gate: float32 [1536, 4096], P('dp', 'mp')
- grad_up: float32 [1536, 4096], P('dp', 'mp')
- grad_down: float32 [4096, 1536], P('mp', 'dp')
- logged: float32 [3], replicated
All inputs are finite; a program needn't handle non-finite values. No bound on the sum of `resets` on one device may be relied on, other than what follows from the above.
Results may differ from a plain program's by a relative error of at most 0.01.
Values may be sent and summed in bfloat16 or wider, within the bound.
A program may use at most 256 MiB of HBM per device.

v0:
```python
import jax
import jax.numpy as jnp
from jax import lax
from jax.sharding import PartitionSpec as P

D = 1536
HD = 96
HM = 6144
CH = 64


EPS = 1e-06
ALPHA_SHIFT = 1.5
ETA_SHIFT = 0.5
NEG = -1e30


def span_weights(alpha, eta, keep):
    number = alpha.shape[0]
    basis = jnp.eye(number, dtype=alpha.dtype)

    def advance(carry, inputs):
        state, memory = carry
        rate, moment, kept, unit = inputs
        before = memory * kept
        state = moment * kept * state + unit
        memory = rate * kept * memory + state
        return ((state, memory), before)

    start = (jnp.zeros(number, alpha.dtype), jnp.zeros(number, alpha.dtype))
    _, table = lax.scan(advance, start, (alpha, eta, keep, basis))
    return table


def norm_rows(values, gain):
    inverse = lax.rsqrt(jnp.mean(values * values, axis=-1, keepdims=True) + EPS)
    return (values * inverse * gain, inverse)


def norm_back(values, inverse, gain, grad):
    scaled = grad * gain
    inner = jnp.mean(values * scaled, axis=-1, keepdims=True)
    grad_values = inverse * scaled - values * inverse * inverse * inverse * inner
    grad_gain = jnp.sum(grad * values * inverse, axis=0)
    return (grad_values, grad_gain)


def left_dot(first, second):
    return lax.dot_general(
        first, second, (((0,), (0,)), ((), ())), preferred_element_type=jnp.float32
    )


def right_dot(first, second):
    return lax.dot_general(
        first, second, (((1,), (1,)), ((), ())), preferred_element_type=jnp.float32
    )


def plain_dot(first, second):
    return jnp.dot(first, second, preferred_element_type=jnp.float32)


def on_device(
    block_in,
    grad_out,
    resets,
    counts,
    gain_in,
    w_forget,
    w_momentum,
    project_in,
    project_out,
    memory_in,
    memory_out,
    gain_mid,
    gate_weight,
    up_weight,
    down_weight,
):
    high = lax.Precision.HIGHEST
    shared = (
        lax.all_gather(gain_in, ("dp", "mp"), axis=0, tiled=True),
        lax.all_gather(w_forget, ("dp", "mp"), axis=0, tiled=True),
        lax.all_gather(w_momentum, ("dp", "mp"), axis=0, tiled=True),
        lax.all_gather(gain_mid, ("dp", "mp"), axis=0, tiled=True),
    )
    gain_one, forget_vec, moment_vec, gain_two = shared
    project_full, memory_first, merge_full, memory_second, gate_full, up_full, down_full = (
        lax.all_gather(project_in, "dp", axis=1, tiled=True),
        lax.all_gather(memory_in, "dp", axis=0, tiled=True),
        lax.all_gather(project_out, "dp", axis=1, tiled=True),
        lax.all_gather(memory_out, "dp", axis=1, tiled=True),
        lax.all_gather(gate_weight, "dp", axis=0, tiled=True),
        lax.all_gather(up_weight, "dp", axis=0, tiled=True),
        lax.all_gather(down_weight, "dp", axis=1, tiled=True),
    )
    gain_one = gain_one.astype(jnp.float32)
    gain_two = gain_two.astype(jnp.float32)
    local_rows = block_in.shape[0]
    groups = lax.axis_size("mp")
    length = local_rows * groups
    spans = length // CH
    span_rows = local_rows // CH
    member = lax.axis_index("mp")
    heads_here = project_in.shape[2] // HD
    positions = jnp.arange(length, dtype=jnp.int32)
    valid = (positions < counts[0]).astype(jnp.float32)
    keep = (1 - resets[0]).astype(jnp.float32)
    doc_tok = jnp.repeat(jnp.cumsum(resets[0], dtype=jnp.int32), CH)
    inputs_full = block_in.astype(jnp.float32)
    normed, inverse_one = norm_rows(inputs_full, gain_one)
    row_full = lax.all_gather(normed.astype(jnp.bfloat16), "mp", axis=0, tiled=True)
    gate_vectors = jnp.stack([forget_vec, moment_vec], axis=1)
    logits = jnp.mean(plain_dot(row_full, gate_vectors).reshape(spans, CH, 2), axis=1)
    alpha = jax.nn.sigmoid(logits[:, 0] + ALPHA_SHIFT)
    eta = jax.nn.sigmoid(logits[:, 1] + ETA_SHIFT)
    table, table_pull = jax.vjp(lambda rate, moment: span_weights(rate, moment, keep), alpha, eta)
    pre_act = plain_dot(row_full, memory_first)
    features = jax.nn.silu(pre_act).astype(jnp.bfloat16)
    recall_part = plain_dot(features, memory_second)
    triple = jnp.einsum(
        "td,kde->kte", row_full, project_full, preferred_element_type=jnp.float32
    ).astype(jnp.bfloat16)
    query = triple[0].reshape(length, heads_here, HD)
    keys = triple[1].reshape(length, heads_here, HD)
    values = triple[2].reshape(length, heads_here, HD)
    block = min(512, length)
    scale = HD ** (-0.5)
    starts = jnp.arange(length // block, dtype=jnp.int32) * block

    def scores_at(start):
        rows = start + jnp.arange(block, dtype=jnp.int32)
        query_rows = lax.dynamic_slice_in_dim(query, start, block, 0)
        doc_rows = lax.dynamic_slice_in_dim(doc_tok, start, block, 0)
        allow = (
            (positions[None, :] <= rows[:, None])
            & (doc_tok[None, :] == doc_rows[:, None])
            & ((valid[None, :] > 0) | (positions[None, :] == rows[:, None]))
        )
        raw = (
            jnp.einsum("thd,shd->hts", query_rows, keys, preferred_element_type=jnp.float32) * scale
        )
        return (jnp.where(allow[None], raw, NEG), query_rows)

    def forward_block(start):
        score, query_rows = scores_at(start)
        top = jnp.max(score, axis=-1, keepdims=True)
        logsum = top + jnp.log(jnp.sum(jnp.exp(score - top), axis=-1, keepdims=True))
        prob = jnp.exp(score - logsum).astype(jnp.bfloat16)
        context_rows = jnp.einsum("hts,shd->thd", prob, values, preferred_element_type=jnp.float32)
        return (context_rows, logsum)

    contexts, logsums = lax.map(forward_block, starts)
    context = contexts.reshape(length, heads_here * HD).astype(jnp.bfloat16)
    attn_part = plain_dot(context, merge_full)
    sim_part = right_dot(features, features) / HM
    sim_rows, out_rows = (
        lax.psum_scatter(sim_part, "mp", scatter_dimension=0, tiled=True),
        lax.psum_scatter(recall_part + attn_part, "mp", scatter_dimension=0, tiled=True),
    )
    table_rows = lax.dynamic_slice_in_dim(table, member * span_rows, span_rows, 0)
    spread_rows = jnp.repeat(jnp.repeat(table_rows, CH, axis=0), CH, axis=1)
    mixing = (sim_rows * spread_rows * valid[None, :] / CH).astype(jnp.bfloat16)
    branch = out_rows + plain_dot(mixing, row_full)
    middle = inputs_full + branch
    normed_two, inverse_two = norm_rows(middle, gain_two)
    normed_two_low = normed_two.astype(jnp.bfloat16)
    mid_all, grad_all = (
        lax.all_gather(normed_two_low, "mp", axis=0, tiled=True),
        lax.all_gather(grad_out, "mp", axis=0, tiled=True),
    )
    gate_pre = plain_dot(mid_all, gate_full)
    up_pre = plain_dot(mid_all, up_full)
    sigma = jax.nn.sigmoid(gate_pre)
    swish = gate_pre * sigma
    hidden = (swish * up_pre).astype(jnp.bfloat16)
    down_part = plain_dot(hidden, down_full)
    grad_hidden = right_dot(grad_all, down_full)
    slope = sigma * (1.0 + gate_pre * (1.0 - sigma))
    grad_gate_pre = (grad_hidden * up_pre * slope).astype(jnp.bfloat16)
    grad_up_pre = (grad_hidden * swish).astype(jnp.bfloat16)
    normed_two_part = right_dot(grad_gate_pre, gate_full) + right_dot(grad_up_pre, up_full)
    ffn_rows, grad_normed_two = (
        lax.psum_scatter(down_part, "mp", scatter_dimension=0, tiled=True),
        lax.psum_scatter(normed_two_part, "mp", scatter_dimension=0, tiled=True),
    )
    result = middle + ffn_rows
    block_out = result.astype(jnp.bfloat16)
    feature_blocks = features.reshape(spans, CH, features.shape[1])
    gram = jnp.einsum(
        "cth,csh->cts", feature_blocks, feature_blocks, preferred_element_type=jnp.float32
    )
    written = (row_full * valid[:, None].astype(jnp.bfloat16)).reshape(spans, CH, row_full.shape[1])
    cross = jnp.einsum("ctd,csd->cts", written, written, preferred_element_type=jnp.float32)
    piece_part = jnp.sum(gram * cross, axis=(1, 2))
    weight = jnp.sum(valid.reshape(spans, CH), axis=1)
    piece = lax.psum(piece_part, "mp")
    surprise = jnp.sqrt(piece / (HM * D * CH))
    numer = jnp.stack([jnp.sum(weight * surprise), jnp.sum(weight * alpha), jnp.sum(weight * eta)])
    total_numer, total_weight = lax.psum((numer, jnp.sum(weight)), "dp")
    logged = total_numer / total_weight
    grad_full = grad_out.astype(jnp.float32)
    grad_down = left_dot(hidden, grad_all)
    grad_gate = left_dot(mid_all, grad_gate_pre)
    grad_up = left_dot(mid_all, grad_up_pre)
    back_two, grad_gain_two = norm_back(middle, inverse_two, gain_two, grad_normed_two)
    grad_middle = grad_full + back_two
    grad_branch = grad_middle.astype(jnp.bfloat16)
    grad_mixing = right_dot(grad_branch, row_full)
    grad_rows = left_dot(mixing, grad_branch)
    scaled_mixing = grad_mixing / CH * valid[None, :]
    grad_sim_rows = (scaled_mixing * spread_rows).astype(jnp.bfloat16)
    grad_blocks = jnp.sum((scaled_mixing * sim_rows).reshape(span_rows, CH, spans, CH), axis=(1, 3))
    branch_all, grad_sim_all = (
        lax.all_gather(grad_branch, "mp", axis=0, tiled=True),
        lax.all_gather(grad_sim_rows, "mp", axis=0, tiled=True),
    )
    grad_memory_second = left_dot(features, branch_all)
    grad_features = (
        right_dot(branch_all, memory_second)
        + (plain_dot(grad_sim_all, features) + left_dot(grad_sim_all, features)) / HM
    )
    sig_pre = jax.nn.sigmoid(pre_act)
    grad_pre = (grad_features * sig_pre * (1.0 + pre_act * (1.0 - sig_pre))).astype(jnp.bfloat16)
    grad_memory_first = left_dot(row_full, grad_pre)
    grad_rows = grad_rows + right_dot(grad_pre, memory_first)
    grad_merge = left_dot(context, branch_all)
    grad_context = (
        right_dot(branch_all, merge_full).astype(jnp.bfloat16).reshape(length, heads_here, HD)
    )

    def backward_block(carry, inputs):
        grad_keys, grad_vals = carry
        start, logsum = inputs
        score, query_rows = scores_at(start)
        prob = jnp.exp(score - logsum)
        grad_ctx_rows = lax.dynamic_slice_in_dim(grad_context, start, block, 0)
        grad_prob = jnp.einsum(
            "thd,shd->hts", grad_ctx_rows, values, preferred_element_type=jnp.float32
        )
        inner = jnp.sum(prob * grad_prob, axis=-1, keepdims=True)
        grad_score = (prob * (grad_prob - inner)).astype(jnp.bfloat16)
        grad_query = (
            jnp.einsum("hts,shd->thd", grad_score, keys, preferred_element_type=jnp.float32) * scale
        )
        grad_keys = (
            grad_keys
            + jnp.einsum("hts,thd->shd", grad_score, query_rows, preferred_element_type=jnp.float32)
            * scale
        )
        grad_vals = grad_vals + jnp.einsum(
            "hts,thd->shd",
            prob.astype(jnp.bfloat16),
            grad_ctx_rows,
            preferred_element_type=jnp.float32,
        )
        return ((grad_keys, grad_vals), grad_query)

    zero_heads = jnp.zeros((length, heads_here, HD), jnp.float32)
    (grad_keys, grad_vals), grad_queries = lax.scan(
        backward_block, (zero_heads, zero_heads), (starts, logsums)
    )
    grad_triple = jnp.stack(
        [
            grad_queries.reshape(length, -1),
            grad_keys.reshape(length, -1),
            grad_vals.reshape(length, -1),
        ]
    ).astype(jnp.bfloat16)
    grad_project = jnp.einsum(
        "td,kte->kde", row_full, grad_triple, preferred_element_type=jnp.float32
    )
    grad_rows = grad_rows + jnp.einsum(
        "kte,kde->td", grad_triple, project_full, preferred_element_type=jnp.float32
    )
    grad_table = lax.dynamic_update_slice_in_dim(
        jnp.zeros((spans, spans), jnp.float32), grad_blocks, member * span_rows, 0
    )
    grad_alpha, grad_eta = table_pull(grad_table)
    grad_logits = jnp.stack(
        [grad_alpha * alpha * (1.0 - alpha), grad_eta * eta * (1.0 - eta)], axis=1
    )
    grad_tokens = jnp.repeat(grad_logits, CH, axis=0) / CH
    grad_vectors = jnp.dot(grad_tokens.T, row_full, precision=high)
    grad_rows = grad_rows + jnp.dot(grad_tokens, gate_vectors.T.astype(jnp.float32), precision=high)
    grad_normed = lax.psum_scatter(grad_rows, "mp", scatter_dimension=0, tiled=True)
    back_one, grad_gain_one = norm_back(inputs_full, inverse_one, gain_one, grad_normed)
    grad_block_in = grad_middle + back_one
    (
        grad_project_in,
        grad_memory_in,
        grad_project_out,
        grad_memory_out,
        grad_gate_out,
        grad_up_out,
        grad_down_out,
    ) = (
        lax.psum_scatter(grad_project, "dp", scatter_dimension=1, tiled=True),
        lax.psum_scatter(grad_memory_first, "dp", scatter_dimension=0, tiled=True),
        lax.psum_scatter(grad_merge, "dp", scatter_dimension=1, tiled=True),
        lax.psum_scatter(grad_memory_second, "dp", scatter_dimension=1, tiled=True),
        lax.psum_scatter(grad_gate, "dp", scatter_dimension=0, tiled=True),
        lax.psum_scatter(grad_up, "dp", scatter_dimension=0, tiled=True),
        lax.psum_scatter(grad_down, "dp", scatter_dimension=1, tiled=True),
    )
    shared_grads = (
        lax.psum_scatter(grad_gain_one, ("dp", "mp"), scatter_dimension=0, tiled=True),
        lax.psum_scatter(grad_vectors[0], ("dp", "mp"), scatter_dimension=0, tiled=True),
        lax.psum_scatter(grad_vectors[1], ("dp", "mp"), scatter_dimension=0, tiled=True),
        lax.psum_scatter(grad_gain_two, ("dp", "mp"), scatter_dimension=0, tiled=True),
    )
    grad_gain_in, grad_forget, grad_momentum, grad_gain_mid = shared_grads
    return (
        block_out,
        grad_block_in,
        grad_gain_in,
        grad_forget,
        grad_momentum,
        grad_project_in,
        grad_project_out,
        grad_memory_in,
        grad_memory_out,
        grad_gain_mid,
        grad_gate_out,
        grad_up_out,
        grad_down_out,
        logged,
    )


def solution(mesh):
    placed = (
        P(("dp", "mp"), None),
        P(("dp", "mp"), None),
        P("dp", None),
        P("dp"),
        P(("dp", "mp")),
        P(("dp", "mp")),
        P(("dp", "mp")),
        P(None, "dp", "mp"),
        P("mp", "dp"),
        P("dp", "mp"),
        P("mp", "dp"),
        P(("dp", "mp")),
        P("dp", "mp"),
        P("dp", "mp"),
        P("mp", "dp"),
    )
    return jax.shard_map(
        on_device,
        mesh=mesh,
        in_specs=placed,
        out_specs=(
            P(("dp", "mp"), None),
            P(("dp", "mp"), None),
            P(("dp", "mp")),
            P(("dp", "mp")),
            P(("dp", "mp")),
            P(None, "dp", "mp"),
            P("mp", "dp"),
            P("dp", "mp"),
            P("mp", "dp"),
            P(("dp", "mp")),
            P("dp", "mp"),
            P("dp", "mp"),
            P("mp", "dp"),
            P(),
        ),
        check_vma=False,
    )
```

profile of v0, /device:TPU:1, one launch (start us, length us, event | category | flops | bytes accessed | tf_op | source)
XLA Modules:
  0.0 1801.2 jit_solution(7621434846102782426)
XLA Ops:
  10.6 40.7 %all-reduce.10 = (bf16[1536]{0:T(1024)(128)(2,1)S(1)}, bf16[1536]{0:T(1024)(128)(2,1)S(1)}, bf16[1536]{0:T(1024)(128)(2,1)S(1)}, bf16[1536]{0:T(1024)(128)(2,1)S(1)}) all-reduce(bf16[1536]{0:T(1024)(128)(2,1)S(1)} %dynamic-update-slice, bf16[1536]{0:T(1024)(128)(2,1)S(1)} %dynamic-update-slice.2, ...), channel_id=1, replica_groups=mesh['dp'=8,'mp'=4] {'dp','mp'}, use_global_device_ids=true, to_apply=%add | all-reduce | flops 6144 | bytes 24576
  58.3 61.7 %all-gather.13.cloned.1.call-done = bf16[1024,1536]{1,0:T(8,128)(2,1)} async-done(((bf16[256,1536]{1,0:T(8,128)(2,1)}), bf16[1024,1536]{1,0:T(8,128)(2,1)}) %all-gather.13.cloned.1.call-update) | async-done | bytes 3145744 | tf_op jit(solution)/shard_map/all_gather | solution.py:113
  120.0 39.9 %all-gather.15.cloned.1.call-done = bf16[1536,1536]{1,0:T(8,128)(2,1)} async-done(((bf16[192,1536]{1,0:T(8,128)(2,1)}), bf16[1536,1536]{1,0:T(8,128)(2,1)}) %all-gather.15.cloned.1.call-update) | async-done | bytes 4718608 | tf_op jit(solution)/shard_map/all_gather | solution.py:91
  160.0 10.2 multiply_convert_fusion.2
  177.8 18.0 %all-gather.19.cloned.1.call-done = bf16[3,1536,384]{2,1,0:T(8,128)(2,1)} async-done(((bf16[3,192,384]{2,1,0:T(8,128)(2,1)}), bf16[3,1536,384]{2,1,0:T(8,128)(2,1)}) %all-gather.19.cloned.1.call-update) | async-done | bytes 3538960 | tf_op jit(solution)/shard_map/all_gather | solution.py:90
  202.4 23.8 %while.74 = (s32[]{:T(128)}, bf16[2,512,4,96]{1,3,2,0:T(8,128)(2,1)S(1)}, f32[2,4,512,1]{2,1,3,0:T(4,128)S(1)}, s32[2]{0:T(128)S(1)}, s32[1024]{0:T(1024)S(1)}, ...) while((s32[]{:T(128)}, ...), condition=%wide.region_5.6_spmd.clone.clone, body=%wide.region_2.0_spmd.clone.clone.sunk | while | flops 831522304 | bytes 30109956 | solution.py:154
  246.3 16.1 all-gather.21.cloned.1.call-done
  280.5 10.3 psum.21
  291.6 85.7 %while.75 = (s32[]{:T(128)}, f32[16]{0:T(128)S(1)}, f32[16]{0:T(128)S(1)}, f32[16,16]{1,0:T(8,128)S(1)}, f32[16,16]{1,0:T(8,128)S(1)}, /*index=5*/f32[16]{0:T(12...) while((s32[]{:T(128)}, f32[16]{0:T(128)S(1)}, ...), condition=%wide.region_10.11_spmd.clone, body=%wide.region_9.10_spmd.clone.sunk | while | flops 117 | bytes 1151 | solution.py:31
  383.4 71.5 %reduce-scatter.15.cloned.1.call-done = f32[256,1536]{1,0:T(8,128)} async-done(((f32[1024,1536]{1,0:T(8,128)}), f32[256,1536]{1,0:T(8,128)}) %reduce-scatter.15.cloned.1.call-update) | async-done | bytes 1572880 | tf_op jit(solution)/shard_map/reduce_scatter | solution.py:160
  461.8 28.3 %all-gather.25.cloned.1.call-done = bf16[1536,1024]{1,0:T(8,128)(2,1)} async-done(((bf16[192,1024]{1,0:T(8,128)(2,1)}), bf16[1536,1024]{1,0:T(8,128)(2,1)}) %all-gather.25.cloned.1.call-update) | async-done | bytes 3145744 | tf_op jit(solution)/shard_map/all_gather | solution.py:94
  490.1 65.3 %all-gather.23.cloned.1.call-done = bf16[1024,1536]{1,0:T(8,128)(2,1)} async-done(((bf16[256,1536]{1,0:T(8,128)(2,1)}), bf16[1024,1536]{1,0:T(8,128)(2,1)}) %all-gather.23.cloned.1.call-update) | async-done | bytes 3145744 | tf_op jit(solution)/shard_map/all_gather | solution.py:170
  563.6 25.1 %all-gather.27.cloned.1.call-done = bf16[1536,1024]{1,0:T(8,128)(2,1)} async-done(((bf16[192,1024]{1,0:T(8,128)(2,1)}), bf16[1536,1024]{1,0:T(8,128)(2,1)}) %all-gather.27.cloned.1.call-update) | async-done | bytes 3145744 | tf_op jit(solution)/shard_map/all_gather | solution.py:95
  597.0 56.5 %all-gather.31.cloned.1.call-done = bf16[1024,1536]{1,0:T(8,128)(2,1)} async-done(((bf16[256,1536]{1,0:T(8,128)(2,1)}), bf16[1024,1536]{1,0:T(8,128)(2,1)}) %all-gather.31.cloned.1.call-update) | async-done | bytes 3145744 | tf_op jit(solution)/shard_map/all_gather | solution.py:171
  653.5 33.4 %all-gather.29.cloned.1.call-done = bf16[1024,1536]{0,1:T(8,128)(2,1)} async-done(((bf16[1024,192]{0,1:T(8,128)(2,1)}), bf16[1024,1536]{0,1:T(8,128)(2,1)}) %all-gather.29.cloned.1.call-update) | async-done | bytes 3145744 | tf_op jit(solution)/shard_map/all_gather | solution.py:96
  686.8 11.5 multiply_convert_fusion.3
  707.6 110.3 %reduce-scatter.21.cloned.1.call-done = f32[256,1536]{1,0:T(8,128)} async-done(((f32[1024,1536]{1,0:T(8,128)}), f32[256,1536]{1,0:T(8,128)}) %reduce-scatter.21.cloned.1.call-update) | async-done | bytes 1572880 | tf_op jit(solution)/shard_map/reduce_scatter | solution.py:186
  834.2 53.1 %all-gather.33.cloned.1.call-done = bf16[1024,1536]{1,0:T(8,128)(2,1)} async-done(((bf16[256,1536]{1,0:T(8,128)(2,1)}), bf16[1024,1536]{1,0:T(8,128)(2,1)}) %all-gather.33.cloned.1.call-update) | async-done | bytes 3145744 | tf_op jit(solution)/shard_map/all_gather | solution.py:216
  892.4 56.1 %while.77 = (s32[]{:T(128)}, f32[1024,4,96]{0,2,1:T(8,128)S(1)}, f32[1024,4,96]{0,2,1:T(8,128)}, bf16[2,512,4,96]{1,3,2,0:T(8,128)(2,1)}, s32[2]{0:T(128)}, /*in...) while((s32[]{:T(128)}, f32[1024,4,96]{0,2,1:T(8,128)S(1)}, ...), condition=%wide.region_17.18_spmd.clone.clone, body=%wide.region_15.17_spmd.clone.clone.sunk | while | flops 2050033152 | bytes 152720336 | solution.py:261
  967.9 10.8 copy.74
  986.6 125.2 %while.76 = (s32[]{:T(128)}, f32[16]{0:T(128)S(1)}, f32[16]{0:T(128)S(1)}, f32[16]{0:T(128)S(1)}, f32[16]{0:T(128)S(1)}, /*index=5*/f32[16]{0:T(128)S(1)}, f32[1...) while((s32[]{:T(128)}, f32[16]{0:T(128)S(1)}, ...), condition=%wide.region_22.23_spmd.clone, body=%wide.region_19.22_spmd.clone.sunk | while | flops 180 | bytes 711 | solution.py:31
  1135.5 14.2 multiply_convert_fusion.1
  1226.9 13.1 all-reduce.9
  1248.5 25.3 %reduce-scatter.23.cloned.1.call-done = f32[256,1536]{1,0:T(8,128)} async-done(((f32[1024,1536]{1,0:T(8,128)}), f32[256,1536]{1,0:T(8,128)}) %reduce-scatter.23.cloned.1.call-update) | async-done | bytes 1572880 | tf_op jit(solution)/shard_map/reduce_scatter | solution.py:287
  1275.6 44.7 %all-reduce.8 = (f32[1536]{0:T(1024)S(1)}, f32[1536]{0:T(1024)S(1)}, f32[1536]{0:T(1024)S(1)}, f32[1536]{0:T(1024)S(1)}) all-reduce(f32[1536]{0:T(1024)S(1)} %get-tuple-element.717, f32[1536]{0:T(1024)S(1)} %get-tuple-element.720, f32[1536]{0:T(1024)S(1)} %get-tuple-element.719, ...), channel_id=7, replica_groups=mesh['dp'=8,'mp'=4] {'dp','mp'}, use_global_device_ids=true, to_apply=%region_26.27.clone | all-reduce | flops 6144 | bytes 49152
  1322.7 65.6 %reduce-scatter.19.cloned.1.call-done = f32[256,1536]{1,0:T(8,128)} async-done(((f32[1024,1536]{1,0:T(8,128)}), f32[256,1536]{1,0:T(8,128)}) %reduce-scatter.19.cloned.1.call-update) | async-done | bytes 1572880 | tf_op jit(solution)/shard_map/reduce_scatter | solution.py:185
  1393.1 61.4 %reduce-scatter.31.cloned.1.call-done = f32[192,1024]{1,0:T(8,128)} async-done(((f32[1536,1024]{1,0:T(8,128)}), f32[192,1024]{1,0:T(8,128)}) %reduce-scatter.31.cloned.1.call-update) | async-done | bytes 786448 | tf_op jit(solution)/shard_map/reduce_scatter | solution.py:303
  1454.5 66.0 %reduce-scatter.33.cloned.1.call-done = f32[192,1024]{1,0:T(8,128)} async-done(((f32[1536,1024]{1,0:T(8,128)}), f32[192,1024]{1,0:T(8,128)}) %reduce-scatter.33.cloned.1.call-update) | async-done | bytes 786448 | tf_op jit(solution)/shard_map/reduce_scatter | solution.py:304
  1520.5 65.7 %reduce-scatter.35.cloned.1.call-done = f32[1024,192]{0,1:T(8,128)} async-done(((f32[1024,1536]{0,1:T(8,128)}), f32[1024,192]{0,1:T(8,128)}) %reduce-scatter.35.cloned.1.call-update) | async-done | bytes 786448 | tf_op jit(solution)/shard_map/reduce_scatter | solution.py:305
  1586.2 46.8 %reduce-scatter.25.cloned.1.call-done = f32[384,192]{0,1:T(8,128)} async-done(((f32[384,1536]{0,1:T(8,128)}), f32[384,192]{0,1:T(8,128)}) %reduce-scatter.25.cloned.1.call-update) | async-done | bytes 294928 | tf_op jit(solution)/shard_map/reduce_scatter | solution.py:301
  1633.0 80.6 %reduce-scatter.27.cloned.1.call-done = f32[192,1536]{1,0:T(8,128)} async-done(((f32[1536,1536]{1,0:T(8,128)}), f32[192,1536]{1,0:T(8,128)}) %reduce-scatter.27.cloned.1.call-update) | async-done | bytes 1179664 | tf_op jit(solution)/shard_map/reduce_scatter | solution.py:300
  1713.6 80.4 %reduce-scatter.29.cloned.1.call-done = f32[1536,192]{0,1:T(8,128)} async-done(((f32[1536,1536]{0,1:T(8,128)}), f32[1536,192]{0,1:T(8,128)}) %reduce-scatter.29.cloned.1.call-update) | async-done | bytes 1179664 | tf_op jit(solution)/shard_map/reduce_scatter | solution.py:302
  (614 shorter events, 466.6 us)
Async XLA Ops:
  7.2 112.8 %all-gather.13.cloned.1.call-start = ((), (), s32[]{:S(2)}) async-start(), calls=%async_computation.12 | async-start | bytes 3932160 | tf_op jit(solution)/shard_map/all_gather | solution.py:113
  55.6 104.3 %all-gather.15.cloned.1.call-start = ((), (), s32[]{:S(2)}) async-start(), calls=%async_computation.13 | async-start | bytes 5308416 | tf_op jit(solution)/shard_map/all_gather | solution.py:91
  56.4 139.5 %all-gather.19.cloned.1.call-start = ((), (), s32[]{:S(2)}) async-start(), calls=%async_computation.15 | async-start | bytes 3981312 | tf_op jit(solution)/shard_map/all_gather | solution.py:90
  57.1 179.4 %all-gather.17.cloned.1.call-start = ((), (), s32[]{:S(2)}) async-start(), calls=%async_computation.14 | async-start | bytes 5308416 | tf_op jit(solution)/shard_map/all_gather | solution.py:93
  57.7 204.7 %all-gather.21.cloned.1.call-start = ((), (), s32[]{:S(2)}) async-start(), calls=%async_computation.16 | async-start | bytes 1327104 | tf_op jit(solution)/shard_map/all_gather | solution.py:92
  58.3 322.5 %reduce-scatter.17.cloned.1.call-start = ((), (), s32[]{:S(2)}) async-start(), calls=%async_computation.18 | async-start | bytes 5242880 | tf_op jit(solution)/shard_map/reduce_scatter | solution.py:159
  176.8 278.1 %reduce-scatter.15.cloned.1.call-start = ((), (), s32[]{:S(2)}) async-start(), calls=%async_computation.17 | async-start | bytes 7864320 | tf_op jit(solution)/shard_map/reduce_scatter | solution.py:160
  270.1 220.0 %all-gather.25.cloned.1.call-start = ((), (), s32[]{:S(2)}) async-start(), calls=%async_computation.20 | async-start | bytes 3538944 | tf_op jit(solution)/shard_map/all_gather | solution.py:94
  270.9 284.5 %all-gather.23.cloned.1.call-start = ((), (), s32[]{:S(2)}) async-start(), calls=%async_computation.19 | async-start | bytes 3932160 | tf_op jit(solution)/shard_map/all_gather | solution.py:170
  272.2 548.2 %copy-start.26 = (f32[1536]{0:T(1024)}, f32[1536]{0:T(1024)S(1)}, u32[]{:S(2)}) copy-start(f32[1536]{0:T(1024)S(1)} %convert_element_type.116) | copy-start | bytes 18436
  291.6 163.3 %copy-start.9 = (bf16[256,1536]{1,0:T(8,128)(2,1)S(1)}, bf16[256,1536]{1,0:T(8,128)(2,1)}, u32[]{:S(2)}) copy-start(bf16[256,1536]{1,0:T(8,128)(2,1)} %param.23) | copy-start | bytes 2359300
  458.6 361.9 %copy-start.5 = (f32[256,1536]{1,0:T(8,128)}, f32[256,1536]{1,0:T(8,128)S(1)}, u32[]{:S(2)}) copy-start(f32[256,1536]{1,0:T(8,128)S(1)} %get-tuple-element.856) | copy-start | bytes 4718596
  458.6 361.8 %copy-start.37 = (f32[256]{0:T(256)}, f32[256]{0:T(256)S(1)}, u32[]{:S(2)}) copy-start(f32[256]{0:T(256)S(1)} %add_rsqrt_fusion) | copy-start | bytes 3076
  459.9 128.9 %all-gather.27.cloned.1.call-start = ((), (), s32[]{:S(2)}) async-start(), calls=%async_computation.21 | async-start | bytes 3538944 | tf_op jit(solution)/shard_map/all_gather | solution.py:95
  460.5 193.0 %all-gather.31.cloned.1.call-start = ((), (), s32[]{:S(2)}) async-start(), calls=%async_computation.24 | async-start | bytes 3932160 | tf_op jit(solution)/shard_map/all_gather | solution.py:171
  461.2 225.7 %all-gather.29.cloned.1.call-start = ((), (), s32[]{:S(2)}) async-start(), calls=%async_computation.22 | async-start | bytes 3538944 | tf_op jit(solution)/shard_map/all_gather | solution.py:96
  461.8 356.1 %reduce-scatter.21.cloned.1.call-start = ((), (), s32[]{:S(2)}) async-start(), calls=%async_computation.25 | async-start | bytes 7864320 | tf_op jit(solution)/shard_map/reduce_scatter | solution.py:186
  707.4 179.9 %all-gather.33.cloned.1.call-start = ((), (), s32[]{:S(2)}) async-start(), calls=%async_computation.26 | async-start | bytes 3932160 | tf_op jit(solution)/shard_map/all_gather | solution.py:216
  823.2 293.8 %all-gather.35.cloned.1.call-start = ((), (), s32[]{:S(2)}) async-start(), calls=%async_computation.27 | async-start | bytes 2621440 | tf_op jit(solution)/shard_map/all_gather | solution.py:217
  834.1 409.6 %reduce-scatter.37.cloned.1.call-start = ((), (), s32[]{:S(2)}) async-start(), calls=%async_computation.35 | async-start | bytes 7962624
  986.0 287.8 %reduce-scatter.23.cloned.1.call-start = ((), (), s32[]{:S(2)}) async-start(), calls=%async_computation.28 | async-start | bytes 7864320 | tf_op jit(solution)/shard_map/reduce_scatter | solution.py:287
  1164.2 224.1 %reduce-scatter.19.cloned.1.call-start = ((), (), s32[]{:S(2)}) async-start(), calls=%async_computation.23 | async-start | bytes 7864320 | tf_op jit(solution)/shard_map/reduce_scatter | solution.py:185
  1172.9 281.7 %reduce-scatter.31.cloned.1.call-start = ((), (), s32[]{:S(2)}) async-start(), calls=%async_computation.32 | async-start | bytes 7077888 | tf_op jit(solution)/shard_map/reduce_scatter | solution.py:303
  1181.6 338.9 %reduce-scatter.33.cloned.1.call-start = ((), (), s32[]{:S(2)}) async-start(), calls=%async_computation.33 | async-start | bytes 7077888 | tf_op jit(solution)/shard_map/reduce_scatter | solution.py:304
  1190.3 395.9 %reduce-scatter.35.cloned.1.call-start = ((), (), s32[]{:S(2)}) async-start(), calls=%async_computation.34 | async-start | bytes 7077888 | tf_op jit(solution)/shard_map/reduce_scatter | solution.py:305
  1199.2 433.8 %reduce-scatter.25.cloned.1.call-start = ((), (), s32[]{:S(2)}) async-start(), calls=%async_computation.29 | async-start | bytes 2654208 | tf_op jit(solution)/shard_map/reduce_scatter | solution.py:301
  1204.7 508.9 %reduce-scatter.27.cloned.1.call-start = ((), (), s32[]{:S(2)}) async-start(), calls=%async_computation.30 | async-start | bytes 10616832 | tf_op jit(solution)/shard_map/reduce_scatter | solution.py:300
  1214.2 579.8 %reduce-scatter.29.cloned.1.call-start = ((), (), s32[]{:S(2)}) async-start(), calls=%async_computation.31 | async-start | bytes 10616832 | tf_op jit(solution)/shard_map/reduce_scatter | solution.py:302
  1243.7 144.7 %copy-start.6 = (f32[256,1536]{1,0:T(8,128)S(1)}, f32[256,1536]{1,0:T(8,128)}, u32[]{:S(2)}) copy-start(f32[256,1536]{1,0:T(8,128)} %copy-done.5) | copy-start | bytes 4718596
  1243.7 144.7 %copy-start.17 = (bf16[256,1536]{1,0:T(8,128)(2,1)S(1)}, bf16[256,1536]{1,0:T(8,128)(2,1)}, u32[]{:S(2)}) copy-start(bf16[256,1536]{1,0:T(8,128)(2,1)} %param.24) | copy-start | bytes 2359300
  1243.7 144.6 %copy-start.27 = (f32[1536]{0:T(1024)S(1)}, f32[1536]{0:T(1024)}, u32[]{:S(2)}) copy-start(f32[1536]{0:T(1024)} %copy-done.26) | copy-start | bytes 18436
  1243.7 144.6 %copy-start.38 = (f32[256]{0:T(256)S(1)}, f32[256]{0:T(256)}, u32[]{:S(2)}) copy-start(f32[256]{0:T(256)} %copy-done.37) | copy-start | bytes 3076
  (67 other events, 1347.4 us)
Sparse Core Ops, SparseCore 0:
  55.8 64.2 all-gather.12
  121.9 38.0 all-gather.14
  161.9 33.9 all-gather.18
  197.6 38.9 all-gather.16
  238.3 24.0 all-gather.20
  264.5 76.6 reduce-scatter.16
  343.7 111.1 reduce-scatter.14
  456.9 33.1 all-gather.24
  492.3 63.0 all-gather.22
  557.3 31.4 all-gather.26
  590.4 63.0 all-gather.30
  655.4 31.4 all-gather.28
  707.5 110.3 reduce-scatter.20
  823.3 63.9 all-gather.32
  888.7 44.6 all-gather.34
  986.1 64.2 reduce-scatter.36
  1164.3 109.4 reduce-scatter.22
  1276.0 112.3 reduce-scatter.18
  1392.3 62.1 reduce-scatter.30
  1458.7 61.7 reduce-scatter.32
  1524.5 61.7 reduce-scatter.34
  1590.5 42.4 reduce-scatter.24
  1637.1 76.4 reduce-scatter.26
  1717.5 76.4 reduce-scatter.28
where the time goes:
time: 1810 us; the launch traced here: 1800 us
  waiting for transfers between devices  1090 us (60%)
  matrix products  260 us (14%)
  local copies, waits for them, and re-layouts  121 us (7%)
  other arithmetic  116 us (6%)
  blocking collectives  109 us (6%)
  loops' own time  91.6 us (5%)
    reduce_scatter x1, waiting for transfers between devices, on_device(): lax.psum_scatter(normed_two_part, 'mp', scatter_dimension=0, tiled=True)  110 us
    unnamed x2, blocking collectives  85.5 us
    another operation x2, loops' own time, span_weights(): _, table = lax.scan(advance, start, (alpha, eta, keep, basis))  83.5 us
    reduce_scatter x1, waiting for transfers between devices, on_device(): lax.psum_scatter(grad_memory_first, 'dp', scatter_dimension=0, tiled=True)  80.6 us
    reduce_scatter x1, waiting for transfers between devices, on_device(): lax.psum_scatter(grad_memory_second, 'dp', scatter_dimension=1, tiled=True)  80.4 us
    reduce_scatter x1, waiting for transfers between devices, on_device(): lax.psum_scatter(recall_part + attn_part, 'mp', scatter_dimension=0, tile...  71.5 us
    reduce_scatter x1, waiting for transfers between devices, on_device(): lax.psum_scatter(grad_up, 'dp', scatter_dimension=0, tiled=True)  66 us
    reduce_scatter x1, waiting for transfers between devices, on_device(): lax.psum_scatter(grad_down, 'dp', scatter_dimension=1, tiled=True)  65.7 us
  transfers between devices with their start and end apart: 24, of which 21 were waited for; matrix products, arithmetic and copies ran while one was open for 25% of the time, Pallas kernels for 0%

commit v1 on v0

v1 whole, which is shorter than its diff:
```python
import functools

import jax
import jax.numpy as jnp
from jax import lax
from jax.experimental import pallas as pl
from jax.experimental.pallas import tpu as pltpu
from jax.sharding import Mesh
from jax.sharding import PartitionSpec as P

HD = 96
CH = 64
EPS = 1e-06
ALPHA_SHIFT = 1.5
ETA_SHIFT = 0.5
NEG = -1e30
SCALE = HD ** (-0.5)
F32 = jnp.float32
BF16 = jnp.bfloat16
VMEM_LIMIT = 24 * 1024 * 1024

def dot(a, b, ca, cb):
    return lax.dot_general(a, b, (((ca,), (cb,)), ((), ())), preferred_element_type=F32)


def swap(x, axis):
    return lax.ppermute(x, axis, [(0, 1), (1, 0)])


def turn(x):
    return lax.ppermute(x, ("c", "h"), [(0, 0), (1, 2), (2, 1), (3, 3)])


def after(x, *others):
    return lax.optimization_barrier((x,) + others)[0]


def cat(parts, axis=0):
    return jnp.concatenate(parts, axis=axis)


def by_index(index, first, second, axis=0):
    return jnp.where(index == 0, cat([first, second], axis), cat([second, first], axis))


def gather_rows(x):
    c, l = lax.axis_index("c"), lax.axis_index("l")
    half = by_index(l, x, swap(x, "l"))
    return by_index(c, half, swap(half, "c"))


def scatter_rows(x):
    c, l = lax.axis_index("c"), lax.axis_index("l")
    rows = x.shape[0] // 2
    send = lax.dynamic_slice_in_dim(x, (1 - c) * rows, rows, 0).astype(BF16)
    half = lax.dynamic_slice_in_dim(x, c * rows, rows, 0).astype(F32) + swap(send, "c").astype(F32)
    rows = rows // 2
    send = lax.dynamic_slice_in_dim(half, (1 - l) * rows, rows, 0).astype(BF16)
    return lax.dynamic_slice_in_dim(half, l * rows, rows, 0) + swap(send, "l").astype(F32)


def shuffle(plane, v, back=False):
    if len(plane) == 1:
        return v
    share = v.shape[-1] // 4
    b = [v[..., i * share : (i + 1) * share] for i in range(4)]
    if back:
        b = [b[0], b[1], b[3], b[2]]
    x, y = lax.axis_index("x"), lax.axis_index("y")
    b = [jnp.where(x == 0, b[i], b[i ^ 1]) for i in range(4)]
    b = [jnp.where(y == 0, b[i], b[i ^ 2]) for i in range(4)]
    if not back:
        b = [b[0], b[1], b[3], b[2]]
    return cat(b, -1)


def gather_plane(plane, piece, first):
    if len(plane) == 1:
        whole = lax.all_gather(piece, plane, axis=0, tiled=True)
        return whole, piece
    near = {axis: swap(piece, axis) for axis in plane}
    second = "y" if first == "x" else "x"
    far = swap(near[first], second)
    return cat([piece, near["x"], far, near["y"]]), near[first]


def scatter_plane(plane, pairs, first, wait):
    def product(start, stop):
        parts = [dot(left[:, start:stop], right, 0, 0).astype(BF16) for left, right in pairs]
        return cat(parts, 1) if len(parts) > 1 else parts[0]

    width = pairs[0][0].shape[1]
    if len(plane) == 1:
        whole = product(0, width)
        return lax.psum_scatter(whole, plane, scatter_dimension=0, tiled=True).astype(F32)
    w = width // 4
    if first == "x":
        got = swap(wait(product(w, 3 * w)), "x")
        second, mine, other, other_at = "y", got[:w], got[w:], 3
    else:
        got = swap(wait(product(2 * w, 4 * w)), "y")
        second, mine, other, other_at = "x", got[w:], got[:w], 1
    other = product(other_at * w, (other_at + 1) * w).astype(F32) + other.astype(F32)
    other = swap(other.astype(BF16), second)
    mine = product(0, w).astype(F32) + mine.astype(F32)
    return mine + other.astype(F32)


def reduce_group(plane, sources, wait=lambda v: v):
    here = scatter_plane(plane, [(left, right) for left, right, _ in sources], "x", wait)
    there = scatter_plane(plane, [(left, right) for left, _, right in sources], "y", wait)
    mine = here + swap(there.astype(BF16), "h").astype(F32)
    c = lax.axis_index("c")
    rows = mine.shape[0] // 2
    given = lax.dynamic_slice_in_dim(mine, (1 - c) * rows, rows, 0).astype(BF16)
    kept = lax.dynamic_slice_in_dim(mine, c * rows, rows, 0)
    got = swap(given, "c").astype(F32)
    results, start = [], 0
    for _, right, _ in sources:
        n = right.shape[1]
        results.append(by_index(c, kept[:, start : start + n], got[:, start : start + n], 1))
        start += n
    return results


def pack(shards):
    c = lax.axis_index("c")
    low = cat([s[:, : s.shape[1] // 2] for s in shards], 1)
    high = cat([s[:, s.shape[1] // 2 :] for s in shards], 1)
    mine = jnp.where(c == 0, low, high)
    got = swap(jnp.where(c == 0, high, low), "c")
    return by_index(c, mine, got)


def tall(x):
    padding = 128 - x.shape[0]
    wide = cat([x.astype(F32), jnp.zeros((padding, x.shape[1]), F32)])
    return wide.astype(BF16), wide.T.astype(BF16)


def attend_kernel(code_ref, doc_ref, qkv_ref, ctx_ref, lse_ref, bias_ref):
    length = qkv_ref.shape[-1]
    heads = qkv_ref.shape[0] // (3 * HD)
    block = min(256, length)
    fill_bias(code_ref, doc_ref, bias_ref)
    for head in range(heads):
        part = [slice((i * heads + head) * HD, (i * heads + head + 1) * HD) for i in range(3)]
        v = qkv_ref[part[2]]
        q, _ = tall(qkv_ref[part[0]])
        _, k = tall(qkv_ref[part[1]])
        for start in range(0, length, block):
            end = start + block
            cols = slice(start, end)
            s = dot(k[:end], q[:, cols], 1, 0) * SCALE + bias_ref[:end, cols]
            top = jnp.max(s, axis=0, keepdims=True)
            e = jnp.exp(s - top)
            total = jnp.sum(e, axis=0, keepdims=True)
            p = (e * (1.0 / total)).astype(BF16)
            ctx_ref[part[0], cols] = dot(v[:, :end], p, 1, 0).astype(BF16)
            lse_ref[head : head + 1, cols] = top + jnp.log(total)


def fill_bias(code_ref, doc_ref, bias_ref):
    length = bias_ref.shape[0]
    block = min(256, length)
    for start in range(0, length, block):
        u = start + lax.broadcasted_iota(jnp.int32, (block, length), 0)
        t = lax.broadcasted_iota(jnp.int32, (block, length), 1)
        same = code_ref[start : start + block, :] == doc_ref[...]
        allow = ((u <= t) & same) | (u == t)
        bias_ref[start : start + block, :] = jnp.where(allow, 0.0, NEG)


def attend_back_kernel(code_ref, doc_ref, qkv_ref, lse_ref, grad_ref, out_ref, bias_ref, acc_ref):
    length = qkv_ref.shape[-1]
    heads = qkv_ref.shape[0] // (3 * HD)
    block = min(256, length)
    fill_bias(code_ref, doc_ref, bias_ref)
    for head in range(heads):
        part = [slice((i * heads + head) * HD, (i * heads + head + 1) * HD) for i in range(3)]
        q, kt, g = qkv_ref[part[0]], qkv_ref[part[1]], grad_ref[part[0]]
        q_wide, _ = tall(q)
        g_wide, _ = tall(g)
        _, k = tall(kt)
        _, v = tall(qkv_ref[part[2]])
        acc_ref[...] = jnp.zeros_like(acc_ref)
        for start in range(0, length, block):
            end = start + block
            cols = slice(start, end)
            s = dot(k[:end], q_wide[:, cols], 1, 0) * SCALE + bias_ref[:end, cols]
            p = jnp.exp(s - lse_ref[head : head + 1, cols])
            dp = dot(v[:end], g_wide[:, cols], 1, 0)
            inner = jnp.sum(p * dp, axis=0, keepdims=True)
            ds = (p * (dp - inner)).astype(BF16)
            out_ref[part[0], cols] = (dot(kt[:, :end], ds, 1, 0) * SCALE).astype(BF16)
            acc_ref[0, :, :end] += dot(q[:, cols], ds, 1, 1)
            acc_ref[1, :, :end] += dot(g[:, cols], p.astype(BF16), 1, 1)
        out_ref[part[1]] = (acc_ref[0] * SCALE).astype(BF16)
        out_ref[part[2]] = acc_ref[1].astype(BF16)


def attend(code, doc, qkv):
    heads, length = qkv.shape[0] // (3 * HD), qkv.shape[1]
    return pl.pallas_call(
        attend_kernel,
        out_shape=[
            jax.ShapeDtypeStruct((heads * HD, length), BF16),
            jax.ShapeDtypeStruct((heads, length), F32),
        ],
        scratch_shapes=[pltpu.VMEM((length, length), F32)],
        compiler_params=pltpu.CompilerParams(vmem_limit_bytes=VMEM_LIMIT),
        cost_estimate=pl.CostEstimate(
            flops=heads * length * length * HD * 4,
            bytes_accessed=heads * HD * length * 8,
            transcendentals=heads * length * length,
        ),
    )(code, doc, qkv)


def attend_back(code, doc, qkv, lse, grad):
    heads, length = qkv.shape[0] // (3 * HD), qkv.shape[1]
    return pl.pallas_call(
        attend_back_kernel,
        out_shape=jax.ShapeDtypeStruct(qkv.shape, BF16),
        scratch_shapes=[pltpu.VMEM((length, length), F32), pltpu.VMEM((2, HD, length), F32)],
        compiler_params=pltpu.CompilerParams(vmem_limit_bytes=VMEM_LIMIT),
        cost_estimate=pl.CostEstimate(
            flops=heads * length * length * HD * 10,
            bytes_accessed=heads * HD * length * 14,
            transcendentals=heads * length * length,
        ),
    )(code, doc, qkv, lse, grad)


def table_kernel(alpha_ref, eta_ref, keep_ref, table_ref, state_ref):
    spans = table_ref.shape[0]
    place = lax.broadcasted_iota(jnp.int32, (1, table_ref.shape[1]), 1)
    state = jnp.zeros((1, table_ref.shape[1]), F32)
    memory = jnp.zeros((1, table_ref.shape[1]), F32)
    for c in range(spans):
        kept = keep_ref[c : c + 1, :]
        table_ref[c : c + 1, :] = memory * kept
        state_ref[c : c + 1, :] = state * kept
        state = eta_ref[c : c + 1, :] * kept * state + jnp.where(place == c, 1.0, 0.0)
        memory = alpha_ref[c : c + 1, :] * kept * memory + state


def table_back_kernel(alpha_ref, eta_ref, keep_ref, table_ref, state_ref, grad_ref, out_ref, ga_ref, ge_ref):
    spans = table_ref.shape[0]
    wide = (1, table_ref.shape[1])
    grad_state = jnp.zeros(wide, F32)
    grad_memory = jnp.zeros(wide, F32)
    for c in reversed(range(spans)):
        kept = keep_ref[c : c + 1, :]
        grad_state = grad_state + grad_memory
        ga_ref[c : c + 1, :] = grad_memory * table_ref[c : c + 1, :]
        ge_ref[c : c + 1, :] = grad_state * state_ref[c : c + 1, :]
        grad_state = eta_ref[c : c + 1, :] * kept * grad_state
        grad_memory = kept * (alpha_ref[c : c + 1, :] * grad_memory + grad_ref[c : c + 1, :])
    out_ref[0] = jnp.broadcast_to(jnp.sum(ga_ref[...], axis=1, keepdims=True), out_ref.shape[1:])
    out_ref[1] = jnp.broadcast_to(jnp.sum(ge_ref[...], axis=1, keepdims=True), out_ref.shape[1:])


def span_table(alpha, eta, keep):
    spans = alpha.shape[0]
    wide = lambda v: jnp.broadcast_to(v[:, None], (spans, 128))
    square = jax.ShapeDtypeStruct((spans, 128), F32)
    args = (wide(alpha), wide(eta), wide(keep))
    table, state = pl.pallas_call(table_kernel, out_shape=[square, square])(*args)
    return table, (args, table, state)


def span_table_back(kept, grad):
    args, table, state = kept
    spans = table.shape[0]
    scratch = pltpu.VMEM((spans, 128), F32)
    grad = jnp.pad(grad, ((0, 0), (0, 128 - grad.shape[1])))
    both = pl.pallas_call(
        table_back_kernel,
        out_shape=jax.ShapeDtypeStruct((2, spans, 128), F32),
        scratch_shapes=[scratch, scratch],
    )(*args, table, state, grad)
    return both[0, :, 0], both[1, :, 0]


def norm_back(values, inverse, gain, grad):
    scaled = grad * gain
    inner = jnp.mean(values * scaled, axis=-1, keepdims=True)
    grad_values = inverse * scaled - values * inverse * inverse * inverse * inner
    grad_gain = jnp.sum(grad * values * inverse, axis=0)
    return grad_values, grad_gain


def inverse_of(values):
    return lax.rsqrt(jnp.mean(values * values, axis=-1, keepdims=True) + EPS)


def all_sum(plane, v):
    for axis in ("l", "h", "c"):
        v = v + swap(v, axis)
    if len(plane) == 1:
        return lax.psum(v, plane)
    for axis in ("x", "y"):
        v = v + swap(v, axis)
    return v


def all_parts(plane, v):
    for axis in ("l", "h", "c"):
        v = by_index(lax.axis_index(axis), v, swap(v, axis))
    if len(plane) == 1:
        return lax.all_gather(v, plane, axis=0, tiled=True)
    for axis in ("x", "y"):
        v = by_index(lax.axis_index(axis), v, swap(v, axis))
    return v


def on_device(
    plane,
    block_in,
    grad_out,
    resets,
    counts,
    gain_in,
    w_forget,
    w_momentum,
    project_in,
    project_out,
    memory_in,
    memory_out,
    gain_mid,
    gate_weight,
    up_weight,
    down_weight,
):
    relative = functools.partial(shuffle, plane)
    absolute = functools.partial(shuffle, plane, back=True)
    c, l = lax.axis_index("c"), lax.axis_index("l")
    quarter, width = block_in.shape
    length = 4 * quarter
    spans = length // CH
    own_spans = quarter // CH
    member = 2 * c + l
    hidden_units = 4 * memory_in.shape[1]
    units, q_cols, ff = memory_in.shape[1] // 2, project_in.shape[2] // 2, gate_weight.shape[1] // 2

    x_own = relative(turn(block_in))
    flags = turn(cat([resets, counts[:, None]], 1))
    packed = [
        pack([memory_in, project_in[0], project_in[1], project_in[2]]),
        pack([memory_out.T, project_out.T]),
        pack([gate_weight, up_weight, down_weight.T]),
    ]
    far = [swap(packed[0], "h")]
    far.append(swap(after(packed[1], far[0]), "h"))
    far.append(swap(after(packed[2], far[1]), "h"))
    stages = [
        (packed[0], "x"),
        (packed[1], "y"),
        (far[0], "x"),
        (far[1], "y"),
        (packed[2], "x"),
        (far[2], "y"),
    ]
    weights, done = [], None
    for piece, first in stages:
        whole, done = gather_plane(plane, piece if done is None else after(piece, done), first)
        weights.append(whole)
    first_layer, second_layer, feed = (
        (weights[0], weights[2]),
        (weights[1], weights[3]),
        (weights[4], weights[5]),
    )
    both = range(2)

    x_full = gather_rows(x_own)
    vectors = cat([v[None] for v in (gain_in, w_forget, w_momentum, gain_mid)], 0).astype(F32)
    vectors = all_parts(plane, vectors[None])
    vectors = relative(jnp.swapaxes(vectors, 0, 1).reshape(4, width))
    gain_one, gain_two, gates = vectors[0], vectors[3], vectors[1:3]

    resets, count = flags[0, :-1], flags[0, -1]
    positions = jnp.arange(length, dtype=jnp.int32)
    valid = (positions < count).astype(F32)
    keep = (1 - resets).astype(F32)
    doc = jnp.repeat(jnp.cumsum(resets, dtype=jnp.int32), CH).astype(F32)
    code = jnp.where(valid > 0, doc, -1.0)[:, None]
    doc = doc[None, :]

    x_wide = x_full.astype(F32)
    normed = (x_wide * inverse_of(x_wide) * gain_one).astype(BF16)
    x_own = x_own.astype(F32)
    inverse_one = inverse_of(x_own)
    span_sums = jnp.sum(normed.reshape(spans, CH, width).astype(F32), axis=1)
    logits = jnp.sum(span_sums[None] * gates[:, None, :], axis=2) / CH
    alpha = jax.nn.sigmoid(logits[0] + ALPHA_SHIFT)
    eta = jax.nn.sigmoid(logits[1] + ETA_SHIFT)
    table, kept_table = span_table(alpha, eta, keep)

    act, slope_pre, qkv, ctx, lse = [], [], [], [], []
    for i in both:
        pre = dot(normed, first_layer[i][:, :units], 1, 0)
        sig_pre = jax.nn.sigmoid(pre)
        act.append((pre * sig_pre).astype(BF16))
        slope_pre.append((sig_pre * (1.0 + pre * (1.0 - sig_pre))).astype(BF16))
        qkv.append(dot(first_layer[i][:, units:], normed, 0, 1).astype(BF16))
    sim = scatter_rows((dot(act[0], act[0], 1, 1) + dot(act[1], act[1], 1, 1)) / hidden_units)
    for i in both:
        context, logsum = attend(code, doc, qkv[i])
        ctx.append(context)
        lse.append(logsum)
    out_own = scatter_rows(
        sum(dot(act[i], second_layer[i][:, :units], 1, 1) for i in both)
        + sum(dot(ctx[i], second_layer[i][:, units:], 0, 1) for i in both)
    )
    table_own = lax.dynamic_slice_in_dim(table[:, :spans], member * own_spans, own_spans, 0)
    spread = jnp.repeat(jnp.repeat(table_own, CH, axis=0), CH, axis=1)
    mixing = (sim * spread * valid[None, :] / CH).astype(BF16)
    middle = x_own + out_own + dot(mixing, normed, 1, 0)
    inverse_two = inverse_of(middle)
    mid = (middle * inverse_two * gain_two).astype(BF16)
    mid_all = gather_rows(mid)
    grad_own = relative(turn(grad_out))
    grad_all = gather_rows(grad_own)

    hidden, grad_gate_pre, grad_up_pre = [], [], []
    for i in both:
        gate = dot(mid_all, feed[i][:, :ff], 1, 0)
        up = dot(mid_all, feed[i][:, ff : 2 * ff], 1, 0)
        grad_hidden = dot(grad_all, feed[i][:, 2 * ff :], 1, 0)
        sigma = jax.nn.sigmoid(gate)
        swish = gate * sigma
        hidden.append((swish * up).astype(BF16))
        grad_gate_pre.append((grad_hidden * up * (sigma * (1.0 + gate * (1.0 - sigma)))).astype(BF16))
        grad_up_pre.append((grad_hidden * swish).astype(BF16))
    grad_mid = scatter_rows(
        sum(
            dot(grad_gate_pre[i], feed[i][:, :ff], 1, 1) + dot(grad_up_pre[i], feed[i][:, ff : 2 * ff], 1, 1)
            for i in both
        )
    )
    ffn_own = scatter_rows(sum(dot(hidden[i], feed[i][:, 2 * ff :], 1, 1) for i in both))
    block_out = turn(absolute((middle + ffn_own).astype(BF16)))
    grad_gate, grad_up, grad_down = reduce_group(
        plane, [(mid_all, *grad_gate_pre), (mid_all, *grad_up_pre), (grad_all, *hidden)]
    )

    back_two, grad_gain_two = norm_back(middle, inverse_two, gain_two, grad_mid)
    grad_middle = grad_own.astype(F32) + back_two
    branch = grad_middle.astype(BF16)
    branch_all = gather_rows(branch)
    scaled = dot(branch, normed, 1, 1) / CH * valid[None, :]
    grad_sim = gather_rows((scaled * spread).astype(BF16))
    grad_blocks = jnp.sum((scaled * sim).reshape(own_spans, CH, spans, CH), axis=(1, 3))
    grad_table = lax.dynamic_update_slice_in_dim(
        jnp.zeros((spans, spans), F32), grad_blocks, member * own_spans, 0
    )
    for axis in ("c", "l"):
        grad_table = grad_table + swap(grad_table, axis)
    grad_alpha, grad_eta = span_table_back(kept_table, grad_table)
    grad_logits = jnp.stack([grad_alpha * alpha * (1.0 - alpha), grad_eta * eta * (1.0 - eta)]) / CH
    grad_vectors = jnp.sum(grad_logits[:, :, None] * span_sums[None], axis=1)
    own_logits = lax.dynamic_slice_in_dim(grad_logits, member * own_spans, own_spans, 1)
    grad_spans = jnp.sum(own_logits[:, :, None] * gates[:, None, :], axis=0)

    grad_memory_out, grad_project_out = reduce_group(
        plane, [(branch_all, *act), (branch_all, ctx[0].T, ctx[1].T)]
    )
    symmetric = (grad_sim.astype(F32) + grad_sim.T.astype(F32)).astype(BF16)
    grad_pre, grad_qkv = [], []
    for i in both:
        grad_act = (
            dot(branch_all, second_layer[i][:, :units], 1, 0) + dot(symmetric, act[i], 1, 0) / hidden_units
        )
        grad_pre.append((grad_act * slope_pre[i].astype(F32)).astype(BF16))
    (grad_memory_in,) = reduce_group(plane, [(normed, *grad_pre)])
    for i in both:
        grad_ctx = dot(second_layer[i][:, units:], branch_all, 0, 1).astype(BF16)
        grad_qkv.append(attend_back(code, doc, qkv[i], lse[i], grad_ctx))
    (grad_qkv_sum,) = reduce_group(plane, [(normed, grad_qkv[0].T, grad_qkv[1].T)])
    grad_normed = scatter_rows(
        dot(mixing, branch, 0, 0)
        + sum(
            dot(grad_pre[i], first_layer[i][:, :units], 1, 1)
            + dot(grad_qkv[i], first_layer[i][:, units:], 0, 1)
            for i in both
        )
    )
    grad_normed = grad_normed + jnp.repeat(grad_spans, CH, axis=0)
    back_one, grad_gain_one = norm_back(x_own, inverse_one, gain_one, grad_normed)
    grad_block_in = turn(absolute((grad_middle + back_one).astype(BF16))).astype(F32)

    gram = 0.0
    for i in both:
        blocks = act[i].reshape(spans, CH, -1)
        gram = gram + jnp.einsum("cth,csh->cts", blocks, blocks, preferred_element_type=F32)
    written = (normed * valid[:, None].astype(BF16)).reshape(spans, CH, width)
    cross = jnp.einsum("ctd,csd->cts", written, written, preferred_element_type=F32)
    piece = jnp.sum(gram * cross, axis=(1, 2))
    for axis in ("c", "l"):
        piece = piece + swap(piece, axis)
    surprise = jnp.sqrt(piece / (hidden_units * width * CH))
    weight = jnp.sum(valid.reshape(spans, CH), axis=1)
    numbers = jnp.stack(
        [jnp.sum(weight * surprise), jnp.sum(weight * alpha), jnp.sum(weight * eta), jnp.sum(weight)]
    )
    small = jnp.stack([grad_gain_one, grad_vectors[0] * 0.25, grad_vectors[1] * 0.25, grad_gain_two])
    small = cat([absolute(small), jnp.pad(numbers[None], ((0, 0), (0, width - 4)))], 0)
    small = all_sum(plane, small)
    logged = small[4, :3] / small[4, 3]
    share = gain_in.shape[0]
    index = lax.axis_index(plane + ("c", "h", "l"))
    mine = lax.dynamic_slice_in_dim(small, index * share, share, 1)
    grad_project_in = jnp.stack(
        [
            cat([grad_qkv_sum[:, (3 * j + i) * q_cols : (3 * j + i + 1) * q_cols] for j in both], 1)
            for i in range(3)
        ]
    )
    return (
        block_out,
        grad_block_in,
        mine[0],
        mine[1],
        mine[2],
        grad_project_in,
        grad_project_out.T,
        grad_memory_in,
        grad_memory_out.T,
        mine[3],
        grad_gate,
        grad_up,
        grad_down.T,
        logged,
    )


def solution(mesh):
    chips, line = mesh.shape["dp"] // 2, mesh.shape["mp"]
    if chips == 4:
        plane, sizes = ("y", "x"), (2, 2)
    else:
        plane, sizes = ("p",), (chips,)
    fine = Mesh(mesh.devices.reshape(sizes + (2, line // 2, 2)), plane + ("c", "h", "l"))
    dp, mp = plane + ("c",), ("h", "l")
    every = dp + mp
    placed = (
        P(every, None),
        P(every, None),
        P(dp, None),
        P(dp),
        P(every),
        P(every),
        P(every),
        P(None, dp, mp),
        P(mp, dp),
        P(dp, mp),
        P(mp, dp),
        P(every),
        P(dp, mp),
        P(dp, mp),
        P(mp, dp),
    )
    return jax.shard_map(
        functools.partial(on_device, plane),
        mesh=fine,
        in_specs=placed,
        out_specs=(
            P(every, None),
            P(every, None),
            P(every),
            P(every),
            P(every),
            P(None, dp, mp),
            P(mp, dp),
            P(dp, mp),
            P(mp, dp),
            P(every),
            P(dp, mp),
            P(dp, mp),
            P(mp, dp),
            P(),
        ),
        check_vma=False,
    )
```

time: 1810 us -> 903 us (0.50)
  waiting for transfers between devices: 1090 us -> 340 us
  blocking collectives: 109 us -> 0 us
  starting transfers between devices: 1.76 us -> 105 us
  loops' own time: 91.6 us -> 0 us
  matrix products: 260 us -> 204 us
  local copies, waits for them, and re-layouts: 121 us -> 87.4 us
  Pallas kernels: 0 us -> 22.7 us
    reduce_scatter x11 -> x0, waiting for transfers between devices: 674 us -> none  [the longest x1 110 us: on_device(): lax.psum_scatter(normed_two_part, 'mp', scatter_dimension=0, tiled=True)]
    all_gather x12 -> x0, waiting for transfers between devices: 407 us -> none  [the longest x1 65.3 us: on_device(): lax.all_gather(normed_two_low, 'mp', axis=0, tiled=True)]
    ppermute x0 -> x87, waiting for transfers between devices: none -> 340 us  [the longest x82 302 us: swap(): return lax.ppermute(x, axis, [(0, 1), (1, 0)])]
    ppermute x0 -> x87, starting transfers between devices: none -> 105 us  [the longest x82 86.4 us: swap(): return lax.ppermute(x, axis, [(0, 1), (1, 0)])]
    another operation x4 -> x0, loops' own time: 91.6 us -> none  [the longest x2 83.5 us: span_weights(): _, table = lax.scan(advance, start, (alpha, eta, keep, basis))]
    unnamed x2 -> x0, blocking collectives: 85.5 us -> none
    dynamic_slice x106 -> x6, local copies, waits for them, and re-layouts: 60.1 us -> 1.18 us  [the longest x2 0.77 us: on_device(): lax.dynamic_slice_in_dim(table[:, :spans], member * own_spans, own_spans, 0)]
    dot_general x46 -> x80, matrix products: 260 us -> 204 us  [the longest x77 201 us: dot(): lax.dot_general(a, b, (((ca,), (cb,)), ((), ())), preferred_element_type=...]
  transfers between devices with their start and end apart: 24 -> 87, of which waited for: 21 -> 24; matrix products, arithmetic and copies ran while one was open for 25% -> 40% of each run, Pallas kernels for 0% -> 3%
where the time goes in v1:
time: 903 us; the launch traced here: 897 us
  waiting for transfers between devices  340 us (38%)
  matrix products  204 us (23%)
  other arithmetic  133 us (15%)
  starting transfers between devices  105 us (12%)
  local copies, waits for them, and re-layouts  87.4 us (10%)
  Pallas kernels  22.7 us (3%)
    ppermute x82, waiting for transfers between devices, swap(): return lax.ppermute(x, axis, [(0, 1), (1, 0)])  302 us
    dot_general x77, matrix products, dot(): lax.dot_general(a, b, (((ca,), (cb,)), ((), ())), preferred_element_type=...  201 us
    ppermute x82, starting transfers between devices, swap(): return lax.ppermute(x, axis, [(0, 1), (1, 0)])  86.4 us
    select_n x18, other arithmetic, by_index(): jnp.where(index == 0, cat([first, second], axis), cat([second, first], ax...  39.6 us
    ppermute x5, waiting for transfers between devices, turn(): return lax.ppermute(x, ('c', 'h'), [(0, 0), (1, 2), (2, 1), (3, 3)])  38.2 us
    unnamed x284, local copies, waits for them, and re-layouts  32.2 us
    ppermute x5, starting transfers between devices, turn(): return lax.ppermute(x, ('c', 'h'), [(0, 0), (1, 2), (2, 1), (3, 3)])  19.1 us
    concatenate x11, other arithmetic, cat(): return jnp.concatenate(parts, axis=axis)  18.9 us
  transfers between devices with their start and end apart: 87, of which 24 were waited for; matrix products, arithmetic and copies ran while one was open for 40% of the time, Pallas kernels for 3%

profile of v1, /device:TPU:1, one launch (start us, length us, event | category | flops | bytes accessed | tf_op | source)
XLA Modules:
  0.0 896.8 jit_solution(17914605346926277548)
XLA Ops:
  2.1 5.6 collective-permute-start.24
  21.7 5.2 collective-permute-start.4
  32.2 9.0 %collective-permute-start.5 = (f32[4,4,48]{2,1,0:T(4,128)S(1)}, f32[4,4,48]{2,1,0:T(4,128)S(1)}, u32[]{:S(2)}, u32[]{:S(2)}) collective-permute-start(f32[4,4,48]{2,1,0:T(4,128)S(1)} %maximum_select_fusion.23), channel_id=1, source_target_pairs={{0,4},{4,0},{1,5},{5,1},{2,6},{6,2},{3,7},{7,3},{8,12},{12,8},{9,1... | collective-permute-start | bytes 9224 | tf_op jit(solution)/shard_map/ppermute | solution.py:27
  68.8 32.1 %collective-permute-done.42 = bf16[256,1536]{1,0:T(8,128)(2,1)} collective-permute-done((bf16[256,1536]{1,0:T(8,128)(2,1)}, bf16[256,1536]{1,0:T(8,128)(2,1)}, u32[]{:S(2)}, u32[]{:S(2)}) %collective-permute-start.42) | collective-permute-done | bytes 786464 | tf_op jit(solution)/shard_map/ppermute | solution.py:31
  120.9 27.8 %collective-permute-done.43 = bf16[256,1536]{1,0:T(8,128)(2,1)} collective-permute-done((bf16[256,1536]{1,0:T(8,128)(2,1)}, bf16[256,1536]{1,0:T(8,128)(2,1)}, u32[]{:S(2)}, u32[]{:S(2)}) %collective-permute-start.43) | collective-permute-done | bytes 786464 | tf_op jit(solution)/shard_map/ppermute | solution.py:27
  150.5 11.5 %maximum_select_fusion.7 = bf16[512,1536]{1,0:T(8,128)(2,1)} fusion(bf16[256,1536]{1,0:T(8,128)(2,1)} %collective-permute-done.43, bf16[256,384]{1,0:T(8,128)(2,1)S(1)} %copy-done.56, bf16[256,384]{1,0:T(8,128)(2,1)S(1)} %copy-done.53, bf16[256,384]{1,0:T(8,128)(2,1)S(1)} %copy-done.50, bf16[256,384]{1,0:T(8,128)(2,1)S(1)} %get-tuple-element.173, pred[]{:T(512)S(6)} %eq.13), kind=kLoop, calls=%fused_computation.93 | loop fusion | flops 16515072 | bytes 3145729 | tf_op jit(solution)/shard_map/jit(_where)/select_n | solution.py:43
  171.7 8.2 pad_maximum_fusion
  179.9 23.2 %collective-permute-done.15 = bf16[384,960]{0,1:T(8,128)(2,1)} collective-permute-done((bf16[384,960]{0,1:T(8,128)(2,1)}, bf16[384,960]{0,1:T(8,128)(2,1)}, u32[]{:S(2)}, u32[]{:S(2)}) %collective-permute-start.15) | collective-permute-done | bytes 737312 | tf_op jit(solution)/shard_map/ppermute | solution.py:27
  227.5 6.2 fusion.17
  250.6 21.8 %collective-permute-done.22 = bf16[384,960]{0,1:T(8,128)(2,1)S(1)} collective-permute-done((bf16[384,960]{0,1:T(8,128)(2,1)}, bf16[384,960]{0,1:T(8,128)(2,1)S(1)}, u32[]{:S(2)}, u32[]{:S(2)}) %collective-permute-start.22) | collective-permute-done | bytes 737312 | tf_op jit(solution)/shard_map/ppermute | solution.py:27
  298.5 5.9 add_add_fusion.2
  315.6 26.7 %collective-permute-done.57 = f32[16]{0:T(128)S(1)} collective-permute-done((f32[16]{0:T(128)S(1)}, f32[16]{0:T(128)S(1)}, u32[]{:S(2)}, u32[]{:S(2)}) %collective-permute-start.57) | collective-permute-done | bytes 96 | tf_op jit(solution)/shard_map/ppermute | solution.py:27
  364.1 30.3 %collective-permute-done.37 = bf16[384,1536]{1,0:T(8,128)(2,1)S(1)} collective-permute-done((bf16[384,1536]{1,0:T(8,128)(2,1)}, bf16[384,1536]{1,0:T(8,128)(2,1)S(1)}, u32[]{:S(2)}, u32[]{:S(2)}) %collective-permute-start.37) | collective-permute-done | bytes 1179680 | tf_op jit(solution)/shard_map/ppermute | solution.py:27
  400.1 19.6 %collective-permute-done.33 = bf16[384,1536]{1,0:T(8,128)(2,1)S(1)} collective-permute-done((bf16[384,1536]{1,0:T(8,128)(2,1)}, bf16[384,1536]{1,0:T(8,128)(2,1)S(1)}, u32[]{:S(2)}, u32[]{:S(2)}) %collective-permute-start.33) | collective-permute-done | bytes 1179680 | tf_op jit(solution)/shard_map/ppermute | solution.py:27
  472.8 7.3 add_add_fusion.1
  492.8 29.3 %collective-permute-done.81 = bf16[768,1536]{1,0:T(8,128)(2,1)} collective-permute-done((bf16[768,1536]{1,0:T(8,128)(2,1)}, bf16[768,1536]{1,0:T(8,128)(2,1)}, u32[]{:S(2)}, u32[]{:S(2)}) %collective-permute-start.81) | collective-permute-done | bytes 2359328 | tf_op jit(solution)/shard_map/ppermute | solution.py:27
  534.3 5.3 collective-permute-done.83
  565.1 10.7 %collective-permute-done.49 = bf16[256,1024]{1,0:T(8,128)(2,1)S(1)} collective-permute-done((bf16[256,1024]{1,0:T(8,128)(2,1)S(1)}, bf16[256,1024]{1,0:T(8,128)(2,1)S(1)}, u32[]{:S(2)}, u32[]{:S(2)}) %collective-permute-start.49) | collective-permute-done | bytes 524320 | tf_op jit(solution)/shard_map/ppermute | solution.py:27
  588.6 5.3 copy.189
  619.8 5.2 shard_map.257
  627.5 6.8 fusion.174
  639.3 5.2 shard_map.258
  674.5 7.7 multiply_convert_fusion.4
  685.9 11.1 %add_add_fusion = f32[1024,1536]{1,0:T(8,128)S(1)} fusion(f32[1024,1536]{1,0:T(8,128)} %fusion.191, f32[1024,1536]{1,0:T(8,128)} %fusion.11, f32[1024,1536]{1,0:T(8,128)} %fusion.38, f32[1024,1536]{1,0:T(8,128)S(1)} %bitcast.177, bf16[1024,768]{1,0:T(8,128)(2,1)} %copy-done.69, bf16[1536,1344]{1,0:T(8,128)(2,1)} %pad_maximum_fusion), kind=kOutput, calls=%fused_computation | convolution fusion | flops 2422210560 | bytes 35389440 | tf_op jit(solution)/shard_map/dot_general | solution.py:23
  719.5 10.7 %collective-permute-done.77 = bf16[768,768]{1,0:T(8,128)(2,1)} collective-permute-done((bf16[768,768]{1,0:T(8,128)(2,1)}, bf16[768,768]{1,0:T(8,128)(2,1)}, u32[]{:S(2)}, u32[]{:S(2)}) %collective-permute-start.77) | collective-permute-done | bytes 1179680 | tf_op jit(solution)/shard_map/ppermute | solution.py:27
  733.2 15.3 %collective-permute-done.75 = bf16[768,768]{1,0:T(8,128)(2,1)S(1)} collective-permute-done((bf16[768,768]{1,0:T(8,128)(2,1)}, bf16[768,768]{1,0:T(8,128)(2,1)S(1)}, u32[]{:S(2)}, u32[]{:S(2)}) %collective-permute-start.75) | collective-permute-done | bytes 1179680 | tf_op jit(solution)/shard_map/ppermute | solution.py:27
  751.6 6.3 collective-permute-done.66
  777.2 10.3 %collective-permute-done.67 = bf16[384,576]{0,1:T(8,128)(2,1)} collective-permute-done((bf16[384,576]{0,1:T(8,128)(2,1)}, bf16[384,576]{0,1:T(8,128)(2,1)}, u32[]{:S(2)}, u32[]{:S(2)}) %collective-permute-start.67) | collective-permute-done | bytes 442400 | tf_op jit(solution)/shard_map/ppermute | solution.py:27
  803.9 36.5 %collective-permute-done.79 = bf16[384,768]{1,0:T(8,128)(2,1)} collective-permute-done((bf16[384,768]{1,0:T(8,128)(2,1)}, bf16[384,768]{1,0:T(8,128)(2,1)}, u32[]{:S(2)}, u32[]{:S(2)}) %collective-permute-start.79) | collective-permute-done | bytes 589856 | tf_op jit(solution)/shard_map/ppermute | solution.py:27
  844.6 12.8 %collective-permute-done.58 = f32[5,1536]{1,0:T(8,128)S(1)} collective-permute-done((f32[5,1536]{1,0:T(8,128)S(1)}, f32[5,1536]{1,0:T(8,128)S(1)}, u32[]{:S(2)}, u32[]{:S(2)}) %collective-permute-start.58) | collective-permute-done | bytes 30752 | tf_op jit(solution)/shard_map/ppermute | solution.py:27
  877.9 5.8 collective-permute-start.74
  885.0 6.1 collective-permute-done.55
  (707 shorter events, 462.1 us)
Async XLA Ops:
  14.0 48.8 %collective-permute-start.31 = (bf16[192,1536]{1,0:T(8,128)(2,1)}, bf16[192,1536]{1,0:T(8,128)(2,1)}, u32[]{:S(2)}, u32[]{:S(2)}) collective-permute-start(bf16[192,1536]{1,0:T(8,128)(2,1)} %get-tuple-element.162), channel_id=1, source_target_pairs={{0,4},{4,0},{1,5},{5,1},{2,6},{6,2},{3,7},{7,3},{8,12},{12,8},{9,1... | collective-permute-start | bytes 1769480 | tf_op jit(solution)/shard_map/ppermute | solution.py:27
  17.6 49.0 %collective-permute-start = (bf16[256,1536]{1,0:T(8,128)(2,1)}, bf16[256,1536]{1,0:T(8,128)(2,1)}, u32[]{:S(2)}, u32[]{:S(2)}) collective-permute-start(bf16[256,1536]{1,0:T(8,128)(2,1)} %param.15), channel_id=1, source_target_pairs={{0,0},{2,4},{4,2},{6,6},{1,1},{3,5},{5,3},{7,7},{8,8},{10,12},{12,... | collective-permute-start | bytes 2359304 | tf_op jit(solution)/shard_map/ppermute | solution.py:31
  49.8 51.1 %collective-permute-start.42 = (bf16[256,1536]{1,0:T(8,128)(2,1)}, bf16[256,1536]{1,0:T(8,128)(2,1)}, u32[]{:S(2)}, u32[]{:S(2)}) collective-permute-start(bf16[256,1536]{1,0:T(8,128)(2,1)} %param.16), channel_id=1, source_target_pairs={{0,0},{2,4},{4,2},{6,6},{1,1},{3,5},{5,3},{7,7},{8,8},{10,12},{12,... | collective-permute-start | bytes 2359304 | tf_op jit(solution)/shard_map/ppermute | solution.py:31
  58.4 50.1 %collective-permute-start.16 = (bf16[384,1344]{0,1:T(8,128)(2,1)}, bf16[384,1344]{0,1:T(8,128)(2,1)}, u32[]{:S(2)}, u32[]{:S(2)}) collective-permute-start(bf16[384,1344]{0,1:T(8,128)(2,1)} %copy.176), channel_id=1, source_target_pairs={{0,2},{2,0},{1,3},{3,1},{4,6},{6,4},{5,7},{7,5},{8,10},{10,8},{9,1... | collective-permute-start | bytes 3096584 | tf_op jit(solution)/shard_map/ppermute | solution.py:27
  62.6 49.5 %collective-permute-start.11 = (bf16[384,1344]{0,1:T(8,128)(2,1)}, bf16[384,1344]{0,1:T(8,128)(2,1)}, u32[]{:S(2)}, u32[]{:S(2)}) collective-permute-start(bf16[384,1344]{0,1:T(8,128)(2,1)} %copy.176), channel_id=1, source_target_pairs={{0,16},{16,0},{1,17},{17,1},{2,18},{18,2},{3,19},{19,3},{4,20},{20... | collective-permute-start | bytes 3096584 | tf_op jit(solution)/shard_map/ppermute | solution.py:27
  68.3 48.3 %collective-permute-start.1 = (bf16[256,1536]{1,0:T(8,128)(2,1)S(1)}, bf16[256,1536]{1,0:T(8,128)(2,1)}, u32[]{:S(2)}, u32[]{:S(2)}) collective-permute-start(bf16[256,1536]{1,0:T(8,128)(2,1)S(1)} %get-tuple-element.140), channel_id=1, source_target_pairs={{0,1},{1,0},{2,3},{3,2},{4,5},{5,4},{6,7},{7,6},{8,9},{9,8},{10,11... | collective-permute-start | bytes 2359304 | tf_op jit(solution)/shard_map/ppermute | solution.py:27
  103.3 45.3 %collective-permute-start.43 = (bf16[256,1536]{1,0:T(8,128)(2,1)}, bf16[256,1536]{1,0:T(8,128)(2,1)}, u32[]{:S(2)}, u32[]{:S(2)}) collective-permute-start(bf16[256,1536]{1,0:T(8,128)(2,1)} %pad_maximum_fusion.9), channel_id=1, source_target_pairs={{0,1},{1,0},{2,3},{3,2},{4,5},{5,4},{6,7},{7,6},{8,9},{9,8},{10,11... | collective-permute-start | bytes 2359304 | tf_op jit(solution)/shard_map/ppermute | solution.py:27
  103.9 58.1 %collective-permute-start.14 = (bf16[384,960]{0,1:T(8,128)(2,1)}, bf16[384,960]{0,1:T(8,128)(2,1)}, u32[]{:S(2)}, u32[]{:S(2)}) collective-permute-start(bf16[384,960]{0,1:T(8,128)(2,1)} %maximum_select_fusion.18), channel_id=1, source_target_pairs={{0,16},{16,0},{1,17},{17,1},{2,18},{18,2},{3,19},{19,3},{4,20},{20... | collective-permute-start | bytes 2211848 | tf_op jit(solution)/shard_map/ppermute | solution.py:27
  108.5 54.9 %collective-permute-start.13 = (bf16[384,960]{0,1:T(8,128)(2,1)}, bf16[384,960]{0,1:T(8,128)(2,1)}, u32[]{:S(2)}, u32[]{:S(2)}) collective-permute-start(bf16[384,960]{0,1:T(8,128)(2,1)} %maximum_select_fusion.18), channel_id=1, source_target_pairs={{0,8},{8,0},{1,9},{9,1},{2,10},{10,2},{3,11},{11,3},{4,12},{12,4},... | collective-permute-start | bytes 2211848 | tf_op jit(solution)/shard_map/ppermute | solution.py:27
  112.1 49.9 %collective-permute-start.20 = (bf16[384,960]{0,1:T(8,128)(2,1)}, bf16[384,960]{0,1:T(8,128)(2,1)}, u32[]{:S(2)}, u32[]{:S(2)}) collective-permute-start(bf16[384,960]{0,1:T(8,128)(2,1)} %maximum_select_fusion.18), channel_id=1, source_target_pairs={{0,2},{2,0},{1,3},{3,1},{4,6},{6,4},{5,7},{7,5},{8,10},{10,8},{9,1... | collective-permute-start | bytes 2211848 | tf_op jit(solution)/shard_map/ppermute | solution.py:27
  116.6 51.5 %collective-permute-start.10 = (bf16[384,1344]{0,1:T(8,128)(2,1)}, bf16[384,1344]{0,1:T(8,128)(2,1)}, u32[]{:S(2)}, u32[]{:S(2)}) collective-permute-start(bf16[384,1344]{0,1:T(8,128)(2,1)} %collective-permute-done.9), channel_id=1, source_target_pairs={{0,16},{16,0},{1,17},{17,1},{2,18},{18,2},{3,19},{19,3},{4,20},{20... | collective-permute-start | bytes 3096584 | tf_op jit(solution)/shard_map/ppermute | solution.py:27
  148.6 58.7 %collective-permute-start.2 = (bf16[512,1536]{1,0:T(8,128)(2,1)S(1)}, bf16[512,1536]{1,0:T(8,128)(2,1)}, u32[]{:S(2)}, u32[]{:S(2)}) collective-permute-start(bf16[512,1536]{1,0:T(8,128)(2,1)S(1)} %maximum_select_fusion.5), channel_id=1, source_target_pairs={{0,4},{4,0},{1,5},{5,1},{2,6},{6,2},{3,7},{7,3},{8,12},{12,8},{9,1... | collective-permute-start | bytes 4718600 | tf_op jit(solution)/shard_map/ppermute | solution.py:27
  162.0 76.0 %collective-permute-start.44 = (bf16[512,1536]{1,0:T(8,128)(2,1)}, bf16[512,1536]{1,0:T(8,128)(2,1)}, u32[]{:S(2)}, u32[]{:S(2)}) collective-permute-start(bf16[512,1536]{1,0:T(8,128)(2,1)} %maximum_select_fusion.7), channel_id=1, source_target_pairs={{0,4},{4,0},{1,5},{5,1},{2,6},{6,2},{3,7},{7,3},{8,12},{12,8},{9,1... | collective-permute-start | bytes 4718600 | tf_op jit(solution)/shard_map/ppermute | solution.py:27
  162.0 111.1 %collective-permute-start.19 = (bf16[384,1344]{0,1:T(8,128)(2,1)}, bf16[384,1344]{0,1:T(8,128)(2,1)}, u32[]{:S(2)}, u32[]{:S(2)}) collective-permute-start(bf16[384,1344]{0,1:T(8,128)(2,1)} %collective-permute-done.16), channel_id=1, source_target_pairs={{0,16},{16,0},{1,17},{17,1},{2,18},{18,2},{3,19},{19,3},{4,20},{20... | collective-permute-start | bytes 3096584 | tf_op jit(solution)/shard_map/ppermute | solution.py:27
  163.4 70.3 %collective-permute-start.17 = (bf16[384,1344]{0,1:T(8,128)(2,1)}, bf16[384,1344]{0,1:T(8,128)(2,1)}, u32[]{:S(2)}, u32[]{:S(2)}) collective-permute-start(bf16[384,1344]{0,1:T(8,128)(2,1)} %collective-permute-done.16), channel_id=1, source_target_pairs={{0,8},{8,0},{1,9},{9,1},{2,10},{10,2},{3,11},{11,3},{4,12},{12,4},... | collective-permute-start | bytes 3096584 | tf_op jit(solution)/shard_map/ppermute | solution.py:27
  203.1 148.0 %collective-permute-start.35 = (bf16[384,1536]{1,0:T(8,128)(2,1)}, bf16[384,1536]{1,0:T(8,128)(2,1)}, u32[]{:S(2)}, u32[]{:S(2)}) collective-permute-start(bf16[384,1536]{1,0:T(8,128)(2,1)} %maximum_select_fusion.9), channel_id=1, source_target_pairs={{0,2},{2,0},{1,3},{3,1},{4,6},{6,4},{5,7},{7,5},{8,10},{10,8},{9,1... | collective-permute-start | bytes 3538952 | tf_op jit(solution)/shard_map/ppermute | solution.py:27
  305.3 45.8 %collective-permute-start.32 = (bf16[384,1536]{1,0:T(8,128)(2,1)}, bf16[384,1536]{1,0:T(8,128)(2,1)}, u32[]{:S(2)}, u32[]{:S(2)}) collective-permute-start(bf16[384,1536]{1,0:T(8,128)(2,1)} %maximum_select_fusion.9), channel_id=1, source_target_pairs={{0,8},{8,0},{1,9},{9,1},{2,10},{10,2},{3,11},{11,3},{4,12},{12,4},... | collective-permute-start | bytes 3538952 | tf_op jit(solution)/shard_map/ppermute | solution.py:27
  342.3 77.5 %collective-permute-start.34 = (bf16[384,1536]{1,0:T(8,128)(2,1)}, bf16[384,1536]{1,0:T(8,128)(2,1)}, u32[]{:S(2)}, u32[]{:S(2)}) collective-permute-start(bf16[384,1536]{1,0:T(8,128)(2,1)} %maximum_select_fusion.9), channel_id=1, source_target_pairs={{0,16},{16,0},{1,17},{17,1},{2,18},{18,2},{3,19},{19,3},{4,20},{20... | collective-permute-start | bytes 3538952 | tf_op jit(solution)/shard_map/ppermute | solution.py:27
  352.5 47.5 %collective-permute-start.36 = (bf16[384,1536]{1,0:T(8,128)(2,1)}, bf16[384,1536]{1,0:T(8,128)(2,1)S(1)}, u32[]{:S(2)}, u32[]{:S(2)}) collective-permute-start(bf16[384,1536]{1,0:T(8,128)(2,1)} %collective-permute-done.35), channel_id=1, source_target_pairs={{0,8},{8,0},{1,9},{9,1},{2,10},{10,2},{3,11},{11,3},{4,12},{12,4},... | collective-permute-start | bytes 3538952 | tf_op jit(solution)/shard_map/ppermute | solution.py:27
  359.3 60.4 %collective-permute-start.33 = (bf16[384,1536]{1,0:T(8,128)(2,1)}, bf16[384,1536]{1,0:T(8,128)(2,1)S(1)}, u32[]{:S(2)}, u32[]{:S(2)}) collective-permute-start(bf16[384,1536]{1,0:T(8,128)(2,1)} %collective-permute-done.32), channel_id=1, source_target_pairs={{0,16},{16,0},{1,17},{17,1},{2,18},{18,2},{3,19},{19,3},{4,20},{20... | collective-permute-start | bytes 3538952 | tf_op jit(solution)/shard_map/ppermute | solution.py:27
  470.7 51.4 %collective-permute-start.81 = (bf16[768,1536]{1,0:T(8,128)(2,1)}, bf16[768,1536]{1,0:T(8,128)(2,1)}, u32[]{:S(2)}, u32[]{:S(2)}) collective-permute-start(bf16[768,1536]{1,0:T(8,128)(2,1)} %pad_maximum_fusion.1), channel_id=1, source_target_pairs={{0,8},{8,0},{1,9},{9,1},{2,10},{10,2},{3,11},{11,3},{4,12},{12,4},... | collective-permute-start | bytes 7077896 | tf_op jit(solution)/shard_map/ppermute | solution.py:27
  488.0 51.6 %collective-permute-start.83 = (bf16[768,1536]{1,0:T(8,128)(2,1)}, bf16[768,1536]{1,0:T(8,128)(2,1)S(1)}, u32[]{:S(2)}, u32[]{:S(2)}) collective-permute-start(bf16[768,1536]{1,0:T(8,128)(2,1)} %pad_maximum_fusion.2), channel_id=1, source_target_pairs={{0,16},{16,0},{1,17},{17,1},{2,18},{18,2},{3,19},{19,3},{4,20},{20... | collective-permute-start | bytes 7077896 | tf_op jit(solution)/shard_map/ppermute | solution.py:27
  525.1 137.6 %collective-permute-start.82 = (bf16[384,1536]{1,0:T(8,128)(2,1)}, bf16[384,1536]{1,0:T(8,128)(2,1)}, u32[]{:S(2)}, u32[]{:S(2)}) collective-permute-start(bf16[384,1536]{1,0:T(8,128)(2,1)} %add_convert_fusion.2), channel_id=1, source_target_pairs={{0,16},{16,0},{1,17},{17,1},{2,18},{18,2},{3,19},{19,3},{4,20},{20... | collective-permute-start | bytes 3538952 | tf_op jit(solution)/shard_map/ppermute | solution.py:27
  528.7 49.9 %collective-permute-start.47 = (bf16[256,1536]{1,0:T(8,128)(2,1)}, bf16[256,1536]{1,0:T(8,128)(2,1)}, u32[]{:S(2)}, u32[]{:S(2)}) collective-permute-start(bf16[256,1536]{1,0:T(8,128)(2,1)} %get-tuple-element.137), channel_id=1, source_target_pairs={{0,1},{1,0},{2,3},{3,2},{4,5},{5,4},{6,7},{7,6},{8,9},{9,8},{10,11... | collective-permute-start | bytes 2359304 | tf_op jit(solution)/shard_map/ppermute | solution.py:27
  585.3 77.4 %collective-permute-start.85 = (bf16[384,1536]{1,0:T(8,128)(2,1)}, bf16[384,1536]{1,0:T(8,128)(2,1)}, u32[]{:S(2)}, u32[]{:S(2)}) collective-permute-start(bf16[384,1536]{1,0:T(8,128)(2,1)} %add_convert_fusion), channel_id=1, source_target_pairs={{0,2},{2,0},{1,3},{3,1},{4,6},{6,4},{5,7},{7,5},{8,10},{10,8},{9,1... | collective-permute-start | bytes 3538952 | tf_op jit(solution)/shard_map/ppermute | solution.py:27
  670.3 44.9 %collective-permute-start.63 = (bf16[768,576]{0,1:T(8,128)(2,1)}, bf16[768,576]{0,1:T(8,128)(2,1)}, u32[]{:S(2)}, u32[]{:S(2)}) collective-permute-start(bf16[768,576]{0,1:T(8,128)(2,1)} %convolution_convert_fusion.6), channel_id=1, source_target_pairs={{0,8},{8,0},{1,9},{9,1},{2,10},{10,2},{3,11},{11,3},{4,12},{12,4},... | collective-permute-start | bytes 2654216 | tf_op jit(solution)/shard_map/ppermute | solution.py:27
  673.3 87.5 %collective-permute-start.69 = (bf16[768,960]{0,1:T(8,128)(2,1)}, bf16[768,960]{0,1:T(8,128)(2,1)}, u32[]{:S(2)}, u32[]{:S(2)}) collective-permute-start(bf16[768,960]{0,1:T(8,128)(2,1)} %pad_maximum_fusion.4), channel_id=1, source_target_pairs={{0,8},{8,0},{1,9},{9,1},{2,10},{10,2},{3,11},{11,3},{4,12},{12,4},... | collective-permute-start | bytes 4423688 | tf_op jit(solution)/shard_map/ppermute | solution.py:27
  713.2 53.5 %collective-permute-start.71 = (bf16[768,960]{0,1:T(8,128)(2,1)}, bf16[768,960]{0,1:T(8,128)(2,1)}, u32[]{:S(2)}, u32[]{:S(2)}) collective-permute-start(bf16[768,960]{0,1:T(8,128)(2,1)} %pad_maximum_fusion.5), channel_id=1, source_target_pairs={{0,16},{16,0},{1,17},{17,1},{2,18},{18,2},{3,19},{19,3},{4,20},{20... | collective-permute-start | bytes 4423688 | tf_op jit(solution)/shard_map/ppermute | solution.py:27
  715.2 57.5 %collective-permute-start.51 = (bf16[512,1536]{1,0:T(8,128)(2,1)}, bf16[512,1536]{1,0:T(8,128)(2,1)}, u32[]{:S(2)}, u32[]{:S(2)}) collective-permute-start(bf16[512,1536]{1,0:T(8,128)(2,1)} %dynamic-slice_convert_fusion), channel_id=1, source_target_pairs={{0,4},{4,0},{1,5},{5,1},{2,6},{6,2},{3,7},{7,3},{8,12},{12,8},{9,1... | collective-permute-start | bytes 4718600 | tf_op jit(solution)/shard_map/ppermute | solution.py:27
  787.6 56.0 %collective-permute-start.52 = (bf16[256,1536]{1,0:T(8,128)(2,1)S(1)}, bf16[256,1536]{1,0:T(8,128)(2,1)S(1)}, u32[]{:S(2)}, u32[]{:S(2)}) collective-permute-start(bf16[256,1536]{1,0:T(8,128)(2,1)S(1)} %dynamic-slice_convert_fusion.5), channel_id=1, source_target_pairs={{0,1},{1,0},{2,3},{3,2},{4,5},{5,4},{6,7},{7,6},{8,9},{9,8},{10,11... | collective-permute-start | bytes 2359304 | tf_op jit(solution)/shard_map/ppermute | solution.py:27
  795.5 44.9 %collective-permute-start.79 = (bf16[384,768]{1,0:T(8,128)(2,1)}, bf16[384,768]{1,0:T(8,128)(2,1)}, u32[]{:S(2)}, u32[]{:S(2)}) collective-permute-start(bf16[384,768]{1,0:T(8,128)(2,1)} %fusion.93), channel_id=1, source_target_pairs={{0,2},{2,0},{1,3},{3,1},{4,6},{6,4},{5,7},{7,5},{8,10},{10,8},{9,1... | collective-permute-start | bytes 1769480 | tf_op jit(solution)/shard_map/ppermute | solution.py:27
  802.5 72.4 %collective-permute-start.73 = (bf16[384,960]{0,1:T(8,128)(2,1)}, bf16[384,960]{0,1:T(8,128)(2,1)}, u32[]{:S(2)}, u32[]{:S(2)}) collective-permute-start(bf16[384,960]{0,1:T(8,128)(2,1)} %add_convert_fusion.6), channel_id=1, source_target_pairs={{0,2},{2,0},{1,3},{3,1},{4,6},{6,4},{5,7},{7,5},{8,10},{10,8},{9,1... | collective-permute-start | bytes 2211848 | tf_op jit(solution)/shard_map/ppermute | solution.py:27
  (186 other events, 3774.1 us)

commit v2 on v1

--- a/solution.py
+++ b/solution.py
@@ -4,6 +4,7 @@
 import jax.numpy as jnp
 from jax import lax
 from jax.experimental import pallas as pl
+from jax.experimental.layout import Layout, with_layout_constraint
 from jax.experimental.pallas import tpu as pltpu
 from jax.sharding import Mesh
 from jax.sharding import PartitionSpec as P
@@ -32,15 +33,21 @@
 
 
 def after(x, *others):
-    return lax.optimization_barrier((x,) + others)[0]
+    if isinstance(x, (list, tuple)):
+        return list(lax.optimization_barrier((*x, *others))[: len(x)])
+    return lax.optimization_barrier((x, *others))[0]
 
 
 def cat(parts, axis=0):
     return jnp.concatenate(parts, axis=axis)
 
 
+def by_rows(x):
+    return with_layout_constraint(x, Layout(major_to_minor=tuple(range(x.ndim))))
+
+
 def by_index(index, first, second, axis=0):
-    return jnp.where(index == 0, cat([first, second], axis), cat([second, first], axis))
+    return cat([jnp.where(index == 0, first, second), jnp.where(index == 0, second, first)], axis)
 
 
 def gather_rows(x):
@@ -49,14 +56,22 @@
     return by_index(c, half, swap(half, "c"))
 
 
-def scatter_rows(x):
-    c, l = lax.axis_index("c"), lax.axis_index("l")
-    rows = x.shape[0] // 2
-    send = lax.dynamic_slice_in_dim(x, (1 - c) * rows, rows, 0).astype(BF16)
-    half = lax.dynamic_slice_in_dim(x, c * rows, rows, 0).astype(F32) + swap(send, "c").astype(F32)
-    rows = rows // 2
-    send = lax.dynamic_slice_in_dim(half, (1 - l) * rows, rows, 0).astype(BF16)
-    return lax.dynamic_slice_in_dim(half, l * rows, rows, 0) + swap(send, "l").astype(F32)
+class RowSum:
+    def __init__(self, x):
+        c = lax.axis_index("c")
+        rows = x.shape[0] // 2
+        self.sent = lax.dynamic_slice_in_dim(x, (1 - c) * rows, rows, 0).astype(BF16)
+        self.kept = lax.dynamic_slice_in_dim(x, c * rows, rows, 0)
+
+    def cores(self):
+        l = lax.axis_index("l")
+        half = self.kept.astype(F32) + swap(self.sent, "c").astype(F32)
+        rows = half.shape[0] // 2
+        self.sent = lax.dynamic_slice_in_dim(half, (1 - l) * rows, rows, 0).astype(BF16)
+        self.kept = lax.dynamic_slice_in_dim(half, l * rows, rows, 0)
+
+    def chips(self):
+        return self.kept + swap(self.sent, "l").astype(F32)
 
 
 def shuffle(plane, v, back=False):
@@ -74,62 +89,111 @@
     return cat(b, -1)
 
 
-def gather_plane(plane, piece, first):
-    if len(plane) == 1:
-        whole = lax.all_gather(piece, plane, axis=0, tiled=True)
-        return whole, piece
-    near = {axis: swap(piece, axis) for axis in plane}
-    second = "y" if first == "x" else "x"
-    far = swap(near[first], second)
-    return cat([piece, near["x"], far, near["y"]]), near[first]
-
-
-def scatter_plane(plane, pairs, first, wait):
-    def product(start, stop):
-        parts = [dot(left[:, start:stop], right, 0, 0).astype(BF16) for left, right in pairs]
+class PlaneGather:
+    def __init__(self, plane, piece, first):
+        if len(plane) == 1:
+            self.parts = [lax.all_gather(piece, plane, axis=0, tiled=True)]
+            self.near, self.far = self.parts, self.parts[0]
+            return
+        near = {axis: swap(piece, axis) for axis in plane}
+        second = "y" if first == "x" else "x"
+        self.far = swap(near[first], second)
+        self.near = [near["x"], near["y"]]
+        self.parts = [piece, near["x"], self.far, near["y"]]
+
+    def whole(self):
+        return by_rows(cat(self.parts) if len(self.parts) > 1 else self.parts[0])
+
+
+class PlaneSum:
+    def __init__(self, plane, pairs, first):
+        self.plane, self.pairs, self.first = plane, pairs, first
+        width = pairs[0][0].shape[1]
+        self.w = w = width // 4
+        if len(plane) == 1:
+            self.sent = self.product(0, width)
+        elif first == "x":
+            self.sent = self.product(w, 3 * w)
+        else:
+            self.sent = self.product(2 * w, 4 * w)
+
+    def product(self, start, stop):
+        parts = [dot(left[:, start:stop], right, 0, 0).astype(BF16) for left, right in self.pairs]
         return cat(parts, 1) if len(parts) > 1 else parts[0]
 
-    width = pairs[0][0].shape[1]
-    if len(plane) == 1:
-        whole = product(0, width)
-        return lax.psum_scatter(whole, plane, scatter_dimension=0, tiled=True).astype(F32)
-    w = width // 4
-    if first == "x":
-        got = swap(wait(product(w, 3 * w)), "x")
-        second, mine, other, other_at = "y", got[:w], got[w:], 3
-    else:
-        got = swap(wait(product(2 * w, 4 * w)), "y")
-        second, mine, other, other_at = "x", got[w:], got[:w], 1
-    other = product(other_at * w, (other_at + 1) * w).astype(F32) + other.astype(F32)
-    other = swap(other.astype(BF16), second)
-    mine = product(0, w).astype(F32) + mine.astype(F32)
-    return mine + other.astype(F32)
-
-
-def reduce_group(plane, sources, wait=lambda v: v):
-    here = scatter_plane(plane, [(left, right) for left, right, _ in sources], "x", wait)
-    there = scatter_plane(plane, [(left, right) for left, _, right in sources], "y", wait)
-    mine = here + swap(there.astype(BF16), "h").astype(F32)
+    def second(self, ties=()):
+        if len(self.plane) == 1:
+            self.total = lax.psum_scatter(self.sent, self.plane, scatter_dimension=0, tiled=True).astype(F32)
+            self.sent = self.got = self.total
+            return
+        w = self.w
+        self.got = got = after(swap(self.sent, self.first), *ties)
+        if self.first == "x":
+            self.axis, mine, other, other_at = "y", got[:w], got[w:], 3
+        else:
+            self.axis, mine, other, other_at = "x", got[w:], got[:w], 1
+        other = self.product(other_at * w, (other_at + 1) * w).astype(F32) + other.astype(F32)
+        self.sent = other.astype(BF16)
+        self.total = self.product(0, w).astype(F32) + mine.astype(F32)
+
+    def last(self):
+        if len(self.plane) > 1:
+            self.total = self.total + swap(self.sent, self.axis).astype(F32)
+
+
+class GroupSum:
+    def __init__(self, plane, sources):
+        self.columns = [right.shape[1] for _, right, _ in sources]
+        self.here = PlaneSum(plane, [(left, right) for left, right, _ in sources], "x")
+        self.there = PlaneSum(plane, [(left, right) for left, _, right in sources], "y")
+        self.sent = [self.here.sent, self.there.sent]
+
+    def second(self, ties=()):
+        self.here.second(ties)
+        self.there.second(ties)
+        self.sent = [self.here.sent, self.there.sent]
+
+    def line(self):
+        self.there.last()
+        self.sent = [self.there.total.astype(BF16)]
+        self.here.last()
+        self.sent.append(self.here.total)
+
+    def cores(self, ties=()):
+        got = swap(self.sent[0], "h")
+        mine = self.here.total + (after(got, *ties) if ties else got).astype(F32)
+        c = lax.axis_index("c")
+        rows = mine.shape[0] // 2
+        self.given = lax.dynamic_slice_in_dim(mine, (1 - c) * rows, rows, 0).astype(BF16)
+        self.kept = lax.dynamic_slice_in_dim(mine, c * rows, rows, 0)
+
+    def results(self):
+        c = lax.axis_index("c")
+        got = swap(self.given, "c").astype(F32)
+        results, start = [], 0
+        for n in self.columns:
+            results.append(by_index(c, self.kept[:, start : start + n], got[:, start : start + n], 1))
+            start += n
+        return results
+
+
+def pack(groups, common=()):
     c = lax.axis_index("c")
-    rows = mine.shape[0] // 2
-    given = lax.dynamic_slice_in_dim(mine, (1 - c) * rows, rows, 0).astype(BF16)
-    kept = lax.dynamic_slice_in_dim(mine, c * rows, rows, 0)
-    got = swap(given, "c").astype(F32)
-    results, start = [], 0
-    for _, right, _ in sources:
-        n = right.shape[1]
-        results.append(by_index(c, kept[:, start : start + n], got[:, start : start + n], 1))
-        start += n
+    mine, other, results, start = [], [], [], 0
+    for shards in groups:
+        columns = sum(s.shape[1] // 2 for s in shards) + sum(s.shape[1] for s in common)
+        filled = list(common)
+        if columns % 128:
+            filled.append(jnp.zeros((shards[0].shape[0], 128 - columns % 128), BF16))
+        low = cat([s[:, : s.shape[1] // 2] for s in shards] + filled, 1)
+        high = cat([s[:, s.shape[1] // 2 :] for s in shards] + filled, 1)
+        mine.append(jnp.where(c == 0, low, high))
+        other.append(jnp.where(c == 0, high, low))
+    got = swap(cat(other, 1), "c")
+    for block in mine:
+        results.append(by_rows(by_index(c, block, got[:, start : start + block.shape[1]])))
+        start += block.shape[1]
     return results
-
-
-def pack(shards):
-    c = lax.axis_index("c")
-    low = cat([s[:, : s.shape[1] // 2] for s in shards], 1)
-    high = cat([s[:, s.shape[1] // 2 :] for s in shards], 1)
-    mine = jnp.where(c == 0, low, high)
-    got = swap(jnp.where(c == 0, high, low), "c")
-    return by_index(c, mine, got)
 
 
 def tall(x):
@@ -158,6 +222,41 @@
             p = (e * (1.0 / total)).astype(BF16)
             ctx_ref[part[0], cols] = dot(v[:, :end], p, 1, 0).astype(BF16)
             lse_ref[head : head + 1, cols] = top + jnp.log(total)
+
+
+def sum_kernel(terms, weights, *refs):
+    weight_refs, left_refs, out_ref = refs[:weights], refs[weights:-1], refs[-1]
+    total = None
+    for (which, start, stop, side), left_ref in zip(terms, left_refs):
+        right = weight_refs[which][:, start:stop]
+        part = dot(left_ref[...], right, side, 1)
+        total = part if total is None else total + part
+    out_ref[...] = total.astype(BF16)
+
+
+def sum_dots(weights, terms):
+    left, side = terms[0][0], terms[0][4]
+    rows, width = left.shape[1 - side], weights[0].shape[0]
+    tile, wide = min(512, rows), 512
+    in_specs = [pl.BlockSpec((wide, w.shape[1]), lambda n, m: (n, 0)) for w in weights]
+    for left, _, _, _, side in terms:
+        if side == 1:
+            in_specs.append(pl.BlockSpec((tile, left.shape[1]), lambda n, m: (m, 0)))
+        else:
+            in_specs.append(pl.BlockSpec((left.shape[0], tile), lambda n, m: (0, m)))
+    return pl.pallas_call(
+        functools.partial(sum_kernel, [t[1:] for t in terms], len(weights)),
+        grid=(width // wide, rows // tile),
+        in_specs=in_specs,
+        out_specs=pl.BlockSpec((tile, wide), lambda n, m: (m, n)),
+        out_shape=jax.ShapeDtypeStruct((rows, width), BF16),
+        compiler_params=pltpu.CompilerParams(vmem_limit_bytes=VMEM_LIMIT),
+        cost_estimate=pl.CostEstimate(
+            flops=2 * rows * width * sum(t[3] - t[2] for t in terms),
+            bytes_accessed=2 * sum(w.size for w in weights) + 8 * sum(t[0].size for t in terms),
+            transcendentals=0,
+        ),
+    )(*weights, *[t[0] for t in terms])
 
 
 def fill_bias(code_ref, doc_ref, bias_ref):
@@ -344,39 +443,41 @@
     hidden_units = 4 * memory_in.shape[1]
     units, q_cols, ff = memory_in.shape[1] // 2, project_in.shape[2] // 2, gate_weight.shape[1] // 2
 
-    x_own = relative(turn(block_in))
+    vectors = cat([v[None] for v in (gain_in, w_forget, w_momentum, gain_mid)], 0)
+    for axis in ("l", "h"):
+        vectors = by_index(lax.axis_index(axis), vectors, swap(vectors, axis), 1)
+    first = [memory_in, project_in[0], project_in[1], project_in[2]]
+    x_turned = turn(block_in)
     flags = turn(cat([resets, counts[:, None]], 1))
-    packed = [
-        pack([memory_in, project_in[0], project_in[1], project_in[2]]),
-        pack([memory_out.T, project_out.T]),
-        pack([gate_weight, up_weight, down_weight.T]),
-    ]
-    far = [swap(packed[0], "h")]
-    far.append(swap(after(packed[1], far[0]), "h"))
-    far.append(swap(after(packed[2], far[1]), "h"))
-    stages = [
-        (packed[0], "x"),
-        (packed[1], "y"),
-        (far[0], "x"),
-        (far[1], "y"),
-        (packed[2], "x"),
-        (far[2], "y"),
-    ]
-    weights, done = [], None
-    for piece, first in stages:
-        whole, done = gather_plane(plane, piece if done is None else after(piece, done), first)
-        weights.append(whole)
+    (share0,) = pack([first], [vectors.T])
+    far0 = swap(after(share0, x_turned), "h")
+    late = after([memory_out.T, project_out.T, gate_weight, up_weight, down_weight.T], share0)
+    share1, share2 = pack([late[:2], late[2:]])
+    x_own = relative(x_turned)
+    half = by_index(l, x_own, swap(x_own, "l"))
+    other_half = swap(half, "c")
+    x_full = by_index(c, half, other_half)
+    stages = [PlaneGather(plane, share0, "x")]
+    share1 = after(share1, *stages[0].near)
+    stages.append(PlaneGather(plane, share1, "y"))
+    far0 = after(far0, *stages[0].near)
+    stages.append(PlaneGather(plane, far0, "x"))
+    far1 = swap(after(share1, far0), "h")
+    far1 = after(far1, *stages[2].near, *stages[1].near)
+    grad_turned = turn(after(grad_out, far1))
+    stages.append(PlaneGather(plane, far1, "y"))
+    far2 = swap(after(share2, far1), "h")
+    share2 = after(share2, *stages[3].near, stages[1].far, stages[2].far, grad_turned)
+    stages.append(PlaneGather(plane, share2, "x"))
+    far2 = after(far2, *stages[4].near, stages[3].far)
+    stages.append(PlaneGather(plane, far2, "y"))
     first_layer, second_layer, feed = (
-        (weights[0], weights[2]),
-        (weights[1], weights[3]),
-        (weights[4], weights[5]),
+        [stages[i].whole(), stages[j].whole()] for i, j in ((0, 2), (1, 3), (4, 5))
     )
     both = range(2)
-
-    x_full = gather_rows(x_own)
-    vectors = cat([v[None] for v in (gain_in, w_forget, w_momentum, gain_mid)], 0).astype(F32)
-    vectors = all_parts(plane, vectors[None])
-    vectors = relative(jnp.swapaxes(vectors, 0, 1).reshape(4, width))
+    q_end = units + 3 * q_cols
+    out_end = units + q_cols
+    vectors = first_layer[0][:, q_end : q_end + 4].T.astype(F32)
     gain_one, gain_two, gates = vectors[0], vectors[3], vectors[1:3]
 
     resets, count = flags[0, :-1], flags[0, -1]
@@ -403,24 +504,33 @@
         sig_pre = jax.nn.sigmoid(pre)
         act.append((pre * sig_pre).astype(BF16))
         slope_pre.append((sig_pre * (1.0 + pre * (1.0 - sig_pre))).astype(BF16))
-        qkv.append(dot(first_layer[i][:, units:], normed, 0, 1).astype(BF16))
-    sim = scatter_rows((dot(act[0], act[0], 1, 1) + dot(act[1], act[1], 1, 1)) / hidden_units)
+        qkv.append(dot(first_layer[i][:, units:q_end], normed, 0, 1).astype(BF16))
+    sim_sum = RowSum((dot(act[0], act[0], 1, 1) + dot(act[1], act[1], 1, 1)) / hidden_units)
+    sim_sum.cores()
+    sim = sim_sum.chips()
+    qkv[1] = after(qkv[1], *stages[4].near)
     for i in both:
         context, logsum = attend(code, doc, qkv[i])
         ctx.append(context)
         lse.append(logsum)
-    out_own = scatter_rows(
-        sum(dot(act[i], second_layer[i][:, :units], 1, 1) for i in both)
-        + sum(dot(ctx[i], second_layer[i][:, units:], 0, 1) for i in both)
-    )
+    act_late = after(act, far2)
+    out_sum = RowSum(
+        sum_dots(
+            second_layer,
+            [(act_late[i], i, 0, units, 1) for i in both] + [(ctx[i], i, units, out_end, 0) for i in both],
+        )
+    )
+    out_sum.cores()
+    out_own = out_sum.chips()
     table_own = lax.dynamic_slice_in_dim(table[:, :spans], member * own_spans, own_spans, 0)
     spread = jnp.repeat(jnp.repeat(table_own, CH, axis=0), CH, axis=1)
+    sim = after(sim, *stages[5].near)
     mixing = (sim * spread * valid[None, :] / CH).astype(BF16)
     middle = x_own + out_own + dot(mixing, normed, 1, 0)
     inverse_two = inverse_of(middle)
     mid = (middle * inverse_two * gain_two).astype(BF16)
     mid_all = gather_rows(mid)
-    grad_own = relative(turn(grad_out))
+    grad_own = relative(grad_turned)
     grad_all = gather_rows(grad_own)
 
     hidden, grad_gate_pre, grad_up_pre = [], [], []
@@ -433,28 +543,77 @@
         hidden.append((swish * up).astype(BF16))
         grad_gate_pre.append((grad_hidden * up * (sigma * (1.0 + gate * (1.0 - sigma)))).astype(BF16))
         grad_up_pre.append((grad_hidden * swish).astype(BF16))
-    grad_mid = scatter_rows(
-        sum(
-            dot(grad_gate_pre[i], feed[i][:, :ff], 1, 1) + dot(grad_up_pre[i], feed[i][:, ff : 2 * ff], 1, 1)
-            for i in both
+    mid_sum = RowSum(
+        sum_dots(
+            feed,
+            [(grad_gate_pre[i], i, 0, ff, 1) for i in both] + [(grad_up_pre[i], i, ff, 2 * ff, 1) for i in both],
         )
     )
-    ffn_own = scatter_rows(sum(dot(hidden[i], feed[i][:, 2 * ff :], 1, 1) for i in both))
-    block_out = turn(absolute((middle + ffn_own).astype(BF16)))
-    grad_gate, grad_up, grad_down = reduce_group(
-        plane, [(mid_all, *grad_gate_pre), (mid_all, *grad_up_pre), (grad_all, *hidden)]
-    )
+    mid_sum.cores()
+    mid_late, grad_late = after([mid_all, grad_all], mid_sum.sent)
+    feed_sum = GroupSum(
+        plane, [(mid_late, *grad_gate_pre), (mid_late, *grad_up_pre), (grad_late, *hidden)]
+    )
+    hidden = after(hidden, mid_sum.sent, *feed_sum.sent)
+    ffn_sum = RowSum(sum_dots(feed, [(hidden[i], i, 2 * ff, 3 * ff, 1) for i in both]))
+    grad_mid = after(mid_sum.chips(), ffn_sum.sent)
 
     back_two, grad_gain_two = norm_back(middle, inverse_two, gain_two, grad_mid)
     grad_middle = grad_own.astype(F32) + back_two
     branch = grad_middle.astype(BF16)
     branch_all = gather_rows(branch)
     scaled = dot(branch, normed, 1, 1) / CH * valid[None, :]
-    grad_sim = gather_rows((scaled * spread).astype(BF16))
+    grad_sim_own = (scaled * spread).astype(BF16)
+    grad_sim = gather_rows(grad_sim_own)
     grad_blocks = jnp.sum((scaled * sim).reshape(own_spans, CH, spans, CH), axis=(1, 3))
     grad_table = lax.dynamic_update_slice_in_dim(
         jnp.zeros((spans, spans), F32), grad_blocks, member * own_spans, 0
     )
+
+    feed_sum.second()
+    branch_all = after(branch_all, *feed_sum.sent)
+    out_grad_sum = GroupSum(plane, [(branch_all, *act), (branch_all, ctx[0].T, ctx[1].T)])
+    branch_all = after(branch_all, *out_grad_sum.sent)
+    grad_pre, grad_qkv = [], []
+    for i in both:
+        grad_ctx = dot(second_layer[i][:, units:out_end], branch_all, 0, 1).astype(BF16)
+        grad_qkv.append(attend_back(code, doc, qkv[i], lse[i], grad_ctx))
+    feed_sum.line()
+    out_grad_sum.second()
+    normed_late = after(normed, *feed_sum.sent, *grad_qkv, *out_grad_sum.sent)
+    qkv_sum = GroupSum(plane, [(normed_late, grad_qkv[0].T, grad_qkv[1].T)])
+    out_grad_sum.line()
+    grad_sim, branch_late = after([grad_sim, branch_all], *qkv_sum.sent, *out_grad_sum.sent)
+    symmetric = (grad_sim.astype(F32) + grad_sim.T.astype(F32)).astype(BF16)
+    for i in both:
+        grad_act = (
+            dot(branch_late, second_layer[i][:, :units], 1, 0) + dot(symmetric, act[i], 1, 0) / hidden_units
+        )
+        grad_pre.append((grad_act * slope_pre[i].astype(F32)).astype(BF16))
+        if i == 0:
+            qkv_sum.second()
+            feed_sum.cores([grad_pre[0]])
+            symmetric, branch_late = after([symmetric, branch_late], grad_pre[0], *qkv_sum.sent, feed_sum.given)
+    memory_sum = GroupSum(plane, [(normed, *grad_pre)])
+    ffn_sum.sent = after(ffn_sum.sent, *memory_sum.sent)
+    ffn_sum.cores()
+    ffn_own = ffn_sum.chips()
+    block_out = turn(absolute((middle + ffn_own).astype(BF16)))
+    qkv_sum.line()
+    out_grad_sum.cores(memory_sum.sent)
+    grad_pre_late = after(grad_pre, *memory_sum.sent, *qkv_sum.sent)
+    normed_sum = RowSum(
+        dot(mixing, branch, 0, 0)
+        + sum_dots(
+            first_layer,
+            [(grad_pre_late[i], i, 0, units, 1) for i in both] + [(grad_qkv[i], i, units, q_end, 0) for i in both],
+        ).astype(F32)
+    )
+    normed_sum.cores()
+    memory_sum.second([normed_sum.sent, out_grad_sum.given])
+    qkv_sum.cores(memory_sum.sent)
+
+    grad_table = after(grad_table, *memory_sum.sent)
     for axis in ("c", "l"):
         grad_table = grad_table + swap(grad_table, axis)
     grad_alpha, grad_eta = span_table_back(kept_table, grad_table)
@@ -462,33 +621,16 @@
     grad_vectors = jnp.sum(grad_logits[:, :, None] * span_sums[None], axis=1)
     own_logits = lax.dynamic_slice_in_dim(grad_logits, member * own_spans, own_spans, 1)
     grad_spans = jnp.sum(own_logits[:, :, None] * gates[:, None, :], axis=0)
-
-    grad_memory_out, grad_project_out = reduce_group(
-        plane, [(branch_all, *act), (branch_all, ctx[0].T, ctx[1].T)]
-    )
-    symmetric = (grad_sim.astype(F32) + grad_sim.T.astype(F32)).astype(BF16)
-    grad_pre, grad_qkv = [], []
-    for i in both:
-        grad_act = (
-            dot(branch_all, second_layer[i][:, :units], 1, 0) + dot(symmetric, act[i], 1, 0) / hidden_units
-        )
-        grad_pre.append((grad_act * slope_pre[i].astype(F32)).astype(BF16))
-    (grad_memory_in,) = reduce_group(plane, [(normed, *grad_pre)])
-    for i in both:
-        grad_ctx = dot(second_layer[i][:, units:], branch_all, 0, 1).astype(BF16)
-        grad_qkv.append(attend_back(code, doc, qkv[i], lse[i], grad_ctx))
-    (grad_qkv_sum,) = reduce_group(plane, [(normed, grad_qkv[0].T, grad_qkv[1].T)])
-    grad_normed = scatter_rows(
-        dot(mixing, branch, 0, 0)
-        + sum(
-            dot(grad_pre[i], first_layer[i][:, :units], 1, 1)
-            + dot(grad_qkv[i], first_layer[i][:, units:], 0, 1)
-            for i in both
-        )
-    )
-    grad_normed = grad_normed + jnp.repeat(grad_spans, CH, axis=0)
+    grad_normed = after(normed_sum.chips(), *memory_sum.sent) + jnp.repeat(grad_spans, CH, axis=0)
     back_one, grad_gain_one = norm_back(x_own, inverse_one, gain_one, grad_normed)
     grad_block_in = turn(absolute((grad_middle + back_one).astype(BF16))).astype(F32)
+
+    memory_sum.line()
+    memory_sum.cores([grad_gain_one])
+    grad_gate, grad_up, grad_down = feed_sum.results()
+    (grad_qkv_sum,) = qkv_sum.results()
+    grad_memory_out, grad_project_out = out_grad_sum.results()
+    (grad_memory_in,) = memory_sum.results()
 
     gram = 0.0
     for i in both:
@@ -497,6 +639,7 @@
     written = (normed * valid[:, None].astype(BF16)).reshape(spans, CH, width)
     cross = jnp.einsum("ctd,csd->cts", written, written, preferred_element_type=F32)
     piece = jnp.sum(gram * cross, axis=(1, 2))
+    piece = after(piece, *memory_sum.sent)
     for axis in ("c", "l"):
         piece = piece + swap(piece, axis)
     surprise = jnp.sqrt(piece / (hidden_units * width * CH))

time: 903 us -> 801 us (0.89)
  waiting for transfers between devices: 340 us -> 254 us
  matrix products: 204 us -> 141 us
  Pallas kernels: 22.7 us -> 55.1 us
  local copies, waits for them, and re-layouts: 87.4 us -> 113 us
  starting transfers between devices: 105 us -> 91.1 us
    ppermute x82 -> x78, waiting for transfers between devices: 302 us -> 228 us  [swap(): return lax.ppermute(x, axis, [(0, 1), (1, 0)])]
    dot_general x77 -> x63, matrix products: 201 us -> 131 us  [dot(): lax.dot_general(a, b, (((ca,), (cb,)), ((), ())), preferred_element_type=...]
    pallas_call x0 -> x4, Pallas kernels: none -> 32.3 us  [sum_dots(): pl.pallas_call(functools.partial(sum_kernel, [t[1:] for t in terms], len(...]
    unnamed x284 -> x379, local copies, waits for them, and re-layouts: 32.2 us -> 60.3 us
    select_n x21 -> x23, other arithmetic: 42.7 us -> 17 us  [the longest x20 16.6 us: by_index(): jnp.where(index == 0, first, second)]
    add x7 -> x16, other arithmetic: 8.93 us -> 27.6 us  [the longest x5 10.6 us: cores(): half = self.kept.astype(F32) + swap(self.sent, 'c').astype(F32)]
    ppermute x5, waiting for transfers between devices: 38.2 us -> 26 us  [turn(): return lax.ppermute(x, ('c', 'h'), [(0, 0), (1, 2), (2, 1), (3, 3)])]
    ppermute x82 -> x78, starting transfers between devices: 86.4 us -> 75.1 us  [swap(): return lax.ppermute(x, axis, [(0, 1), (1, 0)])]
  transfers between devices with their start and end apart: 87 -> 83, of which waited for: 24 -> 33; matrix products, arithmetic and copies ran while one was open for 40% -> 39% of each run, Pallas kernels for 3% -> 6%
where the time goes in v2:
time: 801 us; the launch traced here: 789 us
  waiting for transfers between devices  254 us (32%)
  matrix products  141 us (18%)
  other arithmetic  130 us (16%)
  local copies, waits for them, and re-layouts  113 us (14%)
  starting transfers between devices  91.1 us (11%)
  Pallas kernels  55.1 us (7%)
    ppermute x78, waiting for transfers between devices, swap(): return lax.ppermute(x, axis, [(0, 1), (1, 0)])  228 us
    dot_general x63, matrix products, dot(): lax.dot_general(a, b, (((ca,), (cb,)), ((), ())), preferred_element_type=...  131 us
    ppermute x78, starting transfers between devices, swap(): return lax.ppermute(x, axis, [(0, 1), (1, 0)])  75.1 us
    unnamed x379, local copies, waits for them, and re-layouts  60.3 us
    pallas_call x4, Pallas kernels, sum_dots(): pl.pallas_call(functools.partial(sum_kernel, [t[1:] for t in terms], len(...  32.3 us
    concatenate x29, other arithmetic, cat(): return jnp.concatenate(parts, axis=axis)  26.9 us
    ppermute x5, waiting for transfers between devices, turn(): return lax.ppermute(x, ('c', 'h'), [(0, 0), (1, 2), (2, 1), (3, 3)])  26 us
    select_n x20, other arithmetic, by_index(): jnp.where(index == 0, first, second)  16.6 us
  transfers between devices with their start and end apart: 83, of which 33 were waited for; matrix products, arithmetic and copies ran while one was open for 39% of the time, Pallas kernels for 6%

profile of v2, /device:TPU:1, one launch (start us, length us, event | category | flops | bytes accessed | tf_op | source)
XLA Modules:
  0.0 789.3 jit_solution(896299728510622408)
XLA Ops:
  46.9 11.6 %collective-permute-done.6 = bf16[384,1408]{1,0:T(8,128)(2,1)S(1)} collective-permute-done((bf16[384,1408]{1,0:T(8,128)(2,1)}, bf16[384,1408]{1,0:T(8,128)(2,1)S(1)}, u32[]{:S(2)}, u32[]{:S(2)}) %collective-permute-start.6) | collective-permute-done | bytes 1081376 | tf_op jit(solution)/shard_map/ppermute | solution.py:28
  61.0 10.3 %collective-permute-done.17 = bf16[256,1536]{1,0:T(8,128)(2,1)S(1)} collective-permute-done((bf16[256,1536]{1,0:T(8,128)(2,1)S(1)}, bf16[256,1536]{1,0:T(8,128)(2,1)S(1)}, u32[]{:S(2)}, u32[]{:S(2)}) %collective-permute-start.17) | collective-permute-done | bytes 786464 | tf_op jit(solution)/shard_map/ppermute | solution.py:28
  74.1 16.8 %collective-permute-done.10 = bf16[384,1408]{1,0:T(8,128)(2,1)} collective-permute-done((bf16[384,1408]{1,0:T(8,128)(2,1)S(1)}, bf16[384,1408]{1,0:T(8,128)(2,1)}, u32[]{:S(2)}, u32[]{:S(2)}) %collective-permute-start.10) | collective-permute-done | bytes 1081376 | tf_op jit(solution)/shard_map/ppermute | solution.py:28
  95.8 5.9 collective-permute-done.8
  103.1 8.0 %pad_maximum_fusion.refs_0_ = bf16[1536,1408]{1,0:T(8,128)(2,1)S(1)} fusion(bf16[384,1408]{1,0:T(8,128)(2,1)S(1)} %collective-permute-done.6, bf16[384,1408]{1,0:T(8,128)(2,1)S(1)} %collective-permute-done.19, bf16[384,1408]{1,0:T(8,128)(2,1)S(1)} %collective-permute-done.5, bf16[192,1408]{1,0:T(8,128)(2,1)S(1)} %copy-done.101, ...), kind=kLoop, calls=%fused_computation.5 | loop fusion | flops 21626880 | bytes 8650752 | tf_op jit(solution)/shard_map/concatenate | solution.py:42
  115.0 23.7 %collective-permute-done.11 = bf16[384,1024]{1,0:T(8,128)(2,1)} collective-permute-done((bf16[384,1024]{1,0:T(8,128)(2,1)}, bf16[384,1024]{1,0:T(8,128)(2,1)}, u32[]{:S(2)}, u32[]{:S(2)}) %collective-permute-start.11) | collective-permute-done | bytes 786464 | tf_op jit(solution)/shard_map/ppermute | solution.py:28
  154.7 5.1 fusion.59.qkv_ref
  203.0 6.3 multiply_convert_fusion.6
  216.5 17.8 %collective-permute-done.21 = bf16[384,1536]{1,0:T(8,128)(2,1)S(1)} collective-permute-done((bf16[384,1536]{1,0:T(8,128)(2,1)}, bf16[384,1536]{1,0:T(8,128)(2,1)S(1)}, u32[]{:S(2)}, u32[]{:S(2)}) %collective-permute-start.21) | collective-permute-done | bytes 1179680 | tf_op jit(solution)/shard_map/ppermute | solution.py:28
  234.3 5.6 collective-permute-done.23
  240.0 4.8 shard_map.255
  244.9 8.2 %shard_map.256 = bf16[1024,1536]{1,0:T(8,128)(2,1)S(1)} custom-call(bf16[1536,1024]{1,0:T(8,128)(2,1)S(1)} %copy-done.19, bf16[1536,1024]{1,0:T(8,128)(2,1)S(1)} %constant_dynamic-update-slice_fusion.4.refs_1_, bf16[1024,768]{1,0:T(8,128)(2,1)S(1)} %get-tuple-element.76.refs_2_, bf16[1024,768]{1,0:T(8,128)(2,1)S(1)} %get-tuple-element.77.refs_3_, ...), custom_call_target="tpu_custom_call" | custom-call | flops 6039797760 | bytes 22020096 | tf_op jit(solution)/shard_map/pallas_call | solution.py:247
  266.1 5.6 maximum_convert_fusion
  282.0 6.2 collective-permute-done.29
  288.3 13.8 %collective-permute-done.31 = bf16[384,1536]{1,0:T(8,128)(2,1)S(1)} collective-permute-done((bf16[384,1536]{1,0:T(8,128)(2,1)S(1)}, bf16[384,1536]{1,0:T(8,128)(2,1)S(1)}, u32[]{:S(2)}, u32[]{:S(2)}) %collective-permute-start.31) | collective-permute-done | bytes 1179680 | tf_op jit(solution)/shard_map/ppermute | solution.py:28
  310.3 14.0 %collective-permute-done.34 = bf16[256,1536]{1,0:T(8,128)(2,1)S(1)} collective-permute-done((bf16[256,1536]{1,0:T(8,128)(2,1)S(1)}, bf16[256,1536]{1,0:T(8,128)(2,1)S(1)}, u32[]{:S(2)}, u32[]{:S(2)}) %collective-permute-start.34) | collective-permute-done | bytes 786464 | tf_op jit(solution)/shard_map/ppermute | solution.py:28
  327.8 6.8 collective-permute-done.32
  348.4 7.9 shard_map.258
  362.0 7.3 fusion.119
  409.6 4.9 collective-permute-done.39
  430.7 5.0 fusion.179
  435.7 12.2 %collective-permute-done.40 = bf16[256,1024]{1,0:T(8,128)(2,1)} collective-permute-done((bf16[256,1024]{1,0:T(8,128)(2,1)}, bf16[256,1024]{1,0:T(8,128)(2,1)}, u32[]{:S(2)}, u32[]{:S(2)}) %collective-permute-start.40) | collective-permute-done | bytes 524320 | tf_op jit(solution)/shard_map/ppermute | solution.py:28
  479.1 5.2 shard_map.261.refs_5_
  484.3 5.2 shard_map.260.refs_4_
  496.2 16.6 %collective-permute-done.48 = bf16[768,960]{0,1:T(8,128)(2,1)S(1)} collective-permute-done((bf16[768,960]{0,1:T(8,128)(2,1)S(1)}, bf16[768,960]{0,1:T(8,128)(2,1)S(1)}, u32[]{:S(2)}, u32[]{:S(2)}) %collective-permute-start.48) | collective-permute-done | bytes 1474592 | tf_op jit(solution)/shard_map/ppermute | solution.py:28
  523.9 6.8 collective-permute-done.50
  550.3 12.7 %collective-permute-done.54 = bf16[384,1536]{0,1:T(8,128)(2,1)} collective-permute-done((bf16[384,1536]{0,1:T(8,128)(2,1)}, bf16[384,1536]{0,1:T(8,128)(2,1)}, u32[]{:S(2)}, u32[]{:S(2)}) %collective-permute-start.54) | collective-permute-done | bytes 1179680 | tf_op jit(solution)/shard_map/ppermute | solution.py:28
  623.2 11.6 %shard_map.262 = bf16[1024,1536]{1,0:T(8,128)(2,1)S(1)} custom-call(bf16[1536,1408]{1,0:T(8,128)(2,1)S(1)} %copy-done.7, bf16[1536,1408]{1,0:T(8,128)(2,1)S(1)} %copy-done.14, bf16[1024,768]{1,0:T(8,128)(2,1)S(1)} %copy-done.26, bf16[1024,768]{1,0:T(8,128)(2,1)S(1)} %copy-done.32, bf16[576,1024]{1,0:T(8,128)(2,1)S(1)} %copy-done.23, ...), custom_call_target="tpu_custom_call" | custom-call | flops 8455716864 | bytes 30670848 | tf_op jit(solution)/shard_map/pallas_call | solution.py:247
  675.3 17.4 %collective-permute-done.66 = f32[16,16]{1,0:T(8,128)S(1)} collective-permute-done((f32[16,16]{1,0:T(8,128)S(1)}, f32[16,16]{1,0:T(8,128)S(1)}, u32[]{:S(2)}, u32[]{:S(2)}) %collective-permute-start.66) | collective-permute-done | bytes 1056 | tf_op jit(solution)/shard_map/ppermute | solution.py:28
  729.6 13.9 %collective-permute-done.73 = f32[5,1536]{1,0:T(8,128)S(1)} collective-permute-done((f32[5,1536]{1,0:T(8,128)S(1)}, f32[5,1536]{1,0:T(8,128)S(1)}, u32[]{:S(2)}, u32[]{:S(2)}) %collective-permute-start.73) | collective-permute-done | bytes 30752 | tf_op jit(solution)/shard_map/ppermute | solution.py:28
  764.4 12.8 %collective-permute-done.57 = bf16[256,1536]{1,0:T(8,128)(2,1)S(1)} collective-permute-done((bf16[256,1536]{1,0:T(8,128)(2,1)S(1)}, bf16[256,1536]{1,0:T(8,128)(2,1)S(1)}, u32[]{:S(2)}, u32[]{:S(2)}) %collective-permute-start.57) | collective-permute-done | bytes 786464 | tf_op jit(solution)/shard_map/ppermute | solution.py:32
  777.2 8.5 %collective-permute-done.67 = bf16[256,1536]{1,0:T(8,128)(2,1)} collective-permute-done((bf16[256,1536]{1,0:T(8,128)(2,1)}, bf16[256,1536]{1,0:T(8,128)(2,1)}, u32[]{:S(2)}, u32[]{:S(2)}) %collective-permute-start.67) | collective-permute-done | bytes 786464 | tf_op jit(solution)/shard_map/ppermute | solution.py:32
  (796 shorter events, 466.5 us)
Async XLA Ops:
  41.5 49.4 %collective-permute-start.10 = (bf16[384,1408]{1,0:T(8,128)(2,1)S(1)}, bf16[384,1408]{1,0:T(8,128)(2,1)}, u32[]{:S(2)}, u32[]{:S(2)}) collective-permute-start(bf16[384,1408]{1,0:T(8,128)(2,1)S(1)} %copy-done.123), channel_id=1, source_target_pairs={{0,2},{2,0},{1,3},{3,1},{4,6},{6,4},{5,7},{7,5},{8,10},{10,8},{9,1... | collective-permute-start | bytes 3244040 | tf_op jit(solution)/shard_map/ppermute | solution.py:28
  60.7 42.2 %collective-permute-start.19 = (bf16[384,1408]{1,0:T(8,128)(2,1)S(1)}, bf16[384,1408]{1,0:T(8,128)(2,1)S(1)}, u32[]{:S(2)}, u32[]{:S(2)}) collective-permute-start(bf16[384,1408]{1,0:T(8,128)(2,1)S(1)} %collective-permute-done.5), channel_id=1, source_target_pairs={{0,16},{16,0},{1,17},{17,1},{2,18},{18,2},{3,19},{19,3},{4,20},{20... | collective-permute-start | bytes 3244040 | tf_op jit(solution)/shard_map/ppermute | solution.py:28
  72.9 73.6 %collective-permute-start.18 = (bf16[512,1536]{1,0:T(8,128)(2,1)}, bf16[512,1536]{1,0:T(8,128)(2,1)}, u32[]{:S(2)}, u32[]{:S(2)}) collective-permute-start(bf16[512,1536]{1,0:T(8,128)(2,1)} %pad_maximum_fusion.7), channel_id=1, source_target_pairs={{0,4},{4,0},{1,5},{5,1},{2,6},{6,2},{3,7},{7,3},{8,12},{12,8},{9,1... | collective-permute-start | bytes 4718600 | tf_op jit(solution)/shard_map/ppermute | solution.py:28
  90.9 47.8 %collective-permute-start.13 = (bf16[384,1408]{1,0:T(8,128)(2,1)}, bf16[384,1408]{1,0:T(8,128)(2,1)}, u32[]{:S(2)}, u32[]{:S(2)}) collective-permute-start(bf16[384,1408]{1,0:T(8,128)(2,1)} %collective-permute-done.10), channel_id=1, source_target_pairs={{0,16},{16,0},{1,17},{17,1},{2,18},{18,2},{3,19},{19,3},{4,20},{20... | collective-permute-start | bytes 3244040 | tf_op jit(solution)/shard_map/ppermute | solution.py:28
  94.5 44.2 %collective-permute-start.12 = (bf16[384,1408]{1,0:T(8,128)(2,1)}, bf16[384,1408]{1,0:T(8,128)(2,1)}, u32[]{:S(2)}, u32[]{:S(2)}) collective-permute-start(bf16[384,1408]{1,0:T(8,128)(2,1)} %collective-permute-done.10), channel_id=1, source_target_pairs={{0,8},{8,0},{1,9},{9,1},{2,10},{10,2},{3,11},{11,3},{4,12},{12,4},... | collective-permute-start | bytes 3244040 | tf_op jit(solution)/shard_map/ppermute | solution.py:28
  101.7 37.0 %collective-permute-start.11 = (bf16[384,1024]{1,0:T(8,128)(2,1)}, bf16[384,1024]{1,0:T(8,128)(2,1)}, u32[]{:S(2)}, u32[]{:S(2)}) collective-permute-start(bf16[384,1024]{1,0:T(8,128)(2,1)} %pad_maximum_fusion.22), channel_id=1, source_target_pairs={{0,2},{2,0},{1,3},{3,1},{4,6},{6,4},{5,7},{7,5},{8,10},{10,8},{9,1... | collective-permute-start | bytes 2359304 | tf_op jit(solution)/shard_map/ppermute | solution.py:28
  102.8 78.3 %collective-permute-start.9 = (bf16[384,1024]{1,0:T(8,128)(2,1)}, bf16[384,1024]{1,0:T(8,128)(2,1)}, u32[]{:S(2)}, u32[]{:S(2)}) collective-permute-start(bf16[384,1024]{1,0:T(8,128)(2,1)} %collective-permute-done.8), channel_id=1, source_target_pairs={{0,8},{8,0},{1,9},{9,1},{2,10},{10,2},{3,11},{11,3},{4,12},{12,4},... | collective-permute-start | bytes 2359304 | tf_op jit(solution)/shard_map/ppermute | solution.py:28
  138.7 56.3 %collective-permute-start.15 = (bf16[384,1024]{1,0:T(8,128)(2,1)}, bf16[384,1024]{1,0:T(8,128)(2,1)}, u32[]{:S(2)}, u32[]{:S(2)}) collective-permute-start(bf16[384,1024]{1,0:T(8,128)(2,1)} %collective-permute-done.11), channel_id=1, source_target_pairs={{0,16},{16,0},{1,17},{17,1},{2,18},{18,2},{3,19},{19,3},{4,20},{20... | collective-permute-start | bytes 2359304 | tf_op jit(solution)/shard_map/ppermute | solution.py:28
  139.1 57.1 %collective-permute-start.14 = (bf16[384,1024]{1,0:T(8,128)(2,1)}, bf16[384,1024]{1,0:T(8,128)(2,1)}, u32[]{:S(2)}, u32[]{:S(2)}) collective-permute-start(bf16[384,1024]{1,0:T(8,128)(2,1)} %collective-permute-done.11), channel_id=1, source_target_pairs={{0,8},{8,0},{1,9},{9,1},{2,10},{10,2},{3,11},{11,3},{4,12},{12,4},... | collective-permute-start | bytes 2359304 | tf_op jit(solution)/shard_map/ppermute | solution.py:28
  139.4 50.1 %collective-permute-start.22 = (bf16[256,1536]{1,0:T(8,128)(2,1)}, bf16[256,1536]{1,0:T(8,128)(2,1)}, u32[]{:S(2)}, u32[]{:S(2)}) collective-permute-start(bf16[256,1536]{1,0:T(8,128)(2,1)} %param.16), channel_id=1, source_target_pairs={{0,0},{2,4},{4,2},{6,6},{1,1},{3,5},{5,3},{7,7},{8,8},{10,12},{12,... | collective-permute-start | bytes 2359304 | tf_op jit(solution)/shard_map/ppermute | solution.py:32
  146.6 50.9 %collective-permute-start.20 = (bf16[384,1408]{1,0:T(8,128)(2,1)}, bf16[384,1408]{1,0:T(8,128)(2,1)}, u32[]{:S(2)}, u32[]{:S(2)}) collective-permute-start(bf16[384,1408]{1,0:T(8,128)(2,1)} %collective-permute-done.12), channel_id=1, source_target_pairs={{0,16},{16,0},{1,17},{17,1},{2,18},{18,2},{3,19},{19,3},{4,20},{20... | collective-permute-start | bytes 3244040 | tf_op jit(solution)/shard_map/ppermute | solution.py:28
  181.1 53.2 %collective-permute-start.21 = (bf16[384,1536]{1,0:T(8,128)(2,1)}, bf16[384,1536]{1,0:T(8,128)(2,1)S(1)}, u32[]{:S(2)}, u32[]{:S(2)}) collective-permute-start(bf16[384,1536]{1,0:T(8,128)(2,1)} %pad_maximum_fusion.14), channel_id=1, source_target_pairs={{0,2},{2,0},{1,3},{3,1},{4,6},{6,4},{5,7},{7,5},{8,10},{10,8},{9,1... | collective-permute-start | bytes 3538952 | tf_op jit(solution)/shard_map/ppermute | solution.py:28
  192.0 79.6 %collective-permute-start.36 = (bf16[256,1536]{1,0:T(8,128)(2,1)}, bf16[256,1536]{1,0:T(8,128)(2,1)}, u32[]{:S(2)}, u32[]{:S(2)}) collective-permute-start(bf16[256,1536]{1,0:T(8,128)(2,1)} %pad_maximum_fusion.23), channel_id=1, source_target_pairs={{0,1},{1,0},{2,3},{3,2},{4,5},{5,4},{6,7},{7,6},{8,9},{9,8},{10,11... | collective-permute-start | bytes 2359304 | tf_op jit(solution)/shard_map/ppermute | solution.py:28
  197.4 36.9 %collective-permute-start.24 = (bf16[384,1536]{1,0:T(8,128)(2,1)S(1)}, bf16[384,1536]{1,0:T(8,128)(2,1)S(1)}, u32[]{:S(2)}, u32[]{:S(2)}) collective-permute-start(bf16[384,1536]{1,0:T(8,128)(2,1)S(1)} %copy-done.102), channel_id=1, source_target_pairs={{0,16},{16,0},{1,17},{17,1},{2,18},{18,2},{3,19},{19,3},{4,20},{20... | collective-permute-start | bytes 3538952 | tf_op jit(solution)/shard_map/ppermute | solution.py:28
  197.9 42.1 %collective-permute-start.23 = (bf16[384,1536]{1,0:T(8,128)(2,1)S(1)}, bf16[384,1536]{1,0:T(8,128)(2,1)S(1)}, u32[]{:S(2)}, u32[]{:S(2)}) collective-permute-start(bf16[384,1536]{1,0:T(8,128)(2,1)S(1)} %copy-done.102), channel_id=1, source_target_pairs={{0,8},{8,0},{1,9},{9,1},{2,10},{10,2},{3,11},{11,3},{4,12},{12,4},... | collective-permute-start | bytes 3538952 | tf_op jit(solution)/shard_map/ppermute | solution.py:28
  280.3 46.7 %collective-permute-start.37 = (bf16[512,1536]{1,0:T(8,128)(2,1)S(1)}, bf16[512,1536]{1,0:T(8,128)(2,1)S(1)}, u32[]{:S(2)}, u32[]{:S(2)}) collective-permute-start(bf16[512,1536]{1,0:T(8,128)(2,1)S(1)} %pad_maximum_fusion.9), channel_id=1, source_target_pairs={{0,4},{4,0},{1,5},{5,1},{2,6},{6,2},{3,7},{7,3},{8,12},{12,8},{9,1... | collective-permute-start | bytes 4718600 | tf_op jit(solution)/shard_map/ppermute | solution.py:28
  396.8 55.8 %collective-permute-start.45 = (bf16[768,1536]{0,1:T(8,128)(2,1)}, bf16[768,1536]{0,1:T(8,128)(2,1)}, u32[]{:S(2)}, u32[]{:S(2)}) collective-permute-start(bf16[768,1536]{0,1:T(8,128)(2,1)} %pad_maximum_fusion.5), channel_id=1, source_target_pairs={{0,16},{16,0},{1,17},{17,1},{2,18},{18,2},{3,19},{19,3},{4,20},{20... | collective-permute-start | bytes 7077896 | tf_op jit(solution)/shard_map/ppermute | solution.py:28
  399.5 56.1 %collective-permute-start.44 = (bf16[768,1536]{0,1:T(8,128)(2,1)}, bf16[768,1536]{0,1:T(8,128)(2,1)}, u32[]{:S(2)}, u32[]{:S(2)}) collective-permute-start(bf16[768,1536]{0,1:T(8,128)(2,1)} %pad_maximum_fusion.4), channel_id=1, source_target_pairs={{0,8},{8,0},{1,9},{9,1},{2,10},{10,2},{3,11},{11,3},{4,12},{12,4},... | collective-permute-start | bytes 7077896 | tf_op jit(solution)/shard_map/ppermute | solution.py:28
  472.3 40.4 %collective-permute-start.48 = (bf16[768,960]{0,1:T(8,128)(2,1)S(1)}, bf16[768,960]{0,1:T(8,128)(2,1)S(1)}, u32[]{:S(2)}, u32[]{:S(2)}) collective-permute-start(bf16[768,960]{0,1:T(8,128)(2,1)S(1)} %pad_maximum_fusion.12), channel_id=1, source_target_pairs={{0,8},{8,0},{1,9},{9,1},{2,10},{10,2},{3,11},{11,3},{4,12},{12,4},... | collective-permute-start | bytes 4423688 | tf_op jit(solution)/shard_map/ppermute | solution.py:28
  472.8 42.6 %collective-permute-start.49 = (bf16[768,960]{0,1:T(8,128)(2,1)S(1)}, bf16[768,960]{0,1:T(8,128)(2,1)S(1)}, u32[]{:S(2)}, u32[]{:S(2)}) collective-permute-start(bf16[768,960]{0,1:T(8,128)(2,1)S(1)} %pad_maximum_fusion.13), channel_id=1, source_target_pairs={{0,16},{16,0},{1,17},{17,1},{2,18},{18,2},{3,19},{19,3},{4,20},{20... | collective-permute-start | bytes 4423688 | tf_op jit(solution)/shard_map/ppermute | solution.py:28
  493.1 69.9 %collective-permute-start.54 = (bf16[384,1536]{0,1:T(8,128)(2,1)}, bf16[384,1536]{0,1:T(8,128)(2,1)}, u32[]{:S(2)}, u32[]{:S(2)}) collective-permute-start(bf16[384,1536]{0,1:T(8,128)(2,1)} %add_convert_fusion), channel_id=1, source_target_pairs={{0,2},{2,0},{1,3},{3,1},{4,6},{6,4},{5,7},{7,5},{8,10},{10,8},{9,1... | collective-permute-start | bytes 3538952 | tf_op jit(solution)/shard_map/ppermute | solution.py:28
  519.9 55.6 %collective-permute-start.52 = (bf16[768,576]{0,1:T(8,128)(2,1)}, bf16[768,576]{0,1:T(8,128)(2,1)}, u32[]{:S(2)}, u32[]{:S(2)}) collective-permute-start(bf16[768,576]{0,1:T(8,128)(2,1)} %fusion.66), channel_id=1, source_target_pairs={{0,8},{8,0},{1,9},{9,1},{2,10},{10,2},{3,11},{11,3},{4,12},{12,4},... | collective-permute-start | bytes 2654216 | tf_op jit(solution)/shard_map/ppermute | solution.py:28
  521.1 58.0 %collective-permute-start.53 = (bf16[768,576]{0,1:T(8,128)(2,1)}, bf16[768,576]{0,1:T(8,128)(2,1)}, u32[]{:S(2)}, u32[]{:S(2)}) collective-permute-start(bf16[768,576]{0,1:T(8,128)(2,1)} %fusion.69), channel_id=1, source_target_pairs={{0,16},{16,0},{1,17},{17,1},{2,18},{18,2},{3,19},{19,3},{4,20},{20... | collective-permute-start | bytes 2654216 | tf_op jit(solution)/shard_map/ppermute | solution.py:28
  531.9 103.0 %collective-permute-start.63 = (bf16[384,960]{0,1:T(8,128)(2,1)}, bf16[384,960]{0,1:T(8,128)(2,1)}, u32[]{:S(2)}, u32[]{:S(2)}) collective-permute-start(bf16[384,960]{0,1:T(8,128)(2,1)} %add_convert_fusion.4), channel_id=1, source_target_pairs={{0,2},{2,0},{1,3},{3,1},{4,6},{6,4},{5,7},{7,5},{8,10},{10,8},{9,1... | collective-permute-start | bytes 2211848 | tf_op jit(solution)/shard_map/ppermute | solution.py:28
  574.5 90.9 %collective-permute-start.62 = (bf16[768,768]{0,1:T(8,128)(2,1)}, bf16[768,768]{0,1:T(8,128)(2,1)}, u32[]{:S(2)}, u32[]{:S(2)}) collective-permute-start(bf16[768,768]{0,1:T(8,128)(2,1)} %fusion.53), channel_id=1, source_target_pairs={{0,8},{8,0},{1,9},{9,1},{2,10},{10,2},{3,11},{11,3},{4,12},{12,4},... | collective-permute-start | bytes 3538952 | tf_op jit(solution)/shard_map/ppermute | solution.py:28
  578.1 38.2 %collective-permute-start.59 = (bf16[384,576]{0,1:T(8,128)(2,1)}, bf16[384,576]{0,1:T(8,128)(2,1)}, u32[]{:S(2)}, u32[]{:S(2)}) collective-permute-start(bf16[384,576]{0,1:T(8,128)(2,1)} %add_convert_fusion.7), channel_id=1, source_target_pairs={{0,16},{16,0},{1,17},{17,1},{2,18},{18,2},{3,19},{19,3},{4,20},{20... | collective-permute-start | bytes 1327112 | tf_op jit(solution)/shard_map/ppermute | solution.py:28
  592.1 70.1 %collective-permute-start.64 = (bf16[768,768]{0,1:T(8,128)(2,1)}, bf16[768,768]{0,1:T(8,128)(2,1)}, u32[]{:S(2)}, u32[]{:S(2)}) collective-permute-start(bf16[768,768]{0,1:T(8,128)(2,1)} %fusion.56), channel_id=1, source_target_pairs={{0,16},{16,0},{1,17},{17,1},{2,18},{18,2},{3,19},{19,3},{4,20},{20... | collective-permute-start | bytes 3538952 | tf_op jit(solution)/shard_map/ppermute | solution.py:28
  612.0 39.9 %collective-permute-start.55 = (bf16[512,1536]{1,0:T(8,128)(2,1)}, bf16[512,1536]{1,0:T(8,128)(2,1)}, u32[]{:S(2)}, u32[]{:S(2)}) collective-permute-start(bf16[512,1536]{1,0:T(8,128)(2,1)} %constant_dynamic-slice_fusion.2), channel_id=1, source_target_pairs={{0,4},{4,0},{1,5},{5,1},{2,6},{6,2},{3,7},{7,3},{8,12},{12,8},{9,1... | collective-permute-start | bytes 4718600 | tf_op jit(solution)/shard_map/ppermute | solution.py:28
  616.3 54.1 %collective-permute-start.77 = (bf16[384,576]{0,1:T(8,128)(2,1)}, bf16[384,576]{0,1:T(8,128)(2,1)}, u32[]{:S(2)}, u32[]{:S(2)}) collective-permute-start(bf16[384,576]{0,1:T(8,128)(2,1)} %fusion.105), channel_id=1, source_target_pairs={{0,2},{2,0},{1,3},{3,1},{4,6},{6,4},{5,7},{7,5},{8,10},{10,8},{9,1... | collective-permute-start | bytes 1327112 | tf_op jit(solution)/shard_map/ppermute | solution.py:28
  656.5 64.8 %collective-permute-start.56 = (bf16[256,1536]{1,0:T(8,128)(2,1)}, bf16[256,1536]{1,0:T(8,128)(2,1)}, u32[]{:S(2)}, u32[]{:S(2)}) collective-permute-start(bf16[256,1536]{1,0:T(8,128)(2,1)} %dynamic-slice_convert_fusion.3), channel_id=1, source_target_pairs={{0,1},{1,0},{2,3},{3,2},{4,5},{5,4},{6,7},{7,6},{8,9},{9,8},{10,11... | collective-permute-start | bytes 2359304 | tf_op jit(solution)/shard_map/ppermute | solution.py:28
  661.9 55.2 %collective-permute-start.61 = (bf16[256,1536]{1,0:T(8,128)(2,1)}, bf16[256,1536]{1,0:T(8,128)(2,1)}, u32[]{:S(2)}, u32[]{:S(2)}) collective-permute-start(bf16[256,1536]{1,0:T(8,128)(2,1)} %dynamic-slice_convert_fusion.2), channel_id=1, source_target_pairs={{0,1},{1,0},{2,3},{3,2},{4,5},{5,4},{6,7},{7,6},{8,9},{9,8},{10,11... | collective-permute-start | bytes 2359304 | tf_op jit(solution)/shard_map/ppermute | solution.py:28
  712.5 44.3 %collective-permute-start.80 = (bf16[384,768]{0,1:T(8,128)(2,1)}, bf16[384,768]{0,1:T(8,128)(2,1)S(1)}, u32[]{:S(2)}, u32[]{:S(2)}) collective-permute-start(bf16[384,768]{0,1:T(8,128)(2,1)} %fusion.94), channel_id=1, source_target_pairs={{0,2},{2,0},{1,3},{3,1},{4,6},{6,4},{5,7},{7,5},{8,10},{10,8},{9,1... | collective-permute-start | bytes 1769480 | tf_op jit(solution)/shard_map/ppermute | solution.py:28
  (229 other events, 2949.0 us)

commit v3 on v2

--- a/solution.py
+++ b/solution.py
@@ -463,22 +463,38 @@
     far0 = after(far0, *stages[0].near)
     stages.append(PlaneGather(plane, far0, "x"))
     far1 = swap(after(share1, far0), "h")
-    far1 = after(far1, *stages[2].near, *stages[1].near)
-    grad_turned = turn(after(grad_out, far1))
+    first_here = stages[0].whole()
+    both = range(2)
+    q_end = units + 3 * q_cols
+    out_end = units + q_cols
+    vectors = first_here[:, q_end : q_end + 4].T.astype(F32)
+    gain_one, gain_two, gates = vectors[0], vectors[3], vectors[1:3]
+
+    x_wide = x_full.astype(F32)
+    normed = (x_wide * inverse_of(x_wide) * gain_one).astype(BF16)
+
+    act, slope_pre, qkv, ctx, lse = [], [], [], [], []
+
+    def memory(first):
+        pre = dot(normed, first[:, :units], 1, 0)
+        sig_pre = jax.nn.sigmoid(pre)
+        act.append((pre * sig_pre).astype(BF16))
+        slope_pre.append((sig_pre * (1.0 + pre * (1.0 - sig_pre))).astype(BF16))
+
+    memory(first_here)
+    far1 = after(far1, *stages[2].near, *stages[1].near, stages[2].far, act[0])
     stages.append(PlaneGather(plane, far1, "y"))
     far2 = swap(after(share2, far1), "h")
-    share2 = after(share2, *stages[3].near, stages[1].far, stages[2].far, grad_turned)
+    share2 = after(share2, *stages[3].near, stages[1].far, stages[2].far, stages[3].far)
     stages.append(PlaneGather(plane, share2, "x"))
+    grad_turned = turn(after(grad_out, far2))
     far2 = after(far2, *stages[4].near, stages[3].far)
     stages.append(PlaneGather(plane, far2, "y"))
     first_layer, second_layer, feed = (
-        [stages[i].whole(), stages[j].whole()] for i, j in ((0, 2), (1, 3), (4, 5))
-    )
-    both = range(2)
-    q_end = units + 3 * q_cols
-    out_end = units + q_cols
-    vectors = first_layer[0][:, q_end : q_end + 4].T.astype(F32)
-    gain_one, gain_two, gates = vectors[0], vectors[3], vectors[1:3]
+        [first_here, stages[2].whole()],
+        [stages[1].whole(), stages[3].whole()],
+        [stages[4].whole(), stages[5].whole()],
+    )
 
     resets, count = flags[0, :-1], flags[0, -1]
     positions = jnp.arange(length, dtype=jnp.int32)
@@ -488,8 +504,6 @@
     code = jnp.where(valid > 0, doc, -1.0)[:, None]
     doc = doc[None, :]
 
-    x_wide = x_full.astype(F32)
-    normed = (x_wide * inverse_of(x_wide) * gain_one).astype(BF16)
     x_own = x_own.astype(F32)
     inverse_one = inverse_of(x_own)
     span_sums = jnp.sum(normed.reshape(spans, CH, width).astype(F32), axis=1)
@@ -498,12 +512,8 @@
     eta = jax.nn.sigmoid(logits[1] + ETA_SHIFT)
     table, kept_table = span_table(alpha, eta, keep)
 
-    act, slope_pre, qkv, ctx, lse = [], [], [], [], []
+    memory(first_layer[1])
     for i in both:
-        pre = dot(normed, first_layer[i][:, :units], 1, 0)
-        sig_pre = jax.nn.sigmoid(pre)
-        act.append((pre * sig_pre).astype(BF16))
-        slope_pre.append((sig_pre * (1.0 + pre * (1.0 - sig_pre))).astype(BF16))
         qkv.append(dot(first_layer[i][:, units:q_end], normed, 0, 1).astype(BF16))
     sim_sum = RowSum((dot(act[0], act[0], 1, 1) + dot(act[1], act[1], 1, 1)) / hidden_units)
     sim_sum.cores()
@@ -513,11 +523,10 @@
         context, logsum = attend(code, doc, qkv[i])
         ctx.append(context)
         lse.append(logsum)
-    act_late = after(act, far2)
     out_sum = RowSum(
         sum_dots(
             second_layer,
-            [(act_late[i], i, 0, units, 1) for i in both] + [(ctx[i], i, units, out_end, 0) for i in both],
+            [(act[i], i, 0, units, 1) for i in both] + [(ctx[i], i, units, out_end, 0) for i in both],
         )
     )
     out_sum.cores()
@@ -573,7 +582,9 @@
     feed_sum.second()
     branch_all = after(branch_all, *feed_sum.sent)
     out_grad_sum = GroupSum(plane, [(branch_all, *act), (branch_all, ctx[0].T, ctx[1].T)])
-    branch_all = after(branch_all, *out_grad_sum.sent)
+    ffn_sum.sent = after(ffn_sum.sent, branch_all)
+    ffn_sum.cores()
+    branch_all = after(branch_all, *out_grad_sum.sent, ffn_sum.sent)
     grad_pre, grad_qkv = [], []
     for i in both:
         grad_ctx = dot(second_layer[i][:, units:out_end], branch_all, 0, 1).astype(BF16)
@@ -596,9 +607,7 @@
             symmetric, branch_late = after([symmetric, branch_late], grad_pre[0], *qkv_sum.sent, feed_sum.given)
     memory_sum = GroupSum(plane, [(normed, *grad_pre)])
     ffn_sum.sent = after(ffn_sum.sent, *memory_sum.sent)
-    ffn_sum.cores()
-    ffn_own = ffn_sum.chips()
-    block_out = turn(absolute((middle + ffn_own).astype(BF16)))
+    block_out = turn(absolute((middle + ffn_sum.chips()).astype(BF16)))
     qkv_sum.line()
     out_grad_sum.cores(memory_sum.sent)
     grad_pre_late = after(grad_pre, *memory_sum.sent, *qkv_sum.sent)
@@ -621,7 +630,7 @@
     grad_vectors = jnp.sum(grad_logits[:, :, None] * span_sums[None], axis=1)
     own_logits = lax.dynamic_slice_in_dim(grad_logits, member * own_spans, own_spans, 1)
     grad_spans = jnp.sum(own_logits[:, :, None] * gates[:, None, :], axis=0)
-    grad_normed = after(normed_sum.chips(), *memory_sum.sent) + jnp.repeat(grad_spans, CH, axis=0)
+    grad_normed = after(normed_sum.chips(), *memory_sum.sent, block_out) + jnp.repeat(grad_spans, CH, axis=0)
     back_one, grad_gain_one = norm_back(x_own, inverse_one, gain_one, grad_normed)
     grad_block_in = turn(absolute((grad_middle + back_one).astype(BF16))).astype(F32)
 

time: 801 us -> 763 us (0.953)
  local copies, waits for them, and re-layouts: 113 us -> 87.9 us
  other arithmetic: 130 us -> 120 us
    unnamed x379 -> x359, local copies, waits for them, and re-layouts: 60.3 us -> 48.8 us
  transfers between devices with their start and end apart: 83 -> 83, of which waited for: 33 -> 36; matrix products, arithmetic and copies ran while one was open for 39% -> 36% of each run, Pallas kernels for 6% -> 6%
where the time goes in v3:
time: 763 us; the launch traced here: 756 us
  waiting for transfers between devices  259 us (34%)
  matrix products  135 us (18%)
  other arithmetic  120 us (16%)
  starting transfers between devices  93.6 us (12%)
  local copies, waits for them, and re-layouts  87.9 us (12%)
  Pallas kernels  55.1 us (7%)
    ppermute x78, waiting for transfers between devices, swap(): return lax.ppermute(x, axis, [(0, 1), (1, 0)])  229 us
    dot_general x63, matrix products, dot(): lax.dot_general(a, b, (((ca,), (cb,)), ((), ())), preferred_element_type=...  127 us
    ppermute x78, starting transfers between devices, swap(): return lax.ppermute(x, axis, [(0, 1), (1, 0)])  79.5 us
    unnamed x359, local copies, waits for them, and re-layouts  48.8 us
    pallas_call x4, Pallas kernels, sum_dots(): pl.pallas_call(functools.partial(sum_kernel, [t[1:] for t in terms], len(...  32.3 us
    ppermute x5, waiting for transfers between devices, turn(): return lax.ppermute(x, ('c', 'h'), [(0, 0), (1, 2), (2, 1), (3, 3)])  30.7 us
    concatenate x29, other arithmetic, cat(): return jnp.concatenate(parts, axis=axis)  26 us
  transfers between devices with their start and end apart: 83, of which 36 were waited for; matrix products, arithmetic and copies ran while one was open for 36% of the time, Pallas kernels for 6%

profile of v3, /device:TPU:1, one launch (start us, length us, event | category | flops | bytes accessed | tf_op | source)
XLA Modules:
  0.0 755.7 jit_solution(8210308392735999343)
XLA Ops:
  34.9 4.9 collective-permute-done
  47.0 11.3 %collective-permute-done.6 = bf16[384,1408]{1,0:T(8,128)(2,1)S(1)} collective-permute-done((bf16[384,1408]{1,0:T(8,128)(2,1)}, bf16[384,1408]{1,0:T(8,128)(2,1)S(1)}, u32[]{:S(2)}, u32[]{:S(2)}) %collective-permute-start.6) | collective-permute-done | bytes 1081376 | tf_op jit(solution)/shard_map/ppermute | solution.py:28
  60.7 10.1 %collective-permute-done.15 = bf16[256,1536]{1,0:T(8,128)(2,1)S(1)} collective-permute-done((bf16[256,1536]{1,0:T(8,128)(2,1)S(1)}, bf16[256,1536]{1,0:T(8,128)(2,1)S(1)}, u32[]{:S(2)}, u32[]{:S(2)}) %collective-permute-start.15) | collective-permute-done | bytes 786464 | tf_op jit(solution)/shard_map/ppermute | solution.py:28
  73.8 17.2 %collective-permute-done.10 = bf16[384,1408]{1,0:T(8,128)(2,1)} collective-permute-done((bf16[384,1408]{1,0:T(8,128)(2,1)S(1)}, bf16[384,1408]{1,0:T(8,128)(2,1)}, u32[]{:S(2)}, u32[]{:S(2)}) %collective-permute-start.10) | collective-permute-done | bytes 1081376 | tf_op jit(solution)/shard_map/ppermute | solution.py:28
  95.8 5.6 collective-permute-done.8
  102.9 8.1 %pad_maximum_fusion.refs_0_ = bf16[1536,1408]{1,0:T(8,128)(2,1)S(1)} fusion(bf16[384,1408]{1,0:T(8,128)(2,1)S(1)} %collective-permute-done.6, bf16[384,1408]{1,0:T(8,128)(2,1)S(1)} %collective-permute-done.17, bf16[384,1408]{1,0:T(8,128)(2,1)S(1)} %collective-permute-done.5, bf16[192,1408]{1,0:T(8,128)(2,1)S(1)} %get-tuple-element.210, ...), kind=kLoop, calls=%fused_computation.5 | loop fusion | flops 21626880 | bytes 8650752 | tf_op jit(solution)/shard_map/concatenate | solution.py:42
  114.5 5.3 collective-permute-done.12
  129.6 6.1 fusion.59.qkv_ref
  154.0 4.7 shard_map.254
  170.4 6.8 collective-permute-done.19
  188.7 7.5 collective-permute-done.20
  200.7 20.4 %collective-permute-done.23 = bf16[384,1536]{1,0:T(8,128)(2,1)S(1)} collective-permute-done((bf16[384,1536]{1,0:T(8,128)(2,1)S(1)}, bf16[384,1536]{1,0:T(8,128)(2,1)S(1)}, u32[]{:S(2)}, u32[]{:S(2)}) %collective-permute-start.23) | collective-permute-done | bytes 1179680 | tf_op jit(solution)/shard_map/ppermute | solution.py:28
  221.1 4.7 shard_map.255
  225.8 8.2 %shard_map.256 = bf16[1024,1536]{1,0:T(8,128)(2,1)S(1)} custom-call(bf16[1536,1024]{1,0:T(8,128)(2,1)S(1)} %constant_dynamic-update-slice_fusion.refs_0_, bf16[1536,1024]{1,0:T(8,128)(2,1)S(1)} %constant_dynamic-update-slice_fusion.4.refs_1_, bf16[1024,768]{1,0:T(8,128)(2,1)S(1)} %get-tuple-element.288.refs_2_, ...), custom_call_target="tpu_custom_call" | custom-call | flops 6039797760 | bytes 22020096 | tf_op jit(solution)/shard_map/pallas_call | solution.py:247
  244.7 13.0 %collective-permute-done.27 = bf16[256,1024]{1,0:T(8,128)(2,1)S(1)} collective-permute-done((bf16[256,1024]{1,0:T(8,128)(2,1)S(1)}, bf16[256,1024]{1,0:T(8,128)(2,1)S(1)}, u32[]{:S(2)}, u32[]{:S(2)}) %collective-permute-start.27) | collective-permute-done | bytes 524320 | tf_op jit(solution)/shard_map/ppermute | solution.py:28
  265.8 16.0 %collective-permute-done.36 = bf16[256,1536]{1,0:T(8,128)(2,1)S(1)} collective-permute-done((bf16[256,1536]{1,0:T(8,128)(2,1)S(1)}, bf16[256,1536]{1,0:T(8,128)(2,1)S(1)}, u32[]{:S(2)}, u32[]{:S(2)}) %collective-permute-start.36) | collective-permute-done | bytes 786464 | tf_op jit(solution)/shard_map/ppermute | solution.py:28
  283.7 5.4 collective-permute-done.30
  290.1 5.8 collective-permute-done.25
  300.1 15.0 %collective-permute-done.33 = bf16[256,1536]{1,0:T(8,128)(2,1)S(1)} collective-permute-done((bf16[256,1536]{1,0:T(8,128)(2,1)S(1)}, bf16[256,1536]{1,0:T(8,128)(2,1)S(1)}, u32[]{:S(2)}, u32[]{:S(2)}) %collective-permute-start.33) | collective-permute-done | bytes 786464 | tf_op jit(solution)/shard_map/ppermute | solution.py:28
  316.5 9.8 %collective-permute-done.32 = bf16[384,1536]{1,0:T(8,128)(2,1)S(1)} collective-permute-done((bf16[384,1536]{1,0:T(8,128)(2,1)S(1)}, bf16[384,1536]{1,0:T(8,128)(2,1)S(1)}, u32[]{:S(2)}, u32[]{:S(2)}) %collective-permute-start.32) | collective-permute-done | bytes 1179680 | tf_op jit(solution)/shard_map/ppermute | solution.py:28
  339.8 7.9 %shard_map.258 = bf16[1024,1536]{1,0:T(8,128)(2,1)S(1)} custom-call(bf16[1536,1536]{1,0:T(8,128)(2,1)S(1)} %constant_dynamic-update-slice_fusion.12.refs_0_, bf16[1536,1536]{1,0:T(8,128)(2,1)S(1)} %constant_dynamic-update-slice_fusion.16.refs_1_, bf16[1024,512]{1,0:T(8,128)(2,1)S(1)} %get-tuple-element.183.refs_2_, ...), custom_call_target="tpu_custom_call" | custom-call | flops 6442450944 | bytes 26214400 | tf_op jit(solution)/shard_map/pallas_call | solution.py:247
  350.8 7.1 fusion.119
  420.2 5.0 fusion.179
  425.2 11.3 %collective-permute-done.45 = bf16[256,1024]{1,0:T(8,128)(2,1)} collective-permute-done((bf16[256,1024]{1,0:T(8,128)(2,1)}, bf16[256,1024]{1,0:T(8,128)(2,1)}, u32[]{:S(2)}, u32[]{:S(2)}) %collective-permute-start.45) | collective-permute-done | bytes 524320 | tf_op jit(solution)/shard_map/ppermute | solution.py:28
  465.1 4.7 collective-permute-done.47
  475.7 25.6 %collective-permute-done.49 = bf16[768,960]{0,1:T(8,128)(2,1)S(1)} collective-permute-done((bf16[768,960]{0,1:T(8,128)(2,1)S(1)}, bf16[768,960]{0,1:T(8,128)(2,1)S(1)}, u32[]{:S(2)}, u32[]{:S(2)}) %collective-permute-start.49) | collective-permute-done | bytes 1474592 | tf_op jit(solution)/shard_map/ppermute | solution.py:28
  511.9 5.2 shard_map.261.refs_5_
  517.2 5.4 shard_map.260.refs_4_
  545.0 4.7 multiply_convert_fusion.4.refs_2_
  613.2 11.6 %shard_map.262 = bf16[1024,1536]{1,0:T(8,128)(2,1)S(1)} custom-call(bf16[1536,1408]{1,0:T(8,128)(2,1)S(1)} %copy-done.7, bf16[1536,1408]{1,0:T(8,128)(2,1)S(1)} %copy-done.11, bf16[1024,768]{1,0:T(8,128)(2,1)S(1)} %copy-done.24, bf16[1024,768]{1,0:T(8,128)(2,1)S(1)} %copy-done.29, bf16[576,1024]{1,0:T(8,128)(2,1)S(1)} %copy-done.21, ...), custom_call_target="tpu_custom_call" | custom-call | flops 8455716864 | bytes 30670848 | tf_op jit(solution)/shard_map/pallas_call | solution.py:247
  642.2 17.7 %collective-permute-done.57 = bf16[256,1536]{1,0:T(8,128)(2,1)} collective-permute-done((bf16[256,1536]{1,0:T(8,128)(2,1)}, bf16[256,1536]{1,0:T(8,128)(2,1)}, u32[]{:S(2)}, u32[]{:S(2)}) %collective-permute-start.57) | collective-permute-done | bytes 786464 | tf_op jit(solution)/shard_map/ppermute | solution.py:32
  725.6 18.2 %collective-permute-done.80 = bf16[384,768]{0,1:T(8,128)(2,1)S(1)} collective-permute-done((bf16[384,768]{0,1:T(8,128)(2,1)}, bf16[384,768]{0,1:T(8,128)(2,1)S(1)}, u32[]{:S(2)}, u32[]{:S(2)}) %collective-permute-start.80) | collective-permute-done | bytes 589856 | tf_op jit(solution)/shard_map/ppermute | solution.py:28
  (778 shorter events, 440.9 us)
Async XLA Ops:
  41.6 49.4 %collective-permute-start.10 = (bf16[384,1408]{1,0:T(8,128)(2,1)S(1)}, bf16[384,1408]{1,0:T(8,128)(2,1)}, u32[]{:S(2)}, u32[]{:S(2)}) collective-permute-start(bf16[384,1408]{1,0:T(8,128)(2,1)S(1)} %copy-done.107), channel_id=1, source_target_pairs={{0,2},{2,0},{1,3},{3,1},{4,6},{6,4},{5,7},{7,5},{8,10},{10,8},{9,1... | collective-permute-start | bytes 3244040 | tf_op jit(solution)/shard_map/ppermute | solution.py:28
  59.2 35.3 %collective-permute-start.7 = (bf16[384,1024]{1,0:T(8,128)(2,1)}, bf16[384,1024]{1,0:T(8,128)(2,1)S(1)}, u32[]{:S(2)}, u32[]{:S(2)}) collective-permute-start(bf16[384,1024]{1,0:T(8,128)(2,1)} %pad_maximum_fusion.22), channel_id=1, source_target_pairs={{0,8},{8,0},{1,9},{9,1},{2,10},{10,2},{3,11},{11,3},{4,12},{12,4},... | collective-permute-start | bytes 2359304 | tf_op jit(solution)/shard_map/ppermute | solution.py:28
  60.4 42.2 %collective-permute-start.17 = (bf16[384,1408]{1,0:T(8,128)(2,1)S(1)}, bf16[384,1408]{1,0:T(8,128)(2,1)S(1)}, u32[]{:S(2)}, u32[]{:S(2)}) collective-permute-start(bf16[384,1408]{1,0:T(8,128)(2,1)S(1)} %collective-permute-done.5), channel_id=1, source_target_pairs={{0,16},{16,0},{1,17},{17,1},{2,18},{18,2},{3,19},{19,3},{4,20},{20... | collective-permute-start | bytes 3244040 | tf_op jit(solution)/shard_map/ppermute | solution.py:28
  72.5 49.8 %collective-permute-start.16 = (bf16[512,1536]{1,0:T(8,128)(2,1)}, bf16[512,1536]{1,0:T(8,128)(2,1)}, u32[]{:S(2)}, u32[]{:S(2)}) collective-permute-start(bf16[512,1536]{1,0:T(8,128)(2,1)} %pad_maximum_fusion.7), channel_id=1, source_target_pairs={{0,4},{4,0},{1,5},{5,1},{2,6},{6,2},{3,7},{7,3},{8,12},{12,8},{9,1... | collective-permute-start | bytes 4718600 | tf_op jit(solution)/shard_map/ppermute | solution.py:28
  90.9 69.6 %collective-permute-start.13 = (bf16[384,1408]{1,0:T(8,128)(2,1)}, bf16[384,1408]{1,0:T(8,128)(2,1)}, u32[]{:S(2)}, u32[]{:S(2)}) collective-permute-start(bf16[384,1408]{1,0:T(8,128)(2,1)} %collective-permute-done.10), channel_id=1, source_target_pairs={{0,16},{16,0},{1,17},{17,1},{2,18},{18,2},{3,19},{19,3},{4,20},{20... | collective-permute-start | bytes 3244040 | tf_op jit(solution)/shard_map/ppermute | solution.py:28
  101.4 59.1 %collective-permute-start.11 = (bf16[384,1024]{1,0:T(8,128)(2,1)}, bf16[384,1024]{1,0:T(8,128)(2,1)}, u32[]{:S(2)}, u32[]{:S(2)}) collective-permute-start(bf16[384,1024]{1,0:T(8,128)(2,1)} %pad_maximum_fusion.22), channel_id=1, source_target_pairs={{0,2},{2,0},{1,3},{3,1},{4,6},{6,4},{5,7},{7,5},{8,10},{10,8},{9,1... | collective-permute-start | bytes 2359304 | tf_op jit(solution)/shard_map/ppermute | solution.py:28
  102.6 81.9 %collective-permute-start.9 = (bf16[384,1024]{1,0:T(8,128)(2,1)}, bf16[384,1024]{1,0:T(8,128)(2,1)}, u32[]{:S(2)}, u32[]{:S(2)}) collective-permute-start(bf16[384,1024]{1,0:T(8,128)(2,1)} %collective-permute-done.8), channel_id=1, source_target_pairs={{0,8},{8,0},{1,9},{9,1},{2,10},{10,2},{3,11},{11,3},{4,12},{12,4},... | collective-permute-start | bytes 2359304 | tf_op jit(solution)/shard_map/ppermute | solution.py:28
  119.8 40.7 %collective-permute-start.14 = (bf16[384,1408]{1,0:T(8,128)(2,1)}, bf16[384,1408]{1,0:T(8,128)(2,1)}, u32[]{:S(2)}, u32[]{:S(2)}) collective-permute-start(bf16[384,1408]{1,0:T(8,128)(2,1)} %collective-permute-done.12), channel_id=1, source_target_pairs={{0,16},{16,0},{1,17},{17,1},{2,18},{18,2},{3,19},{19,3},{4,20},{20... | collective-permute-start | bytes 3244040 | tf_op jit(solution)/shard_map/ppermute | solution.py:28
  186.9 52.3 %collective-permute-start.28 = (bf16[384,1536]{1,0:T(8,128)(2,1)S(1)}, bf16[384,1536]{1,0:T(8,128)(2,1)S(1)}, u32[]{:S(2)}, u32[]{:S(2)}) collective-permute-start(bf16[384,1536]{1,0:T(8,128)(2,1)S(1)} %copy-done.89), channel_id=1, source_target_pairs={{0,2},{2,0},{1,3},{3,1},{4,6},{6,4},{5,7},{7,5},{8,10},{10,8},{9,1... | collective-permute-start | bytes 3538952 | tf_op jit(solution)/shard_map/ppermute | solution.py:28
  264.3 31.6 %collective-permute-start.25 = (bf16[256,1536]{1,0:T(8,128)(2,1)S(1)}, bf16[256,1536]{1,0:T(8,128)(2,1)S(1)}, u32[]{:S(2)}, u32[]{:S(2)}) collective-permute-start(bf16[256,1536]{1,0:T(8,128)(2,1)S(1)} %dynamic-slice_convert_fusion.6), channel_id=1, source_target_pairs={{0,1},{1,0},{2,3},{3,2},{4,5},{5,4},{6,7},{7,6},{8,9},{9,8},{10,11... | collective-permute-start | bytes 2359304 | tf_op jit(solution)/shard_map/ppermute | solution.py:28
  282.2 33.6 %collective-permute-start.37 = (bf16[512,1536]{1,0:T(8,128)(2,1)S(1)}, bf16[512,1536]{1,0:T(8,128)(2,1)S(1)}, u32[]{:S(2)}, u32[]{:S(2)}) collective-permute-start(bf16[512,1536]{1,0:T(8,128)(2,1)S(1)} %pad_maximum_fusion.9), channel_id=1, source_target_pairs={{0,4},{4,0},{1,5},{5,1},{2,6},{6,2},{3,7},{7,3},{8,12},{12,8},{9,1... | collective-permute-start | bytes 4718600 | tf_op jit(solution)/shard_map/ppermute | solution.py:28
  282.3 33.4 %collective-permute-start.31 = (bf16[384,1536]{1,0:T(8,128)(2,1)S(1)}, bf16[384,1536]{1,0:T(8,128)(2,1)S(1)}, u32[]{:S(2)}, u32[]{:S(2)}) collective-permute-start(bf16[384,1536]{1,0:T(8,128)(2,1)S(1)} %collective-permute-done.22), channel_id=1, source_target_pairs={{0,16},{16,0},{1,17},{17,1},{2,18},{18,2},{3,19},{19,3},{4,20},{20... | collective-permute-start | bytes 3538952 | tf_op jit(solution)/shard_map/ppermute | solution.py:28
  386.8 54.4 %collective-permute-start.43 = (bf16[768,1536]{0,1:T(8,128)(2,1)}, bf16[768,1536]{0,1:T(8,128)(2,1)}, u32[]{:S(2)}, u32[]{:S(2)}) collective-permute-start(bf16[768,1536]{0,1:T(8,128)(2,1)} %pad_maximum_fusion.5), channel_id=1, source_target_pairs={{0,16},{16,0},{1,17},{17,1},{2,18},{18,2},{3,19},{19,3},{4,20},{20... | collective-permute-start | bytes 7077896 | tf_op jit(solution)/shard_map/ppermute | solution.py:28
  389.8 54.6 %collective-permute-start.42 = (bf16[768,1536]{0,1:T(8,128)(2,1)}, bf16[768,1536]{0,1:T(8,128)(2,1)}, u32[]{:S(2)}, u32[]{:S(2)}) collective-permute-start(bf16[768,1536]{0,1:T(8,128)(2,1)} %pad_maximum_fusion.4), channel_id=1, source_target_pairs={{0,8},{8,0},{1,9},{9,1},{2,10},{10,2},{3,11},{11,3},{4,12},{12,4},... | collective-permute-start | bytes 7077896 | tf_op jit(solution)/shard_map/ppermute | solution.py:28
  406.6 31.2 %collective-permute-start.40 = (bf16[256,1536]{1,0:T(8,128)(2,1)}, bf16[256,1536]{1,0:T(8,128)(2,1)}, u32[]{:S(2)}, u32[]{:S(2)}) collective-permute-start(bf16[256,1536]{1,0:T(8,128)(2,1)} %fusion.162), channel_id=1, source_target_pairs={{0,1},{1,0},{2,3},{3,2},{4,5},{5,4},{6,7},{7,6},{8,9},{9,8},{10,11... | collective-permute-start | bytes 2359304 | tf_op jit(solution)/shard_map/ppermute | solution.py:28
  459.7 41.7 %collective-permute-start.49 = (bf16[768,960]{0,1:T(8,128)(2,1)S(1)}, bf16[768,960]{0,1:T(8,128)(2,1)S(1)}, u32[]{:S(2)}, u32[]{:S(2)}) collective-permute-start(bf16[768,960]{0,1:T(8,128)(2,1)S(1)} %pad_maximum_fusion.12), channel_id=1, source_target_pairs={{0,8},{8,0},{1,9},{9,1},{2,10},{10,2},{3,11},{11,3},{4,12},{12,4},... | collective-permute-start | bytes 4423688 | tf_op jit(solution)/shard_map/ppermute | solution.py:28
  462.2 42.0 %collective-permute-start.50 = (bf16[768,960]{0,1:T(8,128)(2,1)S(1)}, bf16[768,960]{0,1:T(8,128)(2,1)S(1)}, u32[]{:S(2)}, u32[]{:S(2)}) collective-permute-start(bf16[768,960]{0,1:T(8,128)(2,1)S(1)} %pad_maximum_fusion.13), channel_id=1, source_target_pairs={{0,16},{16,0},{1,17},{17,1},{2,18},{18,2},{3,19},{19,3},{4,20},{20... | collective-permute-start | bytes 4423688 | tf_op jit(solution)/shard_map/ppermute | solution.py:28
  463.6 41.3 %collective-permute-start.44 = (bf16[512,1536]{1,0:T(8,128)(2,1)S(1)}, bf16[512,1536]{1,0:T(8,128)(2,1)S(1)}, u32[]{:S(2)}, u32[]{:S(2)}) collective-permute-start(bf16[512,1536]{1,0:T(8,128)(2,1)S(1)} %copy-done.105), channel_id=1, source_target_pairs={{0,4},{4,0},{1,5},{5,1},{2,6},{6,2},{3,7},{7,3},{8,12},{12,8},{9,1... | collective-permute-start | bytes 4718600 | tf_op jit(solution)/shard_map/ppermute | solution.py:28
  472.5 77.2 %collective-permute-start.55 = (bf16[384,1536]{0,1:T(8,128)(2,1)}, bf16[384,1536]{0,1:T(8,128)(2,1)}, u32[]{:S(2)}, u32[]{:S(2)}) collective-permute-start(bf16[384,1536]{0,1:T(8,128)(2,1)} %add_convert_fusion), channel_id=1, source_target_pairs={{0,2},{2,0},{1,3},{3,1},{4,6},{6,4},{5,7},{7,5},{8,10},{10,8},{9,1... | collective-permute-start | bytes 3538952 | tf_op jit(solution)/shard_map/ppermute | solution.py:28
  501.6 30.6 %collective-permute-start.52 = (bf16[384,960]{0,1:T(8,128)(2,1)S(1)}, bf16[384,960]{0,1:T(8,128)(2,1)S(1)}, u32[]{:S(2)}, u32[]{:S(2)}) collective-permute-start(bf16[384,960]{0,1:T(8,128)(2,1)S(1)} %add_convert_fusion.6), channel_id=1, source_target_pairs={{0,16},{16,0},{1,17},{17,1},{2,18},{18,2},{3,19},{19,3},{4,20},{20... | collective-permute-start | bytes 2211848 | tf_op jit(solution)/shard_map/ppermute | solution.py:28
  526.6 35.4 %collective-permute-start.53 = (bf16[768,576]{0,1:T(8,128)(2,1)}, bf16[768,576]{0,1:T(8,128)(2,1)}, u32[]{:S(2)}, u32[]{:S(2)}) collective-permute-start(bf16[768,576]{0,1:T(8,128)(2,1)} %fusion.66), channel_id=1, source_target_pairs={{0,8},{8,0},{1,9},{9,1},{2,10},{10,2},{3,11},{11,3},{4,12},{12,4},... | collective-permute-start | bytes 2654216 | tf_op jit(solution)/shard_map/ppermute | solution.py:28
  527.8 36.9 %collective-permute-start.54 = (bf16[768,576]{0,1:T(8,128)(2,1)}, bf16[768,576]{0,1:T(8,128)(2,1)}, u32[]{:S(2)}, u32[]{:S(2)}) collective-permute-start(bf16[768,576]{0,1:T(8,128)(2,1)} %fusion.69), channel_id=1, source_target_pairs={{0,16},{16,0},{1,17},{17,1},{2,18},{18,2},{3,19},{19,3},{4,20},{20... | collective-permute-start | bytes 2654216 | tf_op jit(solution)/shard_map/ppermute | solution.py:28
  532.2 97.9 %collective-permute-start.63 = (bf16[384,960]{0,1:T(8,128)(2,1)}, bf16[384,960]{0,1:T(8,128)(2,1)}, u32[]{:S(2)}, u32[]{:S(2)}) collective-permute-start(bf16[384,960]{0,1:T(8,128)(2,1)} %add_convert_fusion.4), channel_id=1, source_target_pairs={{0,2},{2,0},{1,3},{3,1},{4,6},{6,4},{5,7},{7,5},{8,10},{10,8},{9,1... | collective-permute-start | bytes 2211848 | tf_op jit(solution)/shard_map/ppermute | solution.py:28
  562.0 105.0 %collective-permute-start.62 = (bf16[768,768]{0,1:T(8,128)(2,1)}, bf16[768,768]{0,1:T(8,128)(2,1)}, u32[]{:S(2)}, u32[]{:S(2)}) collective-permute-start(bf16[768,768]{0,1:T(8,128)(2,1)} %fusion.53), channel_id=1, source_target_pairs={{0,8},{8,0},{1,9},{9,1},{2,10},{10,2},{3,11},{11,3},{4,12},{12,4},... | collective-permute-start | bytes 3538952 | tf_op jit(solution)/shard_map/ppermute | solution.py:28
  564.7 39.2 %collective-permute-start.59 = (bf16[384,576]{0,1:T(8,128)(2,1)}, bf16[384,576]{0,1:T(8,128)(2,1)}, u32[]{:S(2)}, u32[]{:S(2)}) collective-permute-start(bf16[384,576]{0,1:T(8,128)(2,1)} %add_convert_fusion.7), channel_id=1, source_target_pairs={{0,16},{16,0},{1,17},{17,1},{2,18},{18,2},{3,19},{19,3},{4,20},{20... | collective-permute-start | bytes 1327112 | tf_op jit(solution)/shard_map/ppermute | solution.py:28
  567.4 31.7 %collective-permute-start.58 = (bf16[384,576]{0,1:T(8,128)(2,1)}, bf16[384,576]{0,1:T(8,128)(2,1)}, u32[]{:S(2)}, u32[]{:S(2)}) collective-permute-start(bf16[384,576]{0,1:T(8,128)(2,1)} %fusion.108), channel_id=1, source_target_pairs={{0,8},{8,0},{1,9},{9,1},{2,10},{10,2},{3,11},{11,3},{4,12},{12,4},... | collective-permute-start | bytes 1327112 | tf_op jit(solution)/shard_map/ppermute | solution.py:28
  577.7 86.1 %collective-permute-start.64 = (bf16[768,768]{0,1:T(8,128)(2,1)}, bf16[768,768]{0,1:T(8,128)(2,1)}, u32[]{:S(2)}, u32[]{:S(2)}) collective-permute-start(bf16[768,768]{0,1:T(8,128)(2,1)} %fusion.56), channel_id=1, source_target_pairs={{0,16},{16,0},{1,17},{17,1},{2,18},{18,2},{3,19},{19,3},{4,20},{20... | collective-permute-start | bytes 3538952 | tf_op jit(solution)/shard_map/ppermute | solution.py:28
  599.2 35.2 %collective-permute-start.56 = (bf16[256,1536]{1,0:T(8,128)(2,1)}, bf16[256,1536]{1,0:T(8,128)(2,1)S(1)}, u32[]{:S(2)}, u32[]{:S(2)}) collective-permute-start(bf16[256,1536]{1,0:T(8,128)(2,1)} %dynamic-slice_convert_fusion.4), channel_id=1, source_target_pairs={{0,1},{1,0},{2,3},{3,2},{4,5},{5,4},{6,7},{7,6},{8,9},{9,8},{10,11... | collective-permute-start | bytes 2359304 | tf_op jit(solution)/shard_map/ppermute | solution.py:28
  603.9 66.3 %collective-permute-start.77 = (bf16[384,576]{0,1:T(8,128)(2,1)}, bf16[384,576]{0,1:T(8,128)(2,1)}, u32[]{:S(2)}, u32[]{:S(2)}) collective-permute-start(bf16[384,576]{0,1:T(8,128)(2,1)} %fusion.105), channel_id=1, source_target_pairs={{0,2},{2,0},{1,3},{3,1},{4,6},{6,4},{5,7},{7,5},{8,10},{10,8},{9,1... | collective-permute-start | bytes 1327112 | tf_op jit(solution)/shard_map/ppermute | solution.py:28
  663.8 32.4 %collective-permute-start.61 = (bf16[256,1536]{1,0:T(8,128)(2,1)}, bf16[256,1536]{1,0:T(8,128)(2,1)}, u32[]{:S(2)}, u32[]{:S(2)}) collective-permute-start(bf16[256,1536]{1,0:T(8,128)(2,1)} %dynamic-slice_convert_fusion.2), channel_id=1, source_target_pairs={{0,1},{1,0},{2,3},{3,2},{4,5},{5,4},{6,7},{7,6},{8,9},{9,8},{10,11... | collective-permute-start | bytes 2359304 | tf_op jit(solution)/shard_map/ppermute | solution.py:28
  706.4 37.4 %collective-permute-start.80 = (bf16[384,768]{0,1:T(8,128)(2,1)}, bf16[384,768]{0,1:T(8,128)(2,1)S(1)}, u32[]{:S(2)}, u32[]{:S(2)}) collective-permute-start(bf16[384,768]{0,1:T(8,128)(2,1)} %fusion.94), channel_id=1, source_target_pairs={{0,2},{2,0},{1,3},{3,1},{4,6},{6,4},{5,7},{7,5},{8,10},{10,8},{9,1... | collective-permute-start | bytes 1769480 | tf_op jit(solution)/shard_map/ppermute | solution.py:28
  720.3 31.8 %collective-permute-start.67 = (bf16[256,1536]{1,0:T(8,128)(2,1)S(1)}, bf16[256,1536]{1,0:T(8,128)(2,1)S(1)}, u32[]{:S(2)}, u32[]{:S(2)}) collective-permute-start(bf16[256,1536]{1,0:T(8,128)(2,1)S(1)} %pad_maximum_fusion.25), channel_id=1, source_target_pairs={{0,0},{2,4},{4,2},{6,6},{1,1},{3,5},{5,3},{7,7},{8,8},{10,12},{12,... | collective-permute-start | bytes 2359304 | tf_op jit(solution)/shard_map/ppermute | solution.py:32
  (219 other events, 3328.9 us)

commit v4 on v3

--- a/solution.py
+++ b/solution.py
@@ -224,9 +224,9 @@
             lse_ref[head : head + 1, cols] = top + jnp.log(total)
 
 
-def sum_kernel(terms, weights, *refs):
+def sum_kernel(terms, weights, extra, *refs):
     weight_refs, left_refs, out_ref = refs[:weights], refs[weights:-1], refs[-1]
-    total = None
+    total = dot(left_refs[-2][...], left_refs[-1][...], 0, 0) if extra else None
     for (which, start, stop, side), left_ref in zip(terms, left_refs):
         right = weight_refs[which][:, start:stop]
         part = dot(left_ref[...], right, side, 1)
@@ -234,7 +234,7 @@
     out_ref[...] = total.astype(BF16)
 
 
-def sum_dots(weights, terms):
+def sum_dots(weights, terms, extra=()):
     left, side = terms[0][0], terms[0][4]
     rows, width = left.shape[1 - side], weights[0].shape[0]
     tile, wide = min(512, rows), 512
@@ -244,8 +244,11 @@
             in_specs.append(pl.BlockSpec((tile, left.shape[1]), lambda n, m: (m, 0)))
         else:
             in_specs.append(pl.BlockSpec((left.shape[0], tile), lambda n, m: (0, m)))
+    if extra:
+        in_specs.append(pl.BlockSpec((extra[0].shape[0], tile), lambda n, m: (0, m)))
+        in_specs.append(pl.BlockSpec((extra[1].shape[0], wide), lambda n, m: (0, n)))
     return pl.pallas_call(
-        functools.partial(sum_kernel, [t[1:] for t in terms], len(weights)),
+        functools.partial(sum_kernel, [t[1:] for t in terms], len(weights), len(extra) > 0),
         grid=(width // wide, rows // tile),
         in_specs=in_specs,
         out_specs=pl.BlockSpec((tile, wide), lambda n, m: (m, n)),
@@ -256,7 +259,7 @@
             bytes_accessed=2 * sum(w.size for w in weights) + 8 * sum(t[0].size for t in terms),
             transcendentals=0,
         ),
-    )(*weights, *[t[0] for t in terms])
+    )(*weights, *[t[0] for t in terms], *extra)
 
 
 def fill_bias(code_ref, doc_ref, bias_ref):
@@ -590,7 +593,7 @@
         grad_ctx = dot(second_layer[i][:, units:out_end], branch_all, 0, 1).astype(BF16)
         grad_qkv.append(attend_back(code, doc, qkv[i], lse[i], grad_ctx))
     feed_sum.line()
-    out_grad_sum.second()
+    out_grad_sum.second(grad_qkv)
     normed_late = after(normed, *feed_sum.sent, *grad_qkv, *out_grad_sum.sent)
     qkv_sum = GroupSum(plane, [(normed_late, grad_qkv[0].T, grad_qkv[1].T)])
     out_grad_sum.line()
@@ -612,11 +615,11 @@
     out_grad_sum.cores(memory_sum.sent)
     grad_pre_late = after(grad_pre, *memory_sum.sent, *qkv_sum.sent)
     normed_sum = RowSum(
-        dot(mixing, branch, 0, 0)
-        + sum_dots(
+        sum_dots(
             first_layer,
             [(grad_pre_late[i], i, 0, units, 1) for i in both] + [(grad_qkv[i], i, units, q_end, 0) for i in both],
-        ).astype(F32)
+            (mixing, branch),
+        )
     )
     normed_sum.cores()
     memory_sum.second([normed_sum.sent, out_grad_sum.given])
@@ -635,7 +638,7 @@
     grad_block_in = turn(absolute((grad_middle + back_one).astype(BF16))).astype(F32)
 
     memory_sum.line()
-    memory_sum.cores([grad_gain_one])
+    memory_sum.cores()
     grad_gate, grad_up, grad_down = feed_sum.results()
     (grad_qkv_sum,) = qkv_sum.results()
     grad_memory_out, grad_project_out = out_grad_sum.results()

time: 763 us -> 749 us (0.982)
  other arithmetic: 120 us -> 110 us
    dot_general x63 -> x62, matrix products: 127 us -> 123 us  [dot(): lax.dot_general(a, b, (((ca,), (cb,)), ((), ())), preferred_element_type=...]
    unnamed x359 -> x367, local copies, waits for them, and re-layouts: 48.8 us -> 48.9 us
  transfers between devices with their start and end apart: 83 -> 83, of which waited for: 36 -> 36; matrix products, arithmetic and copies ran while one was open for 36% -> 35% of each run, Pallas kernels for 6% -> 7%
where the time goes in v4:
time: 749 us; the launch traced here: 742 us
  waiting for transfers between devices  264 us (35%)
  matrix products  132 us (18%)
  other arithmetic  110 us (15%)
  starting transfers between devices  88.5 us (12%)
  local copies, waits for them, and re-layouts  86 us (11%)
  Pallas kernels  57.1 us (8%)
    ppermute x78, waiting for transfers between devices, swap(): return lax.ppermute(x, axis, [(0, 1), (1, 0)])  236 us
    dot_general x62, matrix products, dot(): lax.dot_general(a, b, (((ca,), (cb,)), ((), ())), preferred_element_type=...  123 us
    ppermute x78, starting transfers between devices, swap(): return lax.ppermute(x, axis, [(0, 1), (1, 0)])  75.1 us
    unnamed x367, local copies, waits for them, and re-layouts  48.9 us
    pallas_call x4, Pallas kernels, sum_dots(): pl.pallas_call(functools.partial(sum_kernel, [t[1:] for t in terms], len(...  34.3 us
    ppermute x5, waiting for transfers between devices, turn(): return lax.ppermute(x, ('c', 'h'), [(0, 0), (1, 2), (2, 1), (3, 3)])  28.1 us
    concatenate x29, other arithmetic, cat(): return jnp.concatenate(parts, axis=axis)  23.2 us
  transfers between devices with their start and end apart: 83, of which 36 were waited for; matrix products, arithmetic and copies ran while one was open for 35% of the time, Pallas kernels for 7%

profile of v4, /device:TPU:1, one launch (start us, length us, event | category | flops | bytes accessed | tf_op | source)
XLA Modules:
  0.0 741.8 jit_solution(1452176734506987870)
XLA Ops:
  34.9 4.9 collective-permute-done
  47.0 11.3 %collective-permute-done.6 = bf16[384,1408]{1,0:T(8,128)(2,1)S(1)} collective-permute-done((bf16[384,1408]{1,0:T(8,128)(2,1)}, bf16[384,1408]{1,0:T(8,128)(2,1)S(1)}, u32[]{:S(2)}, u32[]{:S(2)}) %collective-permute-start.6) | collective-permute-done | bytes 1081376 | tf_op jit(solution)/shard_map/ppermute | solution.py:28
  60.7 10.1 %collective-permute-done.15 = bf16[256,1536]{1,0:T(8,128)(2,1)S(1)} collective-permute-done((bf16[256,1536]{1,0:T(8,128)(2,1)S(1)}, bf16[256,1536]{1,0:T(8,128)(2,1)S(1)}, u32[]{:S(2)}, u32[]{:S(2)}) %collective-permute-start.15) | collective-permute-done | bytes 786464 | tf_op jit(solution)/shard_map/ppermute | solution.py:28
  73.8 17.2 %collective-permute-done.10 = bf16[384,1408]{1,0:T(8,128)(2,1)} collective-permute-done((bf16[384,1408]{1,0:T(8,128)(2,1)S(1)}, bf16[384,1408]{1,0:T(8,128)(2,1)}, u32[]{:S(2)}, u32[]{:S(2)}) %collective-permute-start.10) | collective-permute-done | bytes 1081376 | tf_op jit(solution)/shard_map/ppermute | solution.py:28
  95.8 5.6 collective-permute-done.8
  102.9 8.2 %pad_maximum_fusion.refs_0_ = bf16[1536,1408]{1,0:T(8,128)(2,1)S(1)} fusion(bf16[384,1408]{1,0:T(8,128)(2,1)S(1)} %collective-permute-done.6, bf16[384,1408]{1,0:T(8,128)(2,1)S(1)} %collective-permute-done.17, bf16[384,1408]{1,0:T(8,128)(2,1)S(1)} %collective-permute-done.5, bf16[192,1408]{1,0:T(8,128)(2,1)S(1)} %get-tuple-element.212, ...), kind=kLoop, calls=%fused_computation.4 | loop fusion | flops 21626880 | bytes 8650752 | tf_op jit(solution)/shard_map/concatenate | solution.py:42
  114.6 5.2 collective-permute-done.12
  129.9 6.1 fusion.59.qkv_ref
  171.2 6.7 collective-permute-done.19
  189.4 7.5 %collective-permute-done.20 = bf16[384,1024]{1,0:T(8,128)(2,1)S(1)} collective-permute-done((bf16[384,1024]{1,0:T(8,128)(2,1)S(1)}, bf16[384,1024]{1,0:T(8,128)(2,1)S(1)}, u32[]{:S(2)}, u32[]{:S(2)}) %collective-permute-start.20) | collective-permute-done | bytes 786464 | tf_op jit(solution)/shard_map/ppermute | solution.py:28
  201.6 20.1 %collective-permute-done.23 = bf16[384,1536]{1,0:T(8,128)(2,1)S(1)} collective-permute-done((bf16[384,1536]{1,0:T(8,128)(2,1)S(1)}, bf16[384,1536]{1,0:T(8,128)(2,1)S(1)}, u32[]{:S(2)}, u32[]{:S(2)}) %collective-permute-start.23) | collective-permute-done | bytes 1179680 | tf_op jit(solution)/shard_map/ppermute | solution.py:28
  226.4 8.2 %shard_map.256 = bf16[1024,1536]{1,0:T(8,128)(2,1)S(1)} custom-call(bf16[1536,1024]{1,0:T(8,128)(2,1)S(1)} %constant_dynamic-update-slice_fusion.refs_0_, bf16[1536,1024]{1,0:T(8,128)(2,1)S(1)} %constant_dynamic-update-slice_fusion.4.refs_1_, bf16[1024,768]{1,0:T(8,128)(2,1)S(1)} %get-tuple-element.290.refs_2_, ...), custom_call_target="tpu_custom_call" | custom-call | flops 6039797760 | bytes 22020096 | tf_op jit(solution)/shard_map/pallas_call | solution.py:250
  245.4 13.0 %collective-permute-done.27 = bf16[256,1024]{1,0:T(8,128)(2,1)S(1)} collective-permute-done((bf16[256,1024]{1,0:T(8,128)(2,1)S(1)}, bf16[256,1024]{1,0:T(8,128)(2,1)S(1)}, u32[]{:S(2)}, u32[]{:S(2)}) %collective-permute-start.27) | collective-permute-done | bytes 524320 | tf_op jit(solution)/shard_map/ppermute | solution.py:28
  266.4 16.0 %collective-permute-done.36 = bf16[256,1536]{1,0:T(8,128)(2,1)S(1)} collective-permute-done((bf16[256,1536]{1,0:T(8,128)(2,1)S(1)}, bf16[256,1536]{1,0:T(8,128)(2,1)S(1)}, u32[]{:S(2)}, u32[]{:S(2)}) %collective-permute-start.36) | collective-permute-done | bytes 786464 | tf_op jit(solution)/shard_map/ppermute | solution.py:28
  284.3 5.4 collective-permute-done.30
  290.8 5.8 collective-permute-done.25
  300.7 15.0 %collective-permute-done.33 = bf16[256,1536]{1,0:T(8,128)(2,1)S(1)} collective-permute-done((bf16[256,1536]{1,0:T(8,128)(2,1)S(1)}, bf16[256,1536]{1,0:T(8,128)(2,1)S(1)}, u32[]{:S(2)}, u32[]{:S(2)}) %collective-permute-start.33) | collective-permute-done | bytes 786464 | tf_op jit(solution)/shard_map/ppermute | solution.py:28
  317.1 9.8 %collective-permute-done.32 = bf16[384,1536]{1,0:T(8,128)(2,1)S(1)} collective-permute-done((bf16[384,1536]{1,0:T(8,128)(2,1)S(1)}, bf16[384,1536]{1,0:T(8,128)(2,1)S(1)}, u32[]{:S(2)}, u32[]{:S(2)}) %collective-permute-start.32) | collective-permute-done | bytes 1179680 | tf_op jit(solution)/shard_map/ppermute | solution.py:28
  340.2 7.9 %shard_map.258 = bf16[1024,1536]{1,0:T(8,128)(2,1)S(1)} custom-call(bf16[1536,1536]{1,0:T(8,128)(2,1)S(1)} %constant_dynamic-update-slice_fusion.12.refs_0_, bf16[1536,1536]{1,0:T(8,128)(2,1)S(1)} %constant_dynamic-update-slice_fusion.16.refs_1_, bf16[1024,512]{1,0:T(8,128)(2,1)S(1)} %get-tuple-element.185.refs_2_, ...), custom_call_target="tpu_custom_call" | custom-call | flops 6442450944 | bytes 26214400 | tf_op jit(solution)/shard_map/pallas_call | solution.py:250
  351.9 7.3 fusion.119
  420.5 13.7 %collective-permute-done.45 = bf16[256,1024]{1,0:T(8,128)(2,1)} collective-permute-done((bf16[256,1024]{1,0:T(8,128)(2,1)}, bf16[256,1024]{1,0:T(8,128)(2,1)}, u32[]{:S(2)}, u32[]{:S(2)}) %collective-permute-start.45) | collective-permute-done | bytes 524320 | tf_op jit(solution)/shard_map/ppermute | solution.py:28
  462.8 4.7 collective-permute-done.47
  479.1 5.2 shard_map.261.refs_5_
  486.0 5.4 shard_map.260.refs_4_
  491.5 10.6 %collective-permute-done.50 = bf16[768,960]{0,1:T(8,128)(2,1)S(1)} collective-permute-done((bf16[768,960]{0,1:T(8,128)(2,1)S(1)}, bf16[768,960]{0,1:T(8,128)(2,1)S(1)}, u32[]{:S(2)}, u32[]{:S(2)}) %collective-permute-start.50) | collective-permute-done | bytes 1474592 | tf_op jit(solution)/shard_map/ppermute | solution.py:28
  511.3 8.7 %collective-permute-done.51 = bf16[384,960]{0,1:T(8,128)(2,1)S(1)} collective-permute-done((bf16[384,960]{0,1:T(8,128)(2,1)S(1)}, bf16[384,960]{0,1:T(8,128)(2,1)S(1)}, u32[]{:S(2)}, u32[]{:S(2)}) %collective-permute-start.51) | collective-permute-done | bytes 737312 | tf_op jit(solution)/shard_map/ppermute | solution.py:28
  534.0 4.7 multiply_convert_fusion.4.refs_2_
  543.2 5.5 collective-permute-start.82
  580.4 9.4 %collective-permute-done.58 = bf16[384,576]{0,1:T(8,128)(2,1)} collective-permute-done((bf16[384,576]{0,1:T(8,128)(2,1)}, bf16[384,576]{0,1:T(8,128)(2,1)}, u32[]{:S(2)}, u32[]{:S(2)}) %collective-permute-start.58) | collective-permute-done | bytes 442400 | tf_op jit(solution)/shard_map/ppermute | solution.py:28
  603.8 13.6 %shard_map.262 = bf16[1024,1536]{1,0:T(8,128)(2,1)S(1)} custom-call(bf16[1536,1408]{1,0:T(8,128)(2,1)S(1)} %copy-done.7, bf16[1536,1408]{1,0:T(8,128)(2,1)S(1)} %copy-done.13, bf16[1024,768]{1,0:T(8,128)(2,1)S(1)} %copy-done.28, bf16[1024,768]{1,0:T(8,128)(2,1)S(1)} %copy-done.34, bf16[576,1024]{1,0:T(8,128)(2,1)S(1)} %copy-done.24, ...), custom_call_target="tpu_custom_call" | custom-call | flops 8455716864 | bytes 30670848 | tf_op jit(solution)/shard_map/pallas_call | solution.py:250
  631.6 15.1 %collective-permute-done.57 = bf16[256,1536]{1,0:T(8,128)(2,1)} collective-permute-done((bf16[256,1536]{1,0:T(8,128)(2,1)}, bf16[256,1536]{1,0:T(8,128)(2,1)}, u32[]{:S(2)}, u32[]{:S(2)}) %collective-permute-start.57) | collective-permute-done | bytes 786464 | tf_op jit(solution)/shard_map/ppermute | solution.py:32
  710.5 18.7 %collective-permute-done.80 = bf16[384,768]{0,1:T(8,128)(2,1)S(1)} collective-permute-done((bf16[384,768]{0,1:T(8,128)(2,1)}, bf16[384,768]{0,1:T(8,128)(2,1)S(1)}, u32[]{:S(2)}, u32[]{:S(2)}) %collective-permute-start.80) | collective-permute-done | bytes 589856 | tf_op jit(solution)/shard_map/ppermute | solution.py:28
  (784 shorter events, 430.5 us)
Async XLA Ops:
  41.6 49.4 %collective-permute-start.10 = (bf16[384,1408]{1,0:T(8,128)(2,1)S(1)}, bf16[384,1408]{1,0:T(8,128)(2,1)}, u32[]{:S(2)}, u32[]{:S(2)}) collective-permute-start(bf16[384,1408]{1,0:T(8,128)(2,1)S(1)} %copy-done.109), channel_id=1, source_target_pairs={{0,2},{2,0},{1,3},{3,1},{4,6},{6,4},{5,7},{7,5},{8,10},{10,8},{9,1... | collective-permute-start | bytes 3244040 | tf_op jit(solution)/shard_map/ppermute | solution.py:28
  59.2 35.3 %collective-permute-start.7 = (bf16[384,1024]{1,0:T(8,128)(2,1)}, bf16[384,1024]{1,0:T(8,128)(2,1)S(1)}, u32[]{:S(2)}, u32[]{:S(2)}) collective-permute-start(bf16[384,1024]{1,0:T(8,128)(2,1)} %pad_maximum_fusion.22), channel_id=1, source_target_pairs={{0,8},{8,0},{1,9},{9,1},{2,10},{10,2},{3,11},{11,3},{4,12},{12,4},... | collective-permute-start | bytes 2359304 | tf_op jit(solution)/shard_map/ppermute | solution.py:28
  60.4 42.2 %collective-permute-start.17 = (bf16[384,1408]{1,0:T(8,128)(2,1)S(1)}, bf16[384,1408]{1,0:T(8,128)(2,1)S(1)}, u32[]{:S(2)}, u32[]{:S(2)}) collective-permute-start(bf16[384,1408]{1,0:T(8,128)(2,1)S(1)} %collective-permute-done.5), channel_id=1, source_target_pairs={{0,16},{16,0},{1,17},{17,1},{2,18},{18,2},{3,19},{19,3},{4,20},{20... | collective-permute-start | bytes 3244040 | tf_op jit(solution)/shard_map/ppermute | solution.py:28
  71.1 30.4 %collective-permute-start.8 = (bf16[384,1024]{1,0:T(8,128)(2,1)}, bf16[384,1024]{1,0:T(8,128)(2,1)}, u32[]{:S(2)}, u32[]{:S(2)}) collective-permute-start(bf16[384,1024]{1,0:T(8,128)(2,1)} %pad_maximum_fusion.22), channel_id=1, source_target_pairs={{0,16},{16,0},{1,17},{17,1},{2,18},{18,2},{3,19},{19,3},{4,20},{20... | collective-permute-start | bytes 2359304 | tf_op jit(solution)/shard_map/ppermute | solution.py:28
  72.6 49.7 %collective-permute-start.16 = (bf16[512,1536]{1,0:T(8,128)(2,1)}, bf16[512,1536]{1,0:T(8,128)(2,1)}, u32[]{:S(2)}, u32[]{:S(2)}) collective-permute-start(bf16[512,1536]{1,0:T(8,128)(2,1)} %pad_maximum_fusion.7), channel_id=1, source_target_pairs={{0,4},{4,0},{1,5},{5,1},{2,6},{6,2},{3,7},{7,3},{8,12},{12,8},{9,1... | collective-permute-start | bytes 4718600 | tf_op jit(solution)/shard_map/ppermute | solution.py:28
  90.9 70.2 %collective-permute-start.13 = (bf16[384,1408]{1,0:T(8,128)(2,1)}, bf16[384,1408]{1,0:T(8,128)(2,1)}, u32[]{:S(2)}, u32[]{:S(2)}) collective-permute-start(bf16[384,1408]{1,0:T(8,128)(2,1)} %collective-permute-done.10), channel_id=1, source_target_pairs={{0,16},{16,0},{1,17},{17,1},{2,18},{18,2},{3,19},{19,3},{4,20},{20... | collective-permute-start | bytes 3244040 | tf_op jit(solution)/shard_map/ppermute | solution.py:28
  101.4 59.7 %collective-permute-start.11 = (bf16[384,1024]{1,0:T(8,128)(2,1)}, bf16[384,1024]{1,0:T(8,128)(2,1)}, u32[]{:S(2)}, u32[]{:S(2)}) collective-permute-start(bf16[384,1024]{1,0:T(8,128)(2,1)} %pad_maximum_fusion.22), channel_id=1, source_target_pairs={{0,2},{2,0},{1,3},{3,1},{4,6},{6,4},{5,7},{7,5},{8,10},{10,8},{9,1... | collective-permute-start | bytes 2359304 | tf_op jit(solution)/shard_map/ppermute | solution.py:28
  102.6 82.5 %collective-permute-start.9 = (bf16[384,1024]{1,0:T(8,128)(2,1)}, bf16[384,1024]{1,0:T(8,128)(2,1)}, u32[]{:S(2)}, u32[]{:S(2)}) collective-permute-start(bf16[384,1024]{1,0:T(8,128)(2,1)} %collective-permute-done.8), channel_id=1, source_target_pairs={{0,8},{8,0},{1,9},{9,1},{2,10},{10,2},{3,11},{11,3},{4,12},{12,4},... | collective-permute-start | bytes 2359304 | tf_op jit(solution)/shard_map/ppermute | solution.py:28
  119.8 41.4 %collective-permute-start.14 = (bf16[384,1408]{1,0:T(8,128)(2,1)}, bf16[384,1408]{1,0:T(8,128)(2,1)}, u32[]{:S(2)}, u32[]{:S(2)}) collective-permute-start(bf16[384,1408]{1,0:T(8,128)(2,1)} %collective-permute-done.12), channel_id=1, source_target_pairs={{0,16},{16,0},{1,17},{17,1},{2,18},{18,2},{3,19},{19,3},{4,20},{20... | collective-permute-start | bytes 3244040 | tf_op jit(solution)/shard_map/ppermute | solution.py:28
  187.5 52.4 %collective-permute-start.28 = (bf16[384,1536]{1,0:T(8,128)(2,1)S(1)}, bf16[384,1536]{1,0:T(8,128)(2,1)S(1)}, u32[]{:S(2)}, u32[]{:S(2)}) collective-permute-start(bf16[384,1536]{1,0:T(8,128)(2,1)S(1)} %copy-done.90), channel_id=1, source_target_pairs={{0,2},{2,0},{1,3},{3,1},{4,6},{6,4},{5,7},{7,5},{8,10},{10,8},{9,1... | collective-permute-start | bytes 3538952 | tf_op jit(solution)/shard_map/ppermute | solution.py:28
  234.8 29.6 %collective-permute-start.24 = (bf16[512,1536]{1,0:T(8,128)(2,1)S(1)}, bf16[512,1536]{1,0:T(8,128)(2,1)S(1)}, u32[]{:S(2)}, u32[]{:S(2)}) collective-permute-start(bf16[512,1536]{1,0:T(8,128)(2,1)S(1)} %constant_dynamic-slice_fusion.6), channel_id=1, source_target_pairs={{0,4},{4,0},{1,5},{5,1},{2,6},{6,2},{3,7},{7,3},{8,12},{12,8},{9,1... | collective-permute-start | bytes 4718600 | tf_op jit(solution)/shard_map/ppermute | solution.py:28
  265.0 31.6 %collective-permute-start.25 = (bf16[256,1536]{1,0:T(8,128)(2,1)S(1)}, bf16[256,1536]{1,0:T(8,128)(2,1)S(1)}, u32[]{:S(2)}, u32[]{:S(2)}) collective-permute-start(bf16[256,1536]{1,0:T(8,128)(2,1)S(1)} %dynamic-slice_convert_fusion.5), channel_id=1, source_target_pairs={{0,1},{1,0},{2,3},{3,2},{4,5},{5,4},{6,7},{7,6},{8,9},{9,8},{10,11... | collective-permute-start | bytes 2359304 | tf_op jit(solution)/shard_map/ppermute | solution.py:28
  282.9 33.6 %collective-permute-start.37 = (bf16[512,1536]{1,0:T(8,128)(2,1)S(1)}, bf16[512,1536]{1,0:T(8,128)(2,1)S(1)}, u32[]{:S(2)}, u32[]{:S(2)}) collective-permute-start(bf16[512,1536]{1,0:T(8,128)(2,1)S(1)} %pad_maximum_fusion.9), channel_id=1, source_target_pairs={{0,4},{4,0},{1,5},{5,1},{2,6},{6,2},{3,7},{7,3},{8,12},{12,8},{9,1... | collective-permute-start | bytes 4718600 | tf_op jit(solution)/shard_map/ppermute | solution.py:28
  282.9 33.4 %collective-permute-start.31 = (bf16[384,1536]{1,0:T(8,128)(2,1)S(1)}, bf16[384,1536]{1,0:T(8,128)(2,1)S(1)}, u32[]{:S(2)}, u32[]{:S(2)}) collective-permute-start(bf16[384,1536]{1,0:T(8,128)(2,1)S(1)} %collective-permute-done.22), channel_id=1, source_target_pairs={{0,16},{16,0},{1,17},{17,1},{2,18},{18,2},{3,19},{19,3},{4,20},{20... | collective-permute-start | bytes 3538952 | tf_op jit(solution)/shard_map/ppermute | solution.py:28
  385.1 53.8 %collective-permute-start.43 = (bf16[768,1536]{0,1:T(8,128)(2,1)}, bf16[768,1536]{0,1:T(8,128)(2,1)}, u32[]{:S(2)}, u32[]{:S(2)}) collective-permute-start(bf16[768,1536]{0,1:T(8,128)(2,1)} %pad_maximum_fusion.5), channel_id=1, source_target_pairs={{0,16},{16,0},{1,17},{17,1},{2,18},{18,2},{3,19},{19,3},{4,20},{20... | collective-permute-start | bytes 7077896 | tf_op jit(solution)/shard_map/ppermute | solution.py:28
  388.2 54.0 %collective-permute-start.42 = (bf16[768,1536]{0,1:T(8,128)(2,1)}, bf16[768,1536]{0,1:T(8,128)(2,1)}, u32[]{:S(2)}, u32[]{:S(2)}) collective-permute-start(bf16[768,1536]{0,1:T(8,128)(2,1)} %pad_maximum_fusion.4), channel_id=1, source_target_pairs={{0,8},{8,0},{1,9},{9,1},{2,10},{10,2},{3,11},{11,3},{4,12},{12,4},... | collective-permute-start | bytes 7077896 | tf_op jit(solution)/shard_map/ppermute | solution.py:28
  404.3 31.3 %collective-permute-start.40 = (bf16[256,1536]{1,0:T(8,128)(2,1)}, bf16[256,1536]{1,0:T(8,128)(2,1)}, u32[]{:S(2)}, u32[]{:S(2)}) collective-permute-start(bf16[256,1536]{1,0:T(8,128)(2,1)} %fusion.162.refs_7_), channel_id=1, source_target_pairs={{0,1},{1,0},{2,3},{3,2},{4,5},{5,4},{6,7},{7,6},{8,9},{9,8},{10,11... | collective-permute-start | bytes 2359304 | tf_op jit(solution)/shard_map/ppermute | solution.py:28
  456.8 45.2 %collective-permute-start.49 = (bf16[768,960]{0,1:T(8,128)(2,1)S(1)}, bf16[768,960]{0,1:T(8,128)(2,1)S(1)}, u32[]{:S(2)}, u32[]{:S(2)}) collective-permute-start(bf16[768,960]{0,1:T(8,128)(2,1)S(1)} %pad_maximum_fusion.12), channel_id=1, source_target_pairs={{0,8},{8,0},{1,9},{9,1},{2,10},{10,2},{3,11},{11,3},{4,12},{12,4},... | collective-permute-start | bytes 4423688 | tf_op jit(solution)/shard_map/ppermute | solution.py:28
  461.4 40.6 %collective-permute-start.50 = (bf16[768,960]{0,1:T(8,128)(2,1)S(1)}, bf16[768,960]{0,1:T(8,128)(2,1)S(1)}, u32[]{:S(2)}, u32[]{:S(2)}) collective-permute-start(bf16[768,960]{0,1:T(8,128)(2,1)S(1)} %pad_maximum_fusion.13), channel_id=1, source_target_pairs={{0,16},{16,0},{1,17},{17,1},{2,18},{18,2},{3,19},{19,3},{4,20},{20... | collective-permute-start | bytes 4423688 | tf_op jit(solution)/shard_map/ppermute | solution.py:28
  470.3 68.5 %collective-permute-start.55 = (bf16[384,1536]{0,1:T(8,128)(2,1)}, bf16[384,1536]{0,1:T(8,128)(2,1)}, u32[]{:S(2)}, u32[]{:S(2)}) collective-permute-start(bf16[384,1536]{0,1:T(8,128)(2,1)} %add_convert_fusion), channel_id=1, source_target_pairs={{0,2},{2,0},{1,3},{3,1},{4,6},{6,4},{5,7},{7,5},{8,10},{10,8},{9,1... | collective-permute-start | bytes 3538952 | tf_op jit(solution)/shard_map/ppermute | solution.py:28
  508.1 44.5 %collective-permute-start.53 = (bf16[768,576]{0,1:T(8,128)(2,1)}, bf16[768,576]{0,1:T(8,128)(2,1)}, u32[]{:S(2)}, u32[]{:S(2)}) collective-permute-start(bf16[768,576]{0,1:T(8,128)(2,1)} %fusion.66), channel_id=1, source_target_pairs={{0,8},{8,0},{1,9},{9,1},{2,10},{10,2},{3,11},{11,3},{4,12},{12,4},... | collective-permute-start | bytes 2654216 | tf_op jit(solution)/shard_map/ppermute | solution.py:28
  509.5 46.6 %collective-permute-start.54 = (bf16[768,576]{0,1:T(8,128)(2,1)}, bf16[768,576]{0,1:T(8,128)(2,1)}, u32[]{:S(2)}, u32[]{:S(2)}) collective-permute-start(bf16[768,576]{0,1:T(8,128)(2,1)} %fusion.69), channel_id=1, source_target_pairs={{0,16},{16,0},{1,17},{17,1},{2,18},{18,2},{3,19},{19,3},{4,20},{20... | collective-permute-start | bytes 2654216 | tf_op jit(solution)/shard_map/ppermute | solution.py:28
  521.2 97.4 %collective-permute-start.63 = (bf16[384,960]{0,1:T(8,128)(2,1)}, bf16[384,960]{0,1:T(8,128)(2,1)}, u32[]{:S(2)}, u32[]{:S(2)}) collective-permute-start(bf16[384,960]{0,1:T(8,128)(2,1)} %add_convert_fusion.4), channel_id=1, source_target_pairs={{0,2},{2,0},{1,3},{3,1},{4,6},{6,4},{5,7},{7,5},{8,10},{10,8},{9,1... | collective-permute-start | bytes 2211848 | tf_op jit(solution)/shard_map/ppermute | solution.py:28
  552.6 100.1 %collective-permute-start.62 = (bf16[768,768]{0,1:T(8,128)(2,1)}, bf16[768,768]{0,1:T(8,128)(2,1)}, u32[]{:S(2)}, u32[]{:S(2)}) collective-permute-start(bf16[768,768]{0,1:T(8,128)(2,1)} %fusion.53), channel_id=1, source_target_pairs={{0,8},{8,0},{1,9},{9,1},{2,10},{10,2},{3,11},{11,3},{4,12},{12,4},... | collective-permute-start | bytes 3538952 | tf_op jit(solution)/shard_map/ppermute | solution.py:28
  555.4 39.0 %collective-permute-start.59 = (bf16[384,576]{0,1:T(8,128)(2,1)}, bf16[384,576]{0,1:T(8,128)(2,1)}, u32[]{:S(2)}, u32[]{:S(2)}) collective-permute-start(bf16[384,576]{0,1:T(8,128)(2,1)} %add_convert_fusion.7), channel_id=1, source_target_pairs={{0,16},{16,0},{1,17},{17,1},{2,18},{18,2},{3,19},{19,3},{4,20},{20... | collective-permute-start | bytes 1327112 | tf_op jit(solution)/shard_map/ppermute | solution.py:28
  559.0 30.8 %collective-permute-start.58 = (bf16[384,576]{0,1:T(8,128)(2,1)}, bf16[384,576]{0,1:T(8,128)(2,1)}, u32[]{:S(2)}, u32[]{:S(2)}) collective-permute-start(bf16[384,576]{0,1:T(8,128)(2,1)} %fusion.108), channel_id=1, source_target_pairs={{0,8},{8,0},{1,9},{9,1},{2,10},{10,2},{3,11},{11,3},{4,12},{12,4},... | collective-permute-start | bytes 1327112 | tf_op jit(solution)/shard_map/ppermute | solution.py:28
  569.3 79.5 %collective-permute-start.64 = (bf16[768,768]{0,1:T(8,128)(2,1)}, bf16[768,768]{0,1:T(8,128)(2,1)}, u32[]{:S(2)}, u32[]{:S(2)}) collective-permute-start(bf16[768,768]{0,1:T(8,128)(2,1)} %fusion.56), channel_id=1, source_target_pairs={{0,16},{16,0},{1,17},{17,1},{2,18},{18,2},{3,19},{19,3},{4,20},{20... | collective-permute-start | bytes 3538952 | tf_op jit(solution)/shard_map/ppermute | solution.py:28
  589.8 31.8 %collective-permute-start.56 = (bf16[256,1536]{1,0:T(8,128)(2,1)}, bf16[256,1536]{1,0:T(8,128)(2,1)S(1)}, u32[]{:S(2)}, u32[]{:S(2)}) collective-permute-start(bf16[256,1536]{1,0:T(8,128)(2,1)} %dynamic-slice_convert_fusion.3), channel_id=1, source_target_pairs={{0,1},{1,0},{2,3},{3,2},{4,5},{5,4},{6,7},{7,6},{8,9},{9,8},{10,11... | collective-permute-start | bytes 2359304 | tf_op jit(solution)/shard_map/ppermute | solution.py:28
  594.4 61.5 %collective-permute-start.77 = (bf16[384,576]{0,1:T(8,128)(2,1)}, bf16[384,576]{0,1:T(8,128)(2,1)}, u32[]{:S(2)}, u32[]{:S(2)}) collective-permute-start(bf16[384,576]{0,1:T(8,128)(2,1)} %fusion.105), channel_id=1, source_target_pairs={{0,2},{2,0},{1,3},{3,1},{4,6},{6,4},{5,7},{7,5},{8,10},{10,8},{9,1... | collective-permute-start | bytes 1327112 | tf_op jit(solution)/shard_map/ppermute | solution.py:28
  648.7 33.7 %collective-permute-start.61 = (bf16[256,1536]{1,0:T(8,128)(2,1)S(1)}, bf16[256,1536]{1,0:T(8,128)(2,1)}, u32[]{:S(2)}, u32[]{:S(2)}) collective-permute-start(bf16[256,1536]{1,0:T(8,128)(2,1)S(1)} %dynamic-slice_convert_fusion.1), channel_id=1, source_target_pairs={{0,1},{1,0},{2,3},{3,2},{4,5},{5,4},{6,7},{7,6},{8,9},{9,8},{10,11... | collective-permute-start | bytes 2359304 | tf_op jit(solution)/shard_map/ppermute | solution.py:28
  692.6 36.6 %collective-permute-start.80 = (bf16[384,768]{0,1:T(8,128)(2,1)}, bf16[384,768]{0,1:T(8,128)(2,1)S(1)}, u32[]{:S(2)}, u32[]{:S(2)}) collective-permute-start(bf16[384,768]{0,1:T(8,128)(2,1)} %fusion.94), channel_id=1, source_target_pairs={{0,2},{2,0},{1,3},{3,1},{4,6},{6,4},{5,7},{7,5},{8,10},{10,8},{9,1... | collective-permute-start | bytes 1769480 | tf_op jit(solution)/shard_map/ppermute | solution.py:28
  705.8 32.5 %collective-permute-start.67 = (bf16[256,1536]{1,0:T(8,128)(2,1)S(1)}, bf16[256,1536]{1,0:T(8,128)(2,1)S(1)}, u32[]{:S(2)}, u32[]{:S(2)}) collective-permute-start(bf16[256,1536]{1,0:T(8,128)(2,1)S(1)} %pad_maximum_fusion.25), channel_id=1, source_target_pairs={{0,0},{2,4},{4,2},{6,6},{1,1},{3,5},{5,3},{7,7},{8,8},{10,12},{12,... | collective-permute-start | bytes 2359304 | tf_op jit(solution)/shard_map/ppermute | solution.py:32
  (223 other events, 3788.8 us)

commit v5 on v4

--- a/solution.py
+++ b/solution.py
@@ -661,7 +661,7 @@
     )
     small = jnp.stack([grad_gain_one, grad_vectors[0] * 0.25, grad_vectors[1] * 0.25, grad_gain_two])
     small = cat([absolute(small), jnp.pad(numbers[None], ((0, 0), (0, width - 4)))], 0)
-    small = all_sum(plane, small)
+    small = all_sum(plane, after(small, memory_sum.given))
     logged = small[4, :3] / small[4, 3]
     share = gain_in.shape[0]
     index = lax.axis_index(plane + ("c", "h", "l"))

time: 749 us -> 758 us (1.012)
  waiting for transfers between devices: 264 us -> 274 us
    ppermute x5, waiting for transfers between devices: 28.1 us -> 38.2 us  [turn(): return lax.ppermute(x, ('c', 'h'), [(0, 0), (1, 2), (2, 1), (3, 3)])]
    unnamed x367 -> x371, local copies, waits for them, and re-layouts: 48.9 us -> 49.4 us
where the time goes in v5:
time: 758 us; the launch traced here: 750 us
  waiting for transfers between devices  274 us (36%)
  matrix products  130 us (17%)
  other arithmetic  110 us (15%)
  starting transfers between devices  87.6 us (12%)
  local copies, waits for them, and re-layouts  87.4 us (12%)
  Pallas kernels  57 us (8%)
    ppermute x78, waiting for transfers between devices, swap(): return lax.ppermute(x, axis, [(0, 1), (1, 0)])  235 us
    dot_general x62, matrix products, dot(): lax.dot_general(a, b, (((ca,), (cb,)), ((), ())), preferred_element_type=...  121 us
    ppermute x78, starting transfers between devices, swap(): return lax.ppermute(x, axis, [(0, 1), (1, 0)])  73.3 us
    unnamed x371, local copies, waits for them, and re-layouts  49.4 us
    ppermute x5, waiting for transfers between devices, turn(): return lax.ppermute(x, ('c', 'h'), [(0, 0), (1, 2), (2, 1), (3, 3)])  38.2 us
    pallas_call x4, Pallas kernels, sum_dots(): pl.pallas_call(functools.partial(sum_kernel, [t[1:] for t in terms], len(...  34.3 us
    concatenate x29, other arithmetic, cat(): return jnp.concatenate(parts, axis=axis)  23.2 us
  transfers between devices with their start and end apart: 83, of which 36 were waited for; matrix products, arithmetic and copies ran while one was open for 35% of the time, Pallas kernels for 7%

profile of v5, /device:TPU:1, one launch (start us, length us, event | category | flops | bytes accessed | tf_op | source)
XLA Modules:
  0.0 749.9 jit_solution(10544505968476319777)
XLA Ops:
  34.9 4.9 collective-permute-done
  47.0 11.3 %collective-permute-done.6 = bf16[384,1408]{1,0:T(8,128)(2,1)S(1)} collective-permute-done((bf16[384,1408]{1,0:T(8,128)(2,1)}, bf16[384,1408]{1,0:T(8,128)(2,1)S(1)}, u32[]{:S(2)}, u32[]{:S(2)}) %collective-permute-start.6) | collective-permute-done | bytes 1081376 | tf_op jit(solution)/shard_map/ppermute | solution.py:28
  60.7 10.1 %collective-permute-done.15 = bf16[256,1536]{1,0:T(8,128)(2,1)S(1)} collective-permute-done((bf16[256,1536]{1,0:T(8,128)(2,1)S(1)}, bf16[256,1536]{1,0:T(8,128)(2,1)S(1)}, u32[]{:S(2)}, u32[]{:S(2)}) %collective-permute-start.15) | collective-permute-done | bytes 786464 | tf_op jit(solution)/shard_map/ppermute | solution.py:28
  73.8 17.1 %collective-permute-done.10 = bf16[384,1408]{1,0:T(8,128)(2,1)} collective-permute-done((bf16[384,1408]{1,0:T(8,128)(2,1)S(1)}, bf16[384,1408]{1,0:T(8,128)(2,1)}, u32[]{:S(2)}, u32[]{:S(2)}) %collective-permute-start.10) | collective-permute-done | bytes 1081376 | tf_op jit(solution)/shard_map/ppermute | solution.py:28
  95.8 5.6 collective-permute-done.8
  102.9 8.2 %pad_maximum_fusion.refs_0_ = bf16[1536,1408]{1,0:T(8,128)(2,1)S(1)} fusion(bf16[384,1408]{1,0:T(8,128)(2,1)S(1)} %collective-permute-done.6, bf16[384,1408]{1,0:T(8,128)(2,1)S(1)} %collective-permute-done.17, bf16[384,1408]{1,0:T(8,128)(2,1)S(1)} %collective-permute-done.5, bf16[192,1408]{1,0:T(8,128)(2,1)S(1)} %get-tuple-element.214, ...), kind=kLoop, calls=%fused_computation.4 | loop fusion | flops 21626880 | bytes 8650752 | tf_op jit(solution)/shard_map/concatenate | solution.py:42
  114.6 5.2 collective-permute-done.12
  130.0 6.1 fusion.59.qkv_ref
  171.2 6.7 collective-permute-done.19
  189.4 7.5 %collective-permute-done.20 = bf16[384,1024]{1,0:T(8,128)(2,1)S(1)} collective-permute-done((bf16[384,1024]{1,0:T(8,128)(2,1)S(1)}, bf16[384,1024]{1,0:T(8,128)(2,1)S(1)}, u32[]{:S(2)}, u32[]{:S(2)}) %collective-permute-start.20) | collective-permute-done | bytes 786464 | tf_op jit(solution)/shard_map/ppermute | solution.py:28
  201.6 20.1 %collective-permute-done.23 = bf16[384,1536]{1,0:T(8,128)(2,1)S(1)} collective-permute-done((bf16[384,1536]{1,0:T(8,128)(2,1)S(1)}, bf16[384,1536]{1,0:T(8,128)(2,1)S(1)}, u32[]{:S(2)}, u32[]{:S(2)}) %collective-permute-start.23) | collective-permute-done | bytes 1179680 | tf_op jit(solution)/shard_map/ppermute | solution.py:28
  226.4 8.2 %shard_map.256 = bf16[1024,1536]{1,0:T(8,128)(2,1)S(1)} custom-call(bf16[1536,1024]{1,0:T(8,128)(2,1)S(1)} %constant_dynamic-update-slice_fusion.refs_0_, bf16[1536,1024]{1,0:T(8,128)(2,1)S(1)} %constant_dynamic-update-slice_fusion.4.refs_1_, bf16[1024,768]{1,0:T(8,128)(2,1)S(1)} %get-tuple-element.292.refs_2_, ...), custom_call_target="tpu_custom_call" | custom-call | flops 6039797760 | bytes 22020096 | tf_op jit(solution)/shard_map/pallas_call | solution.py:250
  245.4 13.0 %collective-permute-done.27 = bf16[256,1024]{1,0:T(8,128)(2,1)S(1)} collective-permute-done((bf16[256,1024]{1,0:T(8,128)(2,1)S(1)}, bf16[256,1024]{1,0:T(8,128)(2,1)S(1)}, u32[]{:S(2)}, u32[]{:S(2)}) %collective-permute-start.27) | collective-permute-done | bytes 524320 | tf_op jit(solution)/shard_map/ppermute | solution.py:28
  266.5 16.0 %collective-permute-done.36 = bf16[256,1536]{1,0:T(8,128)(2,1)S(1)} collective-permute-done((bf16[256,1536]{1,0:T(8,128)(2,1)S(1)}, bf16[256,1536]{1,0:T(8,128)(2,1)S(1)}, u32[]{:S(2)}, u32[]{:S(2)}) %collective-permute-start.36) | collective-permute-done | bytes 786464 | tf_op jit(solution)/shard_map/ppermute | solution.py:28
  284.4 5.4 collective-permute-done.30
  290.8 5.8 collective-permute-done.25
  300.7 15.0 %collective-permute-done.33 = bf16[256,1536]{1,0:T(8,128)(2,1)S(1)} collective-permute-done((bf16[256,1536]{1,0:T(8,128)(2,1)S(1)}, bf16[256,1536]{1,0:T(8,128)(2,1)S(1)}, u32[]{:S(2)}, u32[]{:S(2)}) %collective-permute-start.33) | collective-permute-done | bytes 786464 | tf_op jit(solution)/shard_map/ppermute | solution.py:28
  317.2 9.8 %collective-permute-done.32 = bf16[384,1536]{1,0:T(8,128)(2,1)S(1)} collective-permute-done((bf16[384,1536]{1,0:T(8,128)(2,1)S(1)}, bf16[384,1536]{1,0:T(8,128)(2,1)S(1)}, u32[]{:S(2)}, u32[]{:S(2)}) %collective-permute-start.32) | collective-permute-done | bytes 1179680 | tf_op jit(solution)/shard_map/ppermute | solution.py:28
  340.2 7.9 %shard_map.258 = bf16[1024,1536]{1,0:T(8,128)(2,1)S(1)} custom-call(bf16[1536,1536]{1,0:T(8,128)(2,1)S(1)} %constant_dynamic-update-slice_fusion.12.refs_0_, bf16[1536,1536]{1,0:T(8,128)(2,1)S(1)} %constant_dynamic-update-slice_fusion.16.refs_1_, bf16[1024,512]{1,0:T(8,128)(2,1)S(1)} %get-tuple-element.187.refs_2_, ...), custom_call_target="tpu_custom_call" | custom-call | flops 6442450944 | bytes 26214400 | tf_op jit(solution)/shard_map/pallas_call | solution.py:250
  352.0 7.3 fusion.119
  420.5 13.7 %collective-permute-done.45 = bf16[256,1024]{1,0:T(8,128)(2,1)} collective-permute-done((bf16[256,1024]{1,0:T(8,128)(2,1)}, bf16[256,1024]{1,0:T(8,128)(2,1)}, u32[]{:S(2)}, u32[]{:S(2)}) %collective-permute-start.45) | collective-permute-done | bytes 524320 | tf_op jit(solution)/shard_map/ppermute | solution.py:28
  479.0 5.2 shard_map.261.refs_5_
  486.0 5.4 shard_map.260.refs_4_
  491.4 10.6 %collective-permute-done.50 = bf16[768,960]{0,1:T(8,128)(2,1)S(1)} collective-permute-done((bf16[768,960]{0,1:T(8,128)(2,1)S(1)}, bf16[768,960]{0,1:T(8,128)(2,1)S(1)}, u32[]{:S(2)}, u32[]{:S(2)}) %collective-permute-start.50) | collective-permute-done | bytes 1474592 | tf_op jit(solution)/shard_map/ppermute | solution.py:28
  511.2 8.7 %collective-permute-done.51 = bf16[384,960]{0,1:T(8,128)(2,1)S(1)} collective-permute-done((bf16[384,960]{0,1:T(8,128)(2,1)S(1)}, bf16[384,960]{0,1:T(8,128)(2,1)S(1)}, u32[]{:S(2)}, u32[]{:S(2)}) %collective-permute-start.51) | collective-permute-done | bytes 737312 | tf_op jit(solution)/shard_map/ppermute | solution.py:28
  534.0 4.7 multiply_convert_fusion.4.refs_2_
  543.1 5.6 collective-permute-start.82
  580.4 9.4 %collective-permute-done.58 = bf16[384,576]{0,1:T(8,128)(2,1)} collective-permute-done((bf16[384,576]{0,1:T(8,128)(2,1)}, bf16[384,576]{0,1:T(8,128)(2,1)}, u32[]{:S(2)}, u32[]{:S(2)}) %collective-permute-start.58) | collective-permute-done | bytes 442400 | tf_op jit(solution)/shard_map/ppermute | solution.py:28
  603.7 13.6 %shard_map.262 = bf16[1024,1536]{1,0:T(8,128)(2,1)S(1)} custom-call(bf16[1536,1408]{1,0:T(8,128)(2,1)S(1)} %copy-done.7, bf16[1536,1408]{1,0:T(8,128)(2,1)S(1)} %copy-done.13, bf16[1024,768]{1,0:T(8,128)(2,1)S(1)} %copy-done.28, bf16[1024,768]{1,0:T(8,128)(2,1)S(1)} %copy-done.34, bf16[576,1024]{1,0:T(8,128)(2,1)S(1)} %copy-done.24, ...), custom_call_target="tpu_custom_call" | custom-call | flops 8455716864 | bytes 30670848 | tf_op jit(solution)/shard_map/pallas_call | solution.py:250
  631.5 15.1 %collective-permute-done.57 = bf16[256,1536]{1,0:T(8,128)(2,1)} collective-permute-done((bf16[256,1536]{1,0:T(8,128)(2,1)}, bf16[256,1536]{1,0:T(8,128)(2,1)}, u32[]{:S(2)}, u32[]{:S(2)}) %collective-permute-start.57) | collective-permute-done | bytes 786464 | tf_op jit(solution)/shard_map/ppermute | solution.py:32
  683.4 20.1 %collective-permute-done.72 = bf16[384,768]{0,1:T(8,128)(2,1)S(1)} collective-permute-done((bf16[384,768]{0,1:T(8,128)(2,1)S(1)}, bf16[384,768]{0,1:T(8,128)(2,1)S(1)}, u32[]{:S(2)}, u32[]{:S(2)}) %collective-permute-start.72) | collective-permute-done | bytes 589856 | tf_op jit(solution)/shard_map/ppermute | solution.py:28
  732.1 14.2 %collective-permute-done.67 = bf16[256,1536]{1,0:T(8,128)(2,1)S(1)} collective-permute-done((bf16[256,1536]{1,0:T(8,128)(2,1)S(1)}, bf16[256,1536]{1,0:T(8,128)(2,1)S(1)}, u32[]{:S(2)}, u32[]{:S(2)}) %collective-permute-start.67) | collective-permute-done | bytes 786464 | tf_op jit(solution)/shard_map/ppermute | solution.py:32
  (788 shorter events, 427.7 us)
Async XLA Ops:
  41.5 29.4 %collective-permute-start.15 = (bf16[256,1536]{1,0:T(8,128)(2,1)S(1)}, bf16[256,1536]{1,0:T(8,128)(2,1)S(1)}, u32[]{:S(2)}, u32[]{:S(2)}) collective-permute-start(bf16[256,1536]{1,0:T(8,128)(2,1)S(1)} %get-tuple-element.180), channel_id=1, source_target_pairs={{0,1},{1,0},{2,3},{3,2},{4,5},{5,4},{6,7},{7,6},{8,9},{9,8},{10,11... | collective-permute-start | bytes 2359304 | tf_op jit(solution)/shard_map/ppermute | solution.py:28
  41.6 49.4 %collective-permute-start.10 = (bf16[384,1408]{1,0:T(8,128)(2,1)S(1)}, bf16[384,1408]{1,0:T(8,128)(2,1)}, u32[]{:S(2)}, u32[]{:S(2)}) collective-permute-start(bf16[384,1408]{1,0:T(8,128)(2,1)S(1)} %copy-done.110), channel_id=1, source_target_pairs={{0,2},{2,0},{1,3},{3,1},{4,6},{6,4},{5,7},{7,5},{8,10},{10,8},{9,1... | collective-permute-start | bytes 3244040 | tf_op jit(solution)/shard_map/ppermute | solution.py:28
  59.2 35.3 %collective-permute-start.7 = (bf16[384,1024]{1,0:T(8,128)(2,1)}, bf16[384,1024]{1,0:T(8,128)(2,1)S(1)}, u32[]{:S(2)}, u32[]{:S(2)}) collective-permute-start(bf16[384,1024]{1,0:T(8,128)(2,1)} %pad_maximum_fusion.22), channel_id=1, source_target_pairs={{0,8},{8,0},{1,9},{9,1},{2,10},{10,2},{3,11},{11,3},{4,12},{12,4},... | collective-permute-start | bytes 2359304 | tf_op jit(solution)/shard_map/ppermute | solution.py:28
  60.4 42.2 %collective-permute-start.17 = (bf16[384,1408]{1,0:T(8,128)(2,1)S(1)}, bf16[384,1408]{1,0:T(8,128)(2,1)S(1)}, u32[]{:S(2)}, u32[]{:S(2)}) collective-permute-start(bf16[384,1408]{1,0:T(8,128)(2,1)S(1)} %collective-permute-done.5), channel_id=1, source_target_pairs={{0,16},{16,0},{1,17},{17,1},{2,18},{18,2},{3,19},{19,3},{4,20},{20... | collective-permute-start | bytes 3244040 | tf_op jit(solution)/shard_map/ppermute | solution.py:28
  71.1 30.3 %collective-permute-start.8 = (bf16[384,1024]{1,0:T(8,128)(2,1)}, bf16[384,1024]{1,0:T(8,128)(2,1)}, u32[]{:S(2)}, u32[]{:S(2)}) collective-permute-start(bf16[384,1024]{1,0:T(8,128)(2,1)} %pad_maximum_fusion.22), channel_id=1, source_target_pairs={{0,16},{16,0},{1,17},{17,1},{2,18},{18,2},{3,19},{19,3},{4,20},{20... | collective-permute-start | bytes 2359304 | tf_op jit(solution)/shard_map/ppermute | solution.py:28
  72.6 49.7 %collective-permute-start.16 = (bf16[512,1536]{1,0:T(8,128)(2,1)}, bf16[512,1536]{1,0:T(8,128)(2,1)}, u32[]{:S(2)}, u32[]{:S(2)}) collective-permute-start(bf16[512,1536]{1,0:T(8,128)(2,1)} %pad_maximum_fusion.7), channel_id=1, source_target_pairs={{0,4},{4,0},{1,5},{5,1},{2,6},{6,2},{3,7},{7,3},{8,12},{12,8},{9,1... | collective-permute-start | bytes 4718600 | tf_op jit(solution)/shard_map/ppermute | solution.py:28
  90.9 70.3 %collective-permute-start.13 = (bf16[384,1408]{1,0:T(8,128)(2,1)}, bf16[384,1408]{1,0:T(8,128)(2,1)}, u32[]{:S(2)}, u32[]{:S(2)}) collective-permute-start(bf16[384,1408]{1,0:T(8,128)(2,1)} %collective-permute-done.10), channel_id=1, source_target_pairs={{0,16},{16,0},{1,17},{17,1},{2,18},{18,2},{3,19},{19,3},{4,20},{20... | collective-permute-start | bytes 3244040 | tf_op jit(solution)/shard_map/ppermute | solution.py:28
  101.5 59.7 %collective-permute-start.11 = (bf16[384,1024]{1,0:T(8,128)(2,1)}, bf16[384,1024]{1,0:T(8,128)(2,1)}, u32[]{:S(2)}, u32[]{:S(2)}) collective-permute-start(bf16[384,1024]{1,0:T(8,128)(2,1)} %pad_maximum_fusion.22), channel_id=1, source_target_pairs={{0,2},{2,0},{1,3},{3,1},{4,6},{6,4},{5,7},{7,5},{8,10},{10,8},{9,1... | collective-permute-start | bytes 2359304 | tf_op jit(solution)/shard_map/ppermute | solution.py:28
  102.6 82.5 %collective-permute-start.9 = (bf16[384,1024]{1,0:T(8,128)(2,1)}, bf16[384,1024]{1,0:T(8,128)(2,1)}, u32[]{:S(2)}, u32[]{:S(2)}) collective-permute-start(bf16[384,1024]{1,0:T(8,128)(2,1)} %collective-permute-done.8), channel_id=1, source_target_pairs={{0,8},{8,0},{1,9},{9,1},{2,10},{10,2},{3,11},{11,3},{4,12},{12,4},... | collective-permute-start | bytes 2359304 | tf_op jit(solution)/shard_map/ppermute | solution.py:28
  119.8 41.4 %collective-permute-start.14 = (bf16[384,1408]{1,0:T(8,128)(2,1)}, bf16[384,1408]{1,0:T(8,128)(2,1)}, u32[]{:S(2)}, u32[]{:S(2)}) collective-permute-start(bf16[384,1408]{1,0:T(8,128)(2,1)} %collective-permute-done.12), channel_id=1, source_target_pairs={{0,16},{16,0},{1,17},{17,1},{2,18},{18,2},{3,19},{19,3},{4,20},{20... | collective-permute-start | bytes 3244040 | tf_op jit(solution)/shard_map/ppermute | solution.py:28
  187.5 52.4 %collective-permute-start.28 = (bf16[384,1536]{1,0:T(8,128)(2,1)S(1)}, bf16[384,1536]{1,0:T(8,128)(2,1)S(1)}, u32[]{:S(2)}, u32[]{:S(2)}) collective-permute-start(bf16[384,1536]{1,0:T(8,128)(2,1)S(1)} %copy-done.90), channel_id=1, source_target_pairs={{0,2},{2,0},{1,3},{3,1},{4,6},{6,4},{5,7},{7,5},{8,10},{10,8},{9,1... | collective-permute-start | bytes 3538952 | tf_op jit(solution)/shard_map/ppermute | solution.py:28
  234.8 29.6 %collective-permute-start.24 = (bf16[512,1536]{1,0:T(8,128)(2,1)S(1)}, bf16[512,1536]{1,0:T(8,128)(2,1)S(1)}, u32[]{:S(2)}, u32[]{:S(2)}) collective-permute-start(bf16[512,1536]{1,0:T(8,128)(2,1)S(1)} %constant_dynamic-slice_fusion.6), channel_id=1, source_target_pairs={{0,4},{4,0},{1,5},{5,1},{2,6},{6,2},{3,7},{7,3},{8,12},{12,8},{9,1... | collective-permute-start | bytes 4718600 | tf_op jit(solution)/shard_map/ppermute | solution.py:28
  265.0 31.6 %collective-permute-start.25 = (bf16[256,1536]{1,0:T(8,128)(2,1)S(1)}, bf16[256,1536]{1,0:T(8,128)(2,1)S(1)}, u32[]{:S(2)}, u32[]{:S(2)}) collective-permute-start(bf16[256,1536]{1,0:T(8,128)(2,1)S(1)} %dynamic-slice_convert_fusion.5), channel_id=1, source_target_pairs={{0,1},{1,0},{2,3},{3,2},{4,5},{5,4},{6,7},{7,6},{8,9},{9,8},{10,11... | collective-permute-start | bytes 2359304 | tf_op jit(solution)/shard_map/ppermute | solution.py:28
  282.9 33.7 %collective-permute-start.37 = (bf16[512,1536]{1,0:T(8,128)(2,1)S(1)}, bf16[512,1536]{1,0:T(8,128)(2,1)S(1)}, u32[]{:S(2)}, u32[]{:S(2)}) collective-permute-start(bf16[512,1536]{1,0:T(8,128)(2,1)S(1)} %pad_maximum_fusion.9), channel_id=1, source_target_pairs={{0,4},{4,0},{1,5},{5,1},{2,6},{6,2},{3,7},{7,3},{8,12},{12,8},{9,1... | collective-permute-start | bytes 4718600 | tf_op jit(solution)/shard_map/ppermute | solution.py:28
  283.0 33.4 %collective-permute-start.31 = (bf16[384,1536]{1,0:T(8,128)(2,1)S(1)}, bf16[384,1536]{1,0:T(8,128)(2,1)S(1)}, u32[]{:S(2)}, u32[]{:S(2)}) collective-permute-start(bf16[384,1536]{1,0:T(8,128)(2,1)S(1)} %collective-permute-done.22), channel_id=1, source_target_pairs={{0,16},{16,0},{1,17},{17,1},{2,18},{18,2},{3,19},{19,3},{4,20},{20... | collective-permute-start | bytes 3538952 | tf_op jit(solution)/shard_map/ppermute | solution.py:28
  298.3 28.7 %collective-permute-start.32 = (bf16[384,1536]{1,0:T(8,128)(2,1)S(1)}, bf16[384,1536]{1,0:T(8,128)(2,1)S(1)}, u32[]{:S(2)}, u32[]{:S(2)}) collective-permute-start(bf16[384,1536]{1,0:T(8,128)(2,1)S(1)} %collective-permute-done.30), channel_id=1, source_target_pairs={{0,8},{8,0},{1,9},{9,1},{2,10},{10,2},{3,11},{11,3},{4,12},{12,4},... | collective-permute-start | bytes 3538952 | tf_op jit(solution)/shard_map/ppermute | solution.py:28
  385.1 53.8 %collective-permute-start.43 = (bf16[768,1536]{0,1:T(8,128)(2,1)}, bf16[768,1536]{0,1:T(8,128)(2,1)}, u32[]{:S(2)}, u32[]{:S(2)}) collective-permute-start(bf16[768,1536]{0,1:T(8,128)(2,1)} %pad_maximum_fusion.5), channel_id=1, source_target_pairs={{0,16},{16,0},{1,17},{17,1},{2,18},{18,2},{3,19},{19,3},{4,20},{20... | collective-permute-start | bytes 7077896 | tf_op jit(solution)/shard_map/ppermute | solution.py:28
  388.1 54.0 %collective-permute-start.42 = (bf16[768,1536]{0,1:T(8,128)(2,1)}, bf16[768,1536]{0,1:T(8,128)(2,1)}, u32[]{:S(2)}, u32[]{:S(2)}) collective-permute-start(bf16[768,1536]{0,1:T(8,128)(2,1)} %pad_maximum_fusion.4), channel_id=1, source_target_pairs={{0,8},{8,0},{1,9},{9,1},{2,10},{10,2},{3,11},{11,3},{4,12},{12,4},... | collective-permute-start | bytes 7077896 | tf_op jit(solution)/shard_map/ppermute | solution.py:28
  404.2 31.2 %collective-permute-start.40 = (bf16[256,1536]{1,0:T(8,128)(2,1)}, bf16[256,1536]{1,0:T(8,128)(2,1)}, u32[]{:S(2)}, u32[]{:S(2)}) collective-permute-start(bf16[256,1536]{1,0:T(8,128)(2,1)} %fusion.161.refs_7_), channel_id=1, source_target_pairs={{0,1},{1,0},{2,3},{3,2},{4,5},{5,4},{6,7},{7,6},{8,9},{9,8},{10,11... | collective-permute-start | bytes 2359304 | tf_op jit(solution)/shard_map/ppermute | solution.py:28
  456.7 45.2 %collective-permute-start.49 = (bf16[768,960]{0,1:T(8,128)(2,1)S(1)}, bf16[768,960]{0,1:T(8,128)(2,1)S(1)}, u32[]{:S(2)}, u32[]{:S(2)}) collective-permute-start(bf16[768,960]{0,1:T(8,128)(2,1)S(1)} %pad_maximum_fusion.12), channel_id=1, source_target_pairs={{0,8},{8,0},{1,9},{9,1},{2,10},{10,2},{3,11},{11,3},{4,12},{12,4},... | collective-permute-start | bytes 4423688 | tf_op jit(solution)/shard_map/ppermute | solution.py:28
  461.4 40.6 %collective-permute-start.50 = (bf16[768,960]{0,1:T(8,128)(2,1)S(1)}, bf16[768,960]{0,1:T(8,128)(2,1)S(1)}, u32[]{:S(2)}, u32[]{:S(2)}) collective-permute-start(bf16[768,960]{0,1:T(8,128)(2,1)S(1)} %pad_maximum_fusion.13), channel_id=1, source_target_pairs={{0,16},{16,0},{1,17},{17,1},{2,18},{18,2},{3,19},{19,3},{4,20},{20... | collective-permute-start | bytes 4423688 | tf_op jit(solution)/shard_map/ppermute | solution.py:28
  470.2 68.5 %collective-permute-start.55 = (bf16[384,1536]{0,1:T(8,128)(2,1)}, bf16[384,1536]{0,1:T(8,128)(2,1)}, u32[]{:S(2)}, u32[]{:S(2)}) collective-permute-start(bf16[384,1536]{0,1:T(8,128)(2,1)} %add_convert_fusion), channel_id=1, source_target_pairs={{0,2},{2,0},{1,3},{3,1},{4,6},{6,4},{5,7},{7,5},{8,10},{10,8},{9,1... | collective-permute-start | bytes 3538952 | tf_op jit(solution)/shard_map/ppermute | solution.py:28
  508.1 44.5 %collective-permute-start.53 = (bf16[768,576]{0,1:T(8,128)(2,1)}, bf16[768,576]{0,1:T(8,128)(2,1)}, u32[]{:S(2)}, u32[]{:S(2)}) collective-permute-start(bf16[768,576]{0,1:T(8,128)(2,1)} %fusion.66), channel_id=1, source_target_pairs={{0,8},{8,0},{1,9},{9,1},{2,10},{10,2},{3,11},{11,3},{4,12},{12,4},... | collective-permute-start | bytes 2654216 | tf_op jit(solution)/shard_map/ppermute | solution.py:28
  509.5 46.6 %collective-permute-start.54 = (bf16[768,576]{0,1:T(8,128)(2,1)}, bf16[768,576]{0,1:T(8,128)(2,1)}, u32[]{:S(2)}, u32[]{:S(2)}) collective-permute-start(bf16[768,576]{0,1:T(8,128)(2,1)} %fusion.69), channel_id=1, source_target_pairs={{0,16},{16,0},{1,17},{17,1},{2,18},{18,2},{3,19},{19,3},{4,20},{20... | collective-permute-start | bytes 2654216 | tf_op jit(solution)/shard_map/ppermute | solution.py:28
  521.1 97.4 %collective-permute-start.63 = (bf16[384,960]{0,1:T(8,128)(2,1)}, bf16[384,960]{0,1:T(8,128)(2,1)}, u32[]{:S(2)}, u32[]{:S(2)}) collective-permute-start(bf16[384,960]{0,1:T(8,128)(2,1)} %add_convert_fusion.4), channel_id=1, source_target_pairs={{0,2},{2,0},{1,3},{3,1},{4,6},{6,4},{5,7},{7,5},{8,10},{10,8},{9,1... | collective-permute-start | bytes 2211848 | tf_op jit(solution)/shard_map/ppermute | solution.py:28
  552.6 100.1 %collective-permute-start.62 = (bf16[768,768]{0,1:T(8,128)(2,1)}, bf16[768,768]{0,1:T(8,128)(2,1)}, u32[]{:S(2)}, u32[]{:S(2)}) collective-permute-start(bf16[768,768]{0,1:T(8,128)(2,1)} %fusion.53), channel_id=1, source_target_pairs={{0,8},{8,0},{1,9},{9,1},{2,10},{10,2},{3,11},{11,3},{4,12},{12,4},... | collective-permute-start | bytes 3538952 | tf_op jit(solution)/shard_map/ppermute | solution.py:28
  555.3 39.0 %collective-permute-start.59 = (bf16[384,576]{0,1:T(8,128)(2,1)}, bf16[384,576]{0,1:T(8,128)(2,1)}, u32[]{:S(2)}, u32[]{:S(2)}) collective-permute-start(bf16[384,576]{0,1:T(8,128)(2,1)} %add_convert_fusion.7), channel_id=1, source_target_pairs={{0,16},{16,0},{1,17},{17,1},{2,18},{18,2},{3,19},{19,3},{4,20},{20... | collective-permute-start | bytes 1327112 | tf_op jit(solution)/shard_map/ppermute | solution.py:28
  559.0 30.8 %collective-permute-start.58 = (bf16[384,576]{0,1:T(8,128)(2,1)}, bf16[384,576]{0,1:T(8,128)(2,1)}, u32[]{:S(2)}, u32[]{:S(2)}) collective-permute-start(bf16[384,576]{0,1:T(8,128)(2,1)} %fusion.108), channel_id=1, source_target_pairs={{0,8},{8,0},{1,9},{9,1},{2,10},{10,2},{3,11},{11,3},{4,12},{12,4},... | collective-permute-start | bytes 1327112 | tf_op jit(solution)/shard_map/ppermute | solution.py:28
  569.2 79.4 %collective-permute-start.64 = (bf16[768,768]{0,1:T(8,128)(2,1)}, bf16[768,768]{0,1:T(8,128)(2,1)}, u32[]{:S(2)}, u32[]{:S(2)}) collective-permute-start(bf16[768,768]{0,1:T(8,128)(2,1)} %fusion.56), channel_id=1, source_target_pairs={{0,16},{16,0},{1,17},{17,1},{2,18},{18,2},{3,19},{19,3},{4,20},{20... | collective-permute-start | bytes 3538952 | tf_op jit(solution)/shard_map/ppermute | solution.py:28
  589.8 31.8 %collective-permute-start.56 = (bf16[256,1536]{1,0:T(8,128)(2,1)}, bf16[256,1536]{1,0:T(8,128)(2,1)S(1)}, u32[]{:S(2)}, u32[]{:S(2)}) collective-permute-start(bf16[256,1536]{1,0:T(8,128)(2,1)} %dynamic-slice_convert_fusion.3), channel_id=1, source_target_pairs={{0,1},{1,0},{2,3},{3,2},{4,5},{5,4},{6,7},{7,6},{8,9},{9,8},{10,11... | collective-permute-start | bytes 2359304 | tf_op jit(solution)/shard_map/ppermute | solution.py:28
  594.3 61.5 %collective-permute-start.78 = (bf16[384,576]{0,1:T(8,128)(2,1)}, bf16[384,576]{0,1:T(8,128)(2,1)}, u32[]{:S(2)}, u32[]{:S(2)}) collective-permute-start(bf16[384,576]{0,1:T(8,128)(2,1)} %fusion.105), channel_id=1, source_target_pairs={{0,2},{2,0},{1,3},{3,1},{4,6},{6,4},{5,7},{7,5},{8,10},{10,8},{9,1... | collective-permute-start | bytes 1327112 | tf_op jit(solution)/shard_map/ppermute | solution.py:28
  648.6 32.3 %collective-permute-start.61 = (bf16[256,1536]{1,0:T(8,128)(2,1)S(1)}, bf16[256,1536]{1,0:T(8,128)(2,1)}, u32[]{:S(2)}, u32[]{:S(2)}) collective-permute-start(bf16[256,1536]{1,0:T(8,128)(2,1)S(1)} %dynamic-slice_convert_fusion.1), channel_id=1, source_target_pairs={{0,1},{1,0},{2,3},{3,2},{4,5},{5,4},{6,7},{7,6},{8,9},{9,8},{10,11... | collective-permute-start | bytes 2359304 | tf_op jit(solution)/shard_map/ppermute | solution.py:28
  (225 other events, 3781.3 us)
